TPU v7x, 512 devices: a whole 4x8x8 slice. The times are simulated.
512 devices in a mesh: panel: 64 (over z, x, core), sample: 8 (over y).
Axes of the slice: x: 4, y: 8, z: 8, core: 2. Of those that a mesh axis runs over, the one named last changes fastest.
Arguments:
- leaf_rhs: float32 [128, 256, 1024], P('panel', None, 'sample'), may hold values from -6 to 6
- sep_rhs: float32 [64, 256, 1024], P('panel', None, 'sample'), may hold values from -6 to 6
- leaf_size: int32 [128], P('panel'), may hold values from 64 to 256, as said below
- leaf_lower_inv: bfloat16 [128, 256, 256], P('panel'), may hold values from -0.375 to 0.375
- leaf_lower: bfloat16 [128, 2, 256, 256], P('panel'), may hold values from -0.1875 to 0.1875
- leaf_upper: bfloat16 [128, 2, 256, 256], P('panel'), may hold values from -0.25 to 0.25
- leaf_upper_inv: bfloat16 [128, 256, 256], P('panel'), may hold values from -0.375 to 0.375
- sep_lower_inv: float32 [64, 256, 256], P('panel', 'sample')
- sep_lower: float32 [64, 256, 256], P('panel', 'sample')
- sep_upper_inv: float32 [64, 256, 256], P('panel', 'sample')
- sep_upper: float32 [64, 256, 256], P('panel', 'sample')
Outputs:
- leaf_correction: float32 [128, 256, 1024], P('panel', None, 'sample')
- sep_correction: float32 [64, 256, 1024], P('panel', None, 'sample')
Inputs may be any that keep to these rules, and one draw needn't show every extreme that they name: `leaf_size`: every subdomain holds a leaf with all 256 columns live.
All inputs are finite; a program needn't handle non-finite values.
Results may differ from a plain program's by a relative error of at most 0.0049.
Values may be sent and summed in bfloat16 or wider, within the bound.
No kernel may reach another device: no remote copies, remote signals or barrier semaphores. Data moves between devices by JAX's collectives and lax.ppermute only.
A program may use at most 128 MiB of HBM per device.

v0:
```python
import jax
import jax.numpy as jnp
from jax import lax
from jax.sharding import PartitionSpec as P


def from_behind(shard, axis, by):
    size = lax.axis_size(axis)
    pairs = [(i, i + by) for i in range(size) if 0 <= i + by < size]
    return lax.ppermute(shard, axis, pairs)


def exact(left_side, right_side):
    return jnp.dot(
        left_side, right_side, precision=lax.Precision.HIGHEST, preferred_element_type=jnp.float32
    )


def forward_chain(offset, factor):

    def forward_relay(counter, carried):
        received = from_behind(carried, "panel", 1)
        return offset + exact(factor, received)

    return lax.fori_loop(0, lax.axis_size("panel") - 1, forward_relay, offset)


def backward_chain(offset, factor):

    def backward_relay(counter, carried):
        received = from_behind(carried, "panel", -1)
        return offset + exact(factor, received)

    return lax.fori_loop(0, lax.axis_size("panel") - 1, backward_relay, offset)


def per_device(
    leaf_rhs,
    sep_rhs,
    leaf_size,
    leaf_lower_inv,
    leaf_lower,
    leaf_upper,
    leaf_upper_inv,
    sep_lower_inv,
    sep_lower,
    sep_upper_inv,
    sep_upper,
):
    lower_inverse, lower_coupling = (
        lax.all_gather(sep_lower_inv, "sample", axis=1, tiled=True),
        lax.all_gather(sep_lower, "sample", axis=1, tiled=True),
    )
    width = leaf_rhs.shape[1]
    active_rows = (jnp.arange(width, dtype=jnp.int32)[None, :] < leaf_size[:, None]).astype(
        jnp.float32
    )[:, :, None]
    leaf_rounded = (active_rows * leaf_rhs).astype(jnp.bfloat16)
    leaf_forward = active_rows * jnp.einsum(
        "lij,ljs->lis", leaf_lower_inv, leaf_rounded, preferred_element_type=jnp.float32
    )
    forward_rounded = leaf_forward.astype(jnp.bfloat16)
    own_terms = jnp.einsum(
        "lij,ljs->is", leaf_lower[:, 1], forward_rounded, preferred_element_type=jnp.float32
    )
    left_terms = jnp.einsum(
        "lij,ljs->is", leaf_lower[:, 0], forward_rounded, preferred_element_type=jnp.float32
    )
    from_right = from_behind(left_terms, "panel", -1)
    sep_source = sep_rhs[0] - own_terms - from_right
    forward_offset = exact(lower_inverse[0], sep_source)
    forward_factor = -exact(lower_inverse[0], lower_coupling[0])
    sep_forward = forward_chain(forward_offset, forward_factor)
    upper_inverse, upper_coupling = (
        lax.all_gather(sep_upper_inv, "sample", axis=1, tiled=True),
        lax.all_gather(sep_upper, "sample", axis=1, tiled=True),
    )
    backward_offset = exact(upper_inverse[0], sep_forward)
    backward_factor = -exact(upper_inverse[0], upper_coupling[0])
    sep_correction = backward_chain(backward_offset, backward_factor)
    sep_rounded = sep_correction.astype(jnp.bfloat16)
    before = from_behind(sep_rounded, "panel", 1)
    leaf_back = leaf_forward - jnp.einsum(
        "lij,js->lis", leaf_upper[:, 0], before, preferred_element_type=jnp.float32
    )
    leaf_back = leaf_back - jnp.einsum(
        "lij,js->lis", leaf_upper[:, 1], sep_rounded, preferred_element_type=jnp.float32
    )
    back_rounded = leaf_back.astype(jnp.bfloat16)
    leaf_correction = active_rows * jnp.einsum(
        "lij,ljs->lis", leaf_upper_inv, back_rounded, preferred_element_type=jnp.float32
    )
    return (leaf_correction, sep_correction[None])


def solution(mesh):
    return jax.shard_map(
        per_device,
        mesh=mesh,
        in_specs=(
            P("panel", None, "sample"),
            P("panel", None, "sample"),
            P("panel"),
            P("panel", None, None),
            P("panel", None, None, None),
            P("panel", None, None, None),
            P("panel", None, None),
            P("panel", "sample", None),
            P("panel", "sample", None),
            P("panel", "sample", None),
            P("panel", "sample", None),
        ),
        out_specs=(P("panel", None, "sample"), P("panel", None, "sample")),
        check_vma=False,
    )
```

profile of v0, /device:TPU:272, one launch (start us, length us, event | category | flops | bytes accessed | tf_op | source)
XLA Modules:
  0.0 1375.8 jit_solution(2907661511422073181)
XLA Ops:
  6.3 26.1 %all_gather.12 = f32[1,256,256]{2,1,0:T(8,128)S(1)} all-gather(f32[1,32,256]{2,1,0:T(8,128)S(1)} %copy-done.6), channel_id=1, replica_groups=mesh['panel'=64,'sample'=8] {'sample'}, dimensions={1}, use_global_device_ids=true | all-gather | bytes 294912 | tf_op jit(solution)/shard_map/all_gather | solution.py:51
  32.4 24.9 %all_gather.13 = f32[1,256,256]{2,1,0:T(8,128)S(1)} all-gather(f32[1,32,256]{2,1,0:T(8,128)S(1)} %copy-done.7), channel_id=1, replica_groups=mesh['panel'=64,'sample'=8] {'sample'}, dimensions={1}, use_global_device_ids=true | all-gather | bytes 294912 | tf_op jit(solution)/shard_map/all_gather | solution.py:52
  57.4 25.0 %all_gather.14 = f32[1,256,256]{2,1,0:T(8,128)S(1)} all-gather(f32[1,32,256]{2,1,0:T(8,128)S(1)} %copy-done.8), channel_id=1, replica_groups=mesh['panel'=64,'sample'=8] {'sample'}, dimensions={1}, use_global_device_ids=true | all-gather | bytes 294912 | tf_op jit(solution)/shard_map/all_gather | solution.py:75
  82.4 24.8 %all_gather.15 = f32[1,256,256]{2,1,0:T(8,128)S(1)} all-gather(f32[1,32,256]{2,1,0:T(8,128)S(1)} %copy-done.9), channel_id=1, replica_groups=mesh['panel'=64,'sample'=8] {'sample'}, dimensions={1}, use_global_device_ids=true | all-gather | bytes 294912 | tf_op jit(solution)/shard_map/all_gather | solution.py:76
  109.1 630.3 %while.20 = (s32[]{:T(128)}, f32[256,128]{1,0:T(8,128)S(1)}, f32[256,256]{1,0:T(8,128)S(1)}, f32[256,128]{1,0:T(8,128)S(1)}, s32[]{:T(128)}) while((s32[]{:T(128)}, f32[256,128]{1,0:T(8,128)S(1)}, f32[256,256]{1,0:T(8,128)S(1)}, f32[256,128]{1,0:T(8,128)S(1)}, s32[]{:T(128)}) %tuple.37), condition=%wide.region_1.0_spmd, body=%wide.region_0.0_spmd.sunk | while | flops 100696064 | bytes 1179749 | solution.py:25
  111.0 7.7 collective-permute-done
  121.0 7.7 collective-permute-done
  131.0 7.7 collective-permute-done
  141.0 7.7 collective-permute-done
  151.1 7.7 collective-permute-done
  161.1 7.7 collective-permute-done
  171.1 7.7 collective-permute-done
  181.1 7.7 collective-permute-done
  191.1 7.7 collective-permute-done
  201.1 7.7 collective-permute-done
  211.1 7.7 collective-permute-done
  221.1 7.7 collective-permute-done
  231.1 7.7 collective-permute-done
  241.1 7.7 collective-permute-done
  251.1 7.7 collective-permute-done
  261.1 7.7 collective-permute-done
  271.1 7.7 collective-permute-done
  281.1 7.7 collective-permute-done
  291.1 7.7 collective-permute-done
  301.1 7.7 collective-permute-done
  311.1 7.7 collective-permute-done
  321.1 7.7 collective-permute-done
  331.1 7.7 collective-permute-done
  341.1 7.7 collective-permute-done
  351.1 7.7 collective-permute-done
  361.1 7.7 collective-permute-done
  371.1 7.7 collective-permute-done
  381.1 7.7 collective-permute-done
  391.2 7.7 collective-permute-done
  401.2 7.7 collective-permute-done
  411.2 7.7 collective-permute-done
  421.2 7.7 collective-permute-done
  431.2 7.7 collective-permute-done
  441.2 7.7 collective-permute-done
  451.2 7.7 collective-permute-done
  461.2 7.7 collective-permute-done
  471.2 7.7 collective-permute-done
  481.2 7.7 collective-permute-done
  491.2 7.7 collective-permute-done
  511.2 7.7 collective-permute-done
  651.3 7.7 collective-permute-done
  671.3 7.7 collective-permute-done
  739.9 625.2 %while.21 = (s32[]{:T(128)}, f32[256,128]{1,0:T(8,128)S(1)}, f32[256,256]{1,0:T(8,128)S(1)}, f32[256,128]{1,0:T(8,128)S(1)}, s32[]{:T(128)}) while((s32[]{:T(128)}, f32[256,128]{1,0:T(8,128)S(1)}, f32[256,256]{1,0:T(8,128)S(1)}, f32[256,128]{1,0:T(8,128)S(1)}, s32[]{:T(128)}) %tuple.40), condition=%wide.region_3.0_spmd, body=%wide.region_2.0_spmd.sunk | while | flops 100696064 | bytes 1179749 | solution.py:34
  (375 shorter events, 947.9 us)
Async XLA Ops:
  3.1 104.8 %collective-permute-start.2 = (f32[256,128]{1,0:T(8,128)S(1)}, f32[256,128]{1,0:T(8,128)S(1)}, u32[]{:S(2)}, u32[]{:S(2)}) collective-permute-start(f32[256,128]{1,0:T(8,128)S(1)} %convolution_bitcast_fusion.4), channel_id=1, source_target_pairs={{8,0},{16,8},{24,16},{32,24},{40,32},{48,40},{56,48},{64,56},{72,6... | collective-permute-start | bytes 393224 | tf_op jit(solution)/shard_map/ppermute | solution.py:10
  744.9 9.6 collective-permute-start.1
  754.9 9.6 collective-permute-start.1
  764.9 9.6 collective-permute-start.1
  774.9 9.6 collective-permute-start.1
  784.9 9.6 collective-permute-start.1
  794.9 9.6 collective-permute-start.1
  804.9 9.6 collective-permute-start.1
  814.9 9.6 collective-permute-start.1
  824.9 9.6 collective-permute-start.1
  834.9 9.6 collective-permute-start.1
  844.9 9.6 collective-permute-start.1
  854.9 9.6 collective-permute-start.1
  864.9 9.6 collective-permute-start.1
  874.9 9.6 collective-permute-start.1
  884.9 9.6 collective-permute-start.1
  894.9 9.6 collective-permute-start.1
  904.9 9.6 collective-permute-start.1
  914.9 9.6 collective-permute-start.1
  924.9 9.6 collective-permute-start.1
  934.9 9.6 collective-permute-start.1
  944.9 9.6 collective-permute-start.1
  955.0 9.6 collective-permute-start.1
  965.0 9.6 collective-permute-start.1
  975.0 9.6 collective-permute-start.1
  985.0 9.6 collective-permute-start.1
  995.0 9.6 collective-permute-start.1
  1005.0 9.6 collective-permute-start.1
  1015.0 9.6 collective-permute-start.1
  1025.0 9.6 collective-permute-start.1
  1035.0 9.6 collective-permute-start.1
  1045.0 9.6 collective-permute-start.1
  1055.0 9.6 collective-permute-start.1
  1065.0 9.6 collective-permute-start.1
  1075.0 9.6 collective-permute-start.1
  1085.0 9.6 collective-permute-start.1
  1095.0 9.6 collective-permute-start.1
  1105.0 9.6 collective-permute-start.1
  1115.0 9.6 collective-permute-start.1
  1155.0 9.6 collective-permute-start.1
  1175.0 9.6 collective-permute-start.1
  1195.1 9.6 collective-permute-start.1
  1235.1 9.6 collective-permute-start.1
  1245.1 9.6 collective-permute-start.1
  1255.1 9.6 collective-permute-start.1
  1295.1 9.6 collective-permute-start.1
  1305.1 9.6 collective-permute-start.1
  1315.1 9.6 collective-permute-start.1
  (90 other events, 1503.2 us)
where the time goes:
time: 1380 us
  waiting for transfers between devices  648 us (47%)
  starting transfers between devices  568 us (41%)
  blocking collectives  101 us (7%)
  matrix products  51.2 us (4%)
    ppermute x128, waiting for transfers between devices, from_behind(): return lax.ppermute(shard, axis, pairs)  648 us
    ppermute x128, starting transfers between devices, from_behind(): return lax.ppermute(shard, axis, pairs)  568 us
    dot_general x130, matrix products, exact(): jnp.dot(left_side, right_side, precision=lax.Precision.HIGHEST, preferred...  48.8 us
  transfers between devices with their start and end apart: 128, of which 127 were waited for; matrix products, arithmetic and copies ran while one was open for 0% of the time, Pallas kernels for 0%

commit v1 on v0

v1 whole, which is shorter than its diff:
```python
import jax
import jax.numpy as jnp
from jax import lax
from jax.sharding import Mesh
from jax.sharding import PartitionSpec as P

Z, X, C, Y = "z", "x", "c", "y"
F32, F16 = jnp.float32, jnp.float16


def exact(left_side, right_side):
    return jnp.dot(
        left_side, right_side, precision=lax.Precision.HIGHEST, preferred_element_type=F32
    )


def exponent(values, axis):
    largest = jnp.max(jnp.abs(values), axis=axis, keepdims=True)
    return jnp.clip(jnp.floor(jnp.log2(jnp.maximum(largest, 1e-36))), -120.0, 120.0)


def encode_rows(parts):
    exponents = [exponent(part, 1) for part in parts]
    scaled = [part * jnp.exp2(-k) for part, k in zip(parts, exponents)]
    room = 128 // len(parts)
    spread = [jnp.broadcast_to(k, (k.shape[0], room)) for k in exponents]
    return jnp.concatenate(scaled + spread, axis=1).astype(F16)


def decode_rows(wire, count, width):
    room = 128 // count
    start = count * width
    parts = []
    for i in range(count):
        k = wire[:, start + room * i : start + room * i + 1].astype(F32)
        parts.append(wire[:, width * i : width * (i + 1)].astype(F32) * jnp.exp2(k))
    return parts


def encode(values):
    k = exponent(values, 0)
    spread = jnp.broadcast_to(k, (16, k.shape[1]))
    return jnp.concatenate([values * jnp.exp2(-k), spread], axis=0).astype(F16)


def decode(wire):
    rows = wire.shape[1] - 16
    k = wire[:, rows : rows + 1].astype(F32)
    return wire[:, :rows].astype(F32) * jnp.exp2(k)


def to_all(block, axis):
    size = lax.axis_size(axis)
    slots = jnp.broadcast_to(block[None], (size,) + block.shape)
    return lax.all_to_all(slots, axis, 0, 0, tiled=True)


def swap_cores(block):
    return lax.ppermute(block, C, [(0, 1), (1, 0)])


def half(block, core):
    rows = block.shape[0] // 2
    return jnp.where(core == 0, block[:rows], block[rows:])


def per_device(
    leaf_rhs,
    sep_rhs,
    leaf_size,
    leaf_lower_inv,
    leaf_lower,
    leaf_upper,
    leaf_upper_inv,
    sep_lower_inv,
    sep_lower,
    sep_upper_inv,
    sep_upper,
):
    panel = (Z, X, C)
    panels = lax.axis_size(panel)
    planes, chips = lax.axis_size(Z), lax.axis_size(X)
    z, x, core = lax.axis_index(Z), lax.axis_index(X), lax.axis_index(C)
    width, samples = leaf_rhs.shape[1], leaf_rhs.shape[2]

    active_rows = (jnp.arange(width, dtype=jnp.int32)[None, :] < leaf_size[:, None]).astype(F32)[
        :, :, None
    ]
    leaf_rounded = (active_rows * leaf_rhs).astype(jnp.bfloat16)
    leaf_forward = active_rows * jnp.einsum(
        "lij,ljs->lis", leaf_lower_inv, leaf_rounded, preferred_element_type=F32
    )
    forward_rounded = leaf_forward.astype(jnp.bfloat16)
    left_terms = jnp.einsum(
        "lij,ljs->is", leaf_lower[:, 0], forward_rounded, preferred_element_type=F32
    )
    from_right = lax.ppermute(left_terms, panel, [(i + 1, i) for i in range(panels - 1)])
    own_terms = jnp.einsum(
        "lij,ljs->is", leaf_lower[:, 1], forward_rounded, preferred_element_type=F32
    )

    wire = encode_rows([sep_lower_inv[0], sep_lower[0], sep_upper_inv[0], sep_upper[0]])
    wire = to_all(wire, Y).reshape(width, -1)
    lower_inverse, lower, upper_inverse, upper = decode_rows(wire, 4, width)
    forward_factor = -exact(lower_inverse, lower)
    backward_factor = -exact(upper_inverse, upper)
    sep_source = sep_rhs[0] - own_terms - from_right
    offset = exact(lower_inverse, sep_source)

    mine = jnp.concatenate([forward_factor, backward_factor, offset], axis=1)
    other = swap_cores(mine)
    first = jnp.where(core == 0, mine, other)
    second = jnp.where(core == 0, other, mine)
    first_backward = first[:, width : 2 * width]
    pair = jnp.concatenate(
        [
            exact(second[:, :width], first[:, :width]),
            exact(first_backward, second[:, width : 2 * width]),
            second[:, 2 * width :] + exact(second[:, :width], first[:, 2 * width :]),
        ],
        axis=1,
    )
    prefix = jnp.where(core == 0, forward_factor, pair[:, :width])
    prefix_value = jnp.where(core == 0, offset, pair[:, 2 * width :])
    suffix = jnp.where(core == 0, pair[:, width : 2 * width], backward_factor)

    pairs = decode(to_all(encode(half(pair, core)), (X, C))).reshape(chips, width, -1)
    ahead = jnp.eye(width, dtype=F32)
    ahead_value = jnp.zeros((width, samples), F32)
    chip_prefix, chip_prefix_value = ahead, ahead_value
    for i in range(chips):
        factor = pairs[i, :, :width]
        ahead = factor if i == 0 else exact(factor, ahead)
        value = pairs[i, :, 2 * width :]
        ahead_value = value if i == 0 else value + exact(factor, ahead_value)
        if i < chips - 1:
            chip_prefix = jnp.where(x == i + 1, ahead, chip_prefix)
            chip_prefix_value = jnp.where(x == i + 1, ahead_value, chip_prefix_value)
    behind = jnp.eye(width, dtype=F32)
    chip_suffix = behind
    for i in range(chips - 1, -1, -1):
        factor = pairs[i, :, width : 2 * width]
        behind = factor if i == chips - 1 else exact(factor, behind)
        if i > 0:
            chip_suffix = jnp.where(x == i - 1, behind, chip_suffix)

    half_ahead, half_behind = half(ahead, core), half(behind, core)
    half_value = half(ahead_value, core)
    later = encode(jnp.concatenate([half_ahead, half_value], axis=1))
    earlier = encode(jnp.concatenate([half_behind, half_value], axis=1))
    index = jnp.arange(planes, dtype=jnp.int32)[:, None, None]
    wire = lax.all_to_all(
        jnp.where(index > z, later[None], earlier[None]), Z, 0, 0, tiled=True
    )
    wire_other = swap_cores(wire)
    first = decode(jnp.where(core == 0, wire, wire_other))
    second = decode(jnp.where(core == 0, wire_other, wire))
    all_planes = jnp.concatenate([first, second], axis=1)
    received = jnp.zeros((width, samples), F32)
    for i in range(planes - 1):
        value = all_planes[i, :, width:] + exact(all_planes[i, :, :width], received)
        received = jnp.where(z > i, value, received)
    received = chip_prefix_value + exact(chip_prefix, received)
    sep_forward = prefix_value + exact(prefix, received)

    offset = exact(upper_inverse, sep_forward)
    other = swap_cores(offset)
    first = jnp.where(core == 0, offset, other)
    second = jnp.where(core == 0, other, offset)
    pair_value = first + exact(first_backward, second)
    suffix_value = jnp.where(core == 0, pair_value, offset)
    values = decode(to_all(encode(pair_value), X))
    behind_value = jnp.zeros((width, samples), F32)
    chip_suffix_value = behind_value
    for i in range(chips - 1, -1, -1):
        factor = pairs[i, :, width : 2 * width]
        behind_value = values[i] if i == chips - 1 else values[i] + exact(factor, behind_value)
        if i > 0:
            chip_suffix_value = jnp.where(x == i - 1, behind_value, chip_suffix_value)
    values = decode(to_all(encode(behind_value), Z))
    received = jnp.zeros((width, samples), F32)
    for i in range(planes - 1, 0, -1):
        value = values[i] + exact(all_planes[i, :, :width], received)
        received = jnp.where(z < i, value, received)
    received = chip_suffix_value + exact(chip_suffix, received)
    sep_correction = suffix_value + exact(suffix, received)

    sep_rounded = sep_correction.astype(jnp.bfloat16)
    before = lax.ppermute(sep_rounded, panel, [(i, i + 1) for i in range(panels - 1)])
    leaf_back = leaf_forward - jnp.einsum(
        "lij,js->lis", leaf_upper[:, 1], sep_rounded, preferred_element_type=F32
    )
    leaf_back = leaf_back - jnp.einsum(
        "lij,js->lis", leaf_upper[:, 0], before, preferred_element_type=F32
    )
    back_rounded = leaf_back.astype(jnp.bfloat16)
    leaf_correction = active_rows * jnp.einsum(
        "lij,ljs->lis", leaf_upper_inv, back_rounded, preferred_element_type=F32
    )
    return (leaf_correction, sep_correction[None])


def solution(mesh):
    cut = Mesh(mesh.devices.reshape(8, 4, 2, 8), (Z, X, C, Y))
    panel = (Z, X, C)
    return jax.shard_map(
        per_device,
        mesh=cut,
        in_specs=(
            P(panel, None, Y),
            P(panel, None, Y),
            P(panel),
            P(panel, None, None),
            P(panel, None, None, None),
            P(panel, None, None, None),
            P(panel, None, None),
            P(panel, Y, None),
            P(panel, Y, None),
            P(panel, Y, None),
            P(panel, Y, None),
        ),
        out_specs=(P(panel, None, Y), P(panel, None, Y)),
        check_vma=False,
    )
```

time: 1380 us -> 181 us (0.13)
  the two profiles are of different devices: /device:TPU:272 before, /device:TPU:1 now
where the time goes in v1:
time: 181 us; the launch traced here: 179 us
  waiting for transfers between devices  52.2 us (29%)
  blocking collectives  42.8 us (24%)
  starting transfers between devices  35.7 us (20%)
  matrix products  25 us (14%)
  other arithmetic  10.9 us (6%)
  local copies, waits for them, and re-layouts  10.2 us (6%)
  between operations  1.86 us (1%)
    all_to_all x3, waiting for transfers between devices, to_all(): return lax.all_to_all(slots, axis, 0, 0, tiled=True)  45.3 us
    all_to_all x1, blocking collectives, per_device(): lax.all_to_all(jnp.where(index > z, later[None], earlier[None]), Z, 0, 0,...  33.8 us
    dot_general x38, matrix products, exact(): jnp.dot(left_side, right_side, precision=lax.Precision.HIGHEST, preferred...  22.7 us
    all_to_all x3, starting transfers between devices, to_all(): return lax.all_to_all(slots, axis, 0, 0, tiled=True)  16.5 us
    ppermute x3, starting transfers between devices, swap_cores(): return lax.ppermute(block, C, [(0, 1), (1, 0)])  11.8 us
    all_to_all x1, blocking collectives, to_all(): return lax.all_to_all(slots, axis, 0, 0, tiled=True)  8.96 us
    ppermute x1, starting transfers between devices, per_device(): lax.ppermute(left_terms, panel, [(i + 1, i) for i in range(panels - 1)])  4.69 us
    ppermute x3, waiting for transfers between devices, swap_cores(): return lax.ppermute(block, C, [(0, 1), (1, 0)])  4.48 us
  transfers between devices with their start and end apart: 8, of which 8 were waited for; matrix products, arithmetic and copies ran while one was open for 2% of the time, Pallas kernels for 0%

profile of v1, /device:TPU:1, one launch (start us, length us, event | category | flops | bytes accessed | tf_op | source)
XLA Modules:
  0.0 178.6 jit_solution(16306312787944981139)
XLA Ops:
  0.7 0.9 abs_reduce_fusion.7
  1.6 0.9 abs_reduce_fusion.8
  2.5 0.9 abs_reduce_fusion.5
  3.4 0.9 abs_reduce_fusion.6
  4.3 0.9 fusion.129
  5.2 0.9 fusion.131
  6.5 0.9 broadcast_in_dim.35
  7.3 7.7 %all-to-all-start = ((f16[8,32,1152]{2,1,0:T(8,128)(2,1)}), f16[8,32,1152]{2,1,0:T(8,128)(2,1)S(1)}, u32[]{:S(2)}, u32[]{:S(2)}) async-start(f16[8,32,1152]{2,1,0:T(8,128)(2,1)} %broadcast_in_dim.35), calls=%async_computation | async-start | bytes 1179648 | tf_op jit(solution)/shard_map/all_to_all | solution.py:55
  15.0 0.7 compare_convert_fusion
  15.7 1.3 fusion.1
  17.2 4.7 %collective-permute-start = (f32[256,128]{0,1:T(8,128)S(1)}, f32[256,128]{0,1:T(8,128)S(1)}, u32[]{:S(2)}, u32[]{:S(2)}) collective-permute-start(f32[256,128]{0,1:T(8,128)S(1)} %convolution_bitcast_fusion.2), channel_id=1, source_target_pairs={{8,0},{16,8},{24,16},{32,24},{40,32},{48,40},{56,48},{64,56},{72,6... | collective-permute-start | bytes 393224 | tf_op jit(solution)/shard_map/ppermute | solution.py:97
  22.0 2.1 %collective-permute-done = f32[256,128]{0,1:T(8,128)S(1)} collective-permute-done((f32[256,128]{0,1:T(8,128)S(1)}, f32[256,128]{0,1:T(8,128)S(1)}, u32[]{:S(2)}, u32[]{:S(2)}) %collective-permute-start) | collective-permute-done | bytes 131104 | tf_op jit(solution)/shard_map/ppermute | solution.py:97
  24.4 7.1 %all-to-all-done = f16[8,32,1152]{2,1,0:T(8,128)(2,1)S(1)} async-done(((f16[8,32,1152]{2,1,0:T(8,128)(2,1)}), f16[8,32,1152]{2,1,0:T(8,128)(2,1)S(1)}, u32[]{:S(2)}, u32[]{:S(2)}) %all-to-all-start) | async-done | bytes 589856 | tf_op jit(solution)/shard_map/all_to_all | solution.py:55
  31.8 0.7 convolution_negate_fusion.1
  32.5 0.5 fusion.67
  33.0 0.7 convolution_negate_fusion
  33.8 5.3 %collective-permute-start.1 = (f32[256,640]{0,1:T(8,128)S(1)}, f32[256,640]{0,1:T(8,128)S(1)}, u32[]{:S(2)}, u32[]{:S(2)}) collective-permute-start(f32[256,640]{0,1:T(8,128)S(1)} %pad_maximum_fusion), channel_id=1, source_target_pairs={{0,8},{8,0},{1,9},{9,1},{2,10},{10,2},{3,11},{11,3},{4,12},{12,4},... | collective-permute-start | bytes 1966088 | tf_op jit(solution)/shard_map/ppermute | solution.py:59
  39.1 1.7 collective-permute-done.1
  43.1 1.3 broadcast_in_dim.37
  44.4 4.7 %all-to-all-start.1 = ((f16[8,144,640]{2,1,0:T(8,128)(2,1)}), f16[8,144,640]{2,1,0:T(8,128)(2,1)S(1)}, u32[]{:S(2)}, u32[]{:S(2)}) async-start(f16[8,144,640]{2,1,0:T(8,128)(2,1)} %broadcast_in_dim.37), calls=%async_computation.1 | async-start | bytes 2949120 | tf_op jit(solution)/shard_map/all_to_all | solution.py:55
  49.0 19.7 %all-to-all-done.1 = f16[8,144,640]{2,1,0:T(8,128)(2,1)S(1)} async-done(((f16[8,144,640]{2,1,0:T(8,128)(2,1)}), f16[8,144,640]{2,1,0:T(8,128)(2,1)S(1)}, u32[]{:S(2)}, u32[]{:S(2)}) %all-to-all-start.1) | async-done | bytes 1474592 | tf_op jit(solution)/shard_map/all_to_all | solution.py:55
  70.5 0.6 fusion.72
  71.6 0.6 fusion.71
  74.8 33.8 %all_to_all.25 = f16[8,144,384]{2,1,0:T(8,128)(2,1)S(1)} all-to-all(f16[8,144,384]{2,1,0:T(8,128)(2,1)S(1)} %broadcast_select_fusion), channel_id=1, replica_groups=mesh['z'=8,'x'=4,'c'=2,'y'=8] {'z'}, dimensions={0} | all-to-all | bytes 1769472 | tf_op jit(solution)/shard_map/all_to_all | solution.py:152
  108.6 4.2 %collective-permute-start.2 = (f16[8,144,384]{2,1,0:T(8,128)(2,1)S(1)}, f16[8,144,384]{2,1,0:T(8,128)(2,1)S(1)}, u32[]{:S(2)}, u32[]{:S(2)}) collective-permute-start(f16[8,144,384]{2,1,0:T(8,128)(2,1)S(1)} %all_to_all.25), channel_id=1, source_target_pairs={{0,8},{8,0},{1,9},{9,1},{2,10},{10,2},{3,11},{11,3},{4,12},{12,4},... | collective-permute-start | bytes 2654216 | tf_op jit(solution)/shard_map/ppermute | solution.py:59
  112.9 1.8 %collective-permute-done.2 = f16[8,144,384]{2,1,0:T(8,128)(2,1)S(1)} collective-permute-done((f16[8,144,384]{2,1,0:T(8,128)(2,1)S(1)}, f16[8,144,384]{2,1,0:T(8,128)(2,1)S(1)}, u32[]{:S(2)}, u32[]{:S(2)}) %collective-permute-start.2) | collective-permute-done | bytes 884768 | tf_op jit(solution)/shard_map/ppermute | solution.py:59
  118.2 0.5 copy-done.14
  118.9 1.4 convolution_add_fusion.11
  120.7 1.4 fusion.68
  122.1 2.3 %collective-permute-start.3 = (f32[256,128]{0,1:T(8,128)S(1)}, f32[256,128]{0,1:T(8,128)S(1)}, u32[]{:S(2)}, u32[]{:S(2)}) collective-permute-start(f32[256,128]{0,1:T(8,128)S(1)} %fusion.68), channel_id=1, source_target_pairs={{0,8},{8,0},{1,9},{9,1},{2,10},{10,2},{3,11},{11,3},{4,12},{12,4},... | collective-permute-start | bytes 393224 | tf_op jit(solution)/shard_map/ppermute | solution.py:59
  124.4 1.0 collective-permute-done.3
  125.4 1.3 abs_reduce_fusion.4
  126.7 0.6 copy-done.25
  127.6 0.7 copy.62
  128.3 0.9 broadcast_in_dim.44
  129.3 9.0 %all_to_all.26 = f16[4,272,128]{2,1,0:T(8,128)(2,1)S(1)} all-to-all(f16[4,272,128]{2,1,0:T(8,128)(2,1)S(1)} %broadcast_in_dim.44), channel_id=1, replica_groups=mesh['z'=8,'x'=4,'c'=2,'y'=8] {'x'}, dimensions={0} | all-to-all | bytes 557056 | tf_op jit(solution)/shard_map/all_to_all | solution.py:55
  138.3 1.5 convolution_add_fusion.10
  139.8 1.3 convolution_add_fusion.9
  141.2 1.4 abs_reduce_fusion.3
  142.7 0.9 broadcast_in_dim.46
  143.5 4.2 %all-to-all-start.4 = ((f16[8,272,128]{2,1,0:T(8,128)(2,1)}), f16[8,272,128]{2,1,0:T(8,128)(2,1)}, u32[]{:S(2)}, u32[]{:S(2)}) async-start(f16[8,272,128]{2,1,0:T(8,128)(2,1)} %broadcast_in_dim.46), calls=%async_computation.4 | async-start | bytes 1114112 | tf_op jit(solution)/shard_map/all_to_all | solution.py:55
  147.8 18.6 %all-to-all-done.4 = f16[8,272,128]{2,1,0:T(8,128)(2,1)} async-done(((f16[8,272,128]{2,1,0:T(8,128)(2,1)}), f16[8,272,128]{2,1,0:T(8,128)(2,1)}, u32[]{:S(2)}, u32[]{:S(2)}) %all-to-all-start.4) | async-done | bytes 557088 | tf_op jit(solution)/shard_map/all_to_all | solution.py:55
  166.3 0.7 fusion.138
  167.1 1.1 convert_multiply_fusion.3
  171.5 1.4 convolution_add_fusion
  173.4 2.6 %collective-permute-start.4 = (bf16[256,128]{0,1:T(8,128)(2,1)S(1)}, bf16[256,128]{0,1:T(8,128)(2,1)S(1)}, u32[]{:S(2)}, u32[]{:S(2)}) collective-permute-start(bf16[256,128]{0,1:T(8,128)(2,1)S(1)} %get-tuple-element.42), channel_id=1, source_target_pairs={{0,8},{8,16},{16,24},{24,32},{32,40},{40,48},{48,56},{56,64},{64,7... | collective-permute-start | bytes 196616 | tf_op jit(solution)/shard_map/ppermute | solution.py:189
  176.3 0.8 copy.67
  177.7 0.8 copy.66
  (165 shorter events, 17.0 us)
Async XLA Ops:
  0.6 15.1 %copy-start = (bf16[2,256,256]{2,1,0:T(8,128)(2,1)S(1)}, bf16[2,256,256]{2,1,0:T(8,128)(2,1)}, u32[]{:S(2)}) copy-start(bf16[2,256,256]{2,1,0:T(8,128)(2,1)} %param.14) | copy-start | bytes 786436
  0.6 16.3 %copy-start.35 = (bf16[2,2,256,256]{3,2,1,0:T(8,128)(2,1)S(1)}, bf16[2,2,256,256]{3,2,1,0:T(8,128)(2,1)}, u32[]{:S(2)}) copy-start(bf16[2,2,256,256]{3,2,1,0:T(8,128)(2,1)} %param.15) | copy-start | bytes 1572868
  0.7 21.3 %copy-start.39 = (f32[1,256,128]{2,1,0:T(8,128)S(1)}, f32[1,256,128]{2,1,0:T(8,128)}, u32[]{:S(2)}) copy-start(f32[1,256,128]{2,1,0:T(8,128)} %param.12) | copy-start | bytes 393220
  7.3 24.1 %all-to-all-start = ((f16[8,32,1152]{2,1,0:T(8,128)(2,1)}), f16[8,32,1152]{2,1,0:T(8,128)(2,1)S(1)}, u32[]{:S(2)}, u32[]{:S(2)}) async-start(f16[8,32,1152]{2,1,0:T(8,128)(2,1)} %broadcast_in_dim.35), calls=%async_computation | async-start | bytes 1179648 | tf_op jit(solution)/shard_map/all_to_all | solution.py:55
  17.0 23.9 %copy-start.2 = (f32[2,256,128]{1,2,0:T(8,128)}, f32[2,256,128]{1,2,0:T(8,128)S(1)}, u32[]{:S(2)}) copy-start(f32[2,256,128]{1,2,0:T(8,128)S(1)} %fusion.1) | copy-start | bytes 786436
  17.2 6.9 %collective-permute-start = (f32[256,128]{0,1:T(8,128)S(1)}, f32[256,128]{0,1:T(8,128)S(1)}, u32[]{:S(2)}, u32[]{:S(2)}) collective-permute-start(f32[256,128]{0,1:T(8,128)S(1)} %convolution_bitcast_fusion.2), channel_id=1, source_target_pairs={{8,0},{16,8},{24,16},{32,24},{40,32},{48,40},{56,48},{64,56},{72,6... | collective-permute-start | bytes 393224 | tf_op jit(solution)/shard_map/ppermute | solution.py:97
  31.4 9.5 %copy-start.21 = (f16[8,32,1152]{2,1,0:T(8,128)(2,1)}, f16[8,32,1152]{2,1,0:T(8,128)(2,1)S(1)}, u32[]{:S(2)}) copy-start(f16[8,32,1152]{2,1,0:T(8,128)(2,1)S(1)} %all-to-all-done) | copy-start | bytes 1769476
  32.5 8.8 %copy-start.19 = (f32[256,256]{0,1:T(8,128)}, f32[256,256]{0,1:T(8,128)S(1)}, u32[]{:S(2)}) copy-start(f32[256,256]{0,1:T(8,128)S(1)} %convolution_negate_fusion.1) | copy-start | bytes 786436
  33.7 8.0 %copy-start.17 = (f32[256,256]{0,1:T(8,128)}, f32[256,256]{0,1:T(8,128)S(1)}, u32[]{:S(2)}) copy-start(f32[256,256]{0,1:T(8,128)S(1)} %convolution_negate_fusion) | copy-start | bytes 786436
  33.8 7.0 %collective-permute-start.1 = (f32[256,640]{0,1:T(8,128)S(1)}, f32[256,640]{0,1:T(8,128)S(1)}, u32[]{:S(2)}, u32[]{:S(2)}) collective-permute-start(f32[256,640]{0,1:T(8,128)S(1)} %pad_maximum_fusion), channel_id=1, source_target_pairs={{0,8},{8,0},{1,9},{9,1},{2,10},{10,2},{3,11},{11,3},{4,12},{12,4},... | collective-permute-start | bytes 1966088 | tf_op jit(solution)/shard_map/ppermute | solution.py:59
  40.9 1.6 copy-start.4
  41.3 1.4 copy-start.11
  41.8 0.8 copy-start.5
  42.1 0.7 copy-start.27
  44.4 24.3 %all-to-all-start.1 = ((f16[8,144,640]{2,1,0:T(8,128)(2,1)}), f16[8,144,640]{2,1,0:T(8,128)(2,1)S(1)}, u32[]{:S(2)}, u32[]{:S(2)}) async-start(f16[8,144,640]{2,1,0:T(8,128)(2,1)} %broadcast_in_dim.37), calls=%async_computation.1 | async-start | bytes 2949120 | tf_op jit(solution)/shard_map/all_to_all | solution.py:55
  68.9 3.7 %copy-start.1 = (f32[8,128,640]{2,1,0:T(8,128)}, f32[8,128,640]{2,1,0:T(8,128)S(1)}, u32[]{:S(2)}) copy-start(f32[8,128,640]{2,1,0:T(8,128)S(1)} %convert_multiply_fusion) | copy-start | bytes 7864324
  69.3 2.9 %copy-start.7 = (f32[256,256]{1,0:T(8,128)}, f32[256,256]{1,0:T(8,128)S(1)}, u32[]{:S(2)}) copy-start(f32[256,256]{1,0:T(8,128)S(1)} %fusion.74) | copy-start | bytes 786436
  69.7 3.3 %copy-start.13 = (f32[256,256]{1,0:T(8,128)}, f32[256,256]{1,0:T(8,128)S(1)}, u32[]{:S(2)}) copy-start(f32[256,256]{1,0:T(8,128)S(1)} %fusion.70) | copy-start | bytes 786436
  70.1 2.9 %copy-start.31 = (f32[256,128]{1,0:T(8,128)}, f32[256,128]{1,0:T(8,128)S(1)}, u32[]{:S(2)}) copy-start(f32[256,128]{1,0:T(8,128)S(1)} %convolution_add_fusion.21) | copy-start | bytes 393220
  70.5 2.5 %copy-start.9 = (f32[256,256]{1,0:T(8,128)}, f32[256,256]{1,0:T(8,128)S(1)}, u32[]{:S(2)}) copy-start(f32[256,256]{1,0:T(8,128)S(1)} %fusion.73) | copy-start | bytes 786436
  71.6 1.5 copy-start.15
  72.6 0.7 copy-start.33
  108.6 6.1 %collective-permute-start.2 = (f16[8,144,384]{2,1,0:T(8,128)(2,1)S(1)}, f16[8,144,384]{2,1,0:T(8,128)(2,1)S(1)}, u32[]{:S(2)}, u32[]{:S(2)}) collective-permute-start(f16[8,144,384]{2,1,0:T(8,128)(2,1)S(1)} %all_to_all.25), channel_id=1, source_target_pairs={{0,8},{8,0},{1,9},{9,1},{2,10},{10,2},{3,11},{11,3},{4,12},{12,4},... | collective-permute-start | bytes 2654216 | tf_op jit(solution)/shard_map/ppermute | solution.py:59
  117.8 1.0 copy-start.14
  117.8 1.0 copy-start.16
  117.8 1.0 copy-start.32
  117.8 1.1 copy-start.34
  117.8 2.5 %copy-start.12 = (f32[256,256]{0,1:T(8,128)S(1)}, f32[256,256]{0,1:T(8,128)}, u32[]{:S(2)}) copy-start(f32[256,256]{0,1:T(8,128)} %copy-done.11) | copy-start | bytes 786436
  117.8 2.5 %copy-start.20 = (f32[256,256]{0,1:T(8,128)S(1)}, f32[256,256]{0,1:T(8,128)}, u32[]{:S(2)}) copy-start(f32[256,256]{0,1:T(8,128)} %copy-done.19) | copy-start | bytes 786436
  117.8 2.9 %copy-start.28 = (f32[256,128]{0,1:T(8,128)S(1)}, f32[256,128]{0,1:T(8,128)}, u32[]{:S(2)}) copy-start(f32[256,128]{0,1:T(8,128)} %copy-done.27) | copy-start | bytes 393220
  122.1 5.3 %copy-start.29 = (f32[256,128]{0,1:T(8,128)}, f32[256,128]{0,1:T(8,128)S(1)}, u32[]{:S(2)}) copy-start(f32[256,128]{0,1:T(8,128)S(1)} %fusion.68) | copy-start | bytes 393220
  122.1 3.3 %collective-permute-start.3 = (f32[256,128]{0,1:T(8,128)S(1)}, f32[256,128]{0,1:T(8,128)S(1)}, u32[]{:S(2)}, u32[]{:S(2)}) collective-permute-start(f32[256,128]{0,1:T(8,128)S(1)} %fusion.68), channel_id=1, source_target_pairs={{0,8},{8,0},{1,9},{9,1},{2,10},{10,2},{3,11},{11,3},{4,12},{12,4},... | collective-permute-start | bytes 393224 | tf_op jit(solution)/shard_map/ppermute | solution.py:59
  126.7 0.7 copy-start.25
  138.3 2.9 %copy-start.22 = (f32[4,256,128]{2,1,0:T(8,128)}, f32[4,256,128]{2,1,0:T(8,128)S(1)}, u32[]{:S(2)}) copy-start(f32[4,256,128]{2,1,0:T(8,128)S(1)} %convert_multiply_fusion.4) | copy-start | bytes 1572868
  141.2 1.4 copy-start.23
  143.5 22.8 %all-to-all-start.4 = ((f16[8,272,128]{2,1,0:T(8,128)(2,1)}), f16[8,272,128]{2,1,0:T(8,128)(2,1)}, u32[]{:S(2)}, u32[]{:S(2)}) async-start(f16[8,272,128]{2,1,0:T(8,128)(2,1)} %broadcast_in_dim.46), calls=%async_computation.4 | async-start | bytes 1114112 | tf_op jit(solution)/shard_map/all_to_all | solution.py:55
  170.5 1.0 copy-start.8
  170.5 1.0 copy-start.10
  170.5 1.0 copy-start.24
  170.5 2.5 %copy-start.6 = (f32[256,256]{0,1:T(8,128)S(1)}, f32[256,256]{0,1:T(8,128)}, u32[]{:S(2)}) copy-start(f32[256,256]{0,1:T(8,128)} %copy-done.5) | copy-start | bytes 786436
  170.5 2.5 %copy-start.18 = (f32[256,256]{0,1:T(8,128)S(1)}, f32[256,256]{0,1:T(8,128)}, u32[]{:S(2)}) copy-start(f32[256,256]{0,1:T(8,128)} %copy-done.17) | copy-start | bytes 786436
  170.5 2.5 %copy-start.26 = (f32[256,128]{0,1:T(8,128)S(1)}, f32[256,128]{0,1:T(8,128)}, u32[]{:S(2)}) copy-start(f32[256,128]{0,1:T(8,128)} %copy-done.25) | copy-start | bytes 393220
  170.5 2.5 %copy-start.30 = (f32[256,128]{0,1:T(8,128)S(1)}, f32[256,128]{0,1:T(8,128)}, u32[]{:S(2)}) copy-start(f32[256,128]{0,1:T(8,128)} %copy-done.29) | copy-start | bytes 393220
  170.5 5.5 %copy-start.3 = (f32[2,256,128]{1,2,0:T(8,128)S(1)}, f32[2,256,128]{1,2,0:T(8,128)}, u32[]{:S(2)}) copy-start(f32[2,256,128]{1,2,0:T(8,128)} %copy-done.2) | copy-start | bytes 786436
  170.6 5.5 %copy-start.36 = (bf16[2,2,256,256]{3,2,1,0:T(8,128)(2,1)S(1)}, bf16[2,2,256,256]{3,2,1,0:T(8,128)(2,1)}, u32[]{:S(2)}) copy-start(bf16[2,2,256,256]{3,2,1,0:T(8,128)(2,1)} %param.16) | copy-start | bytes 1572868
  171.5 5.9 %copy-start.37 = (bf16[2,2,256,256]{3,2,1,0:T(8,128)(2,1)S(1)}, bf16[2,2,256,256]{3,2,1,0:T(8,128)(2,1)}, u32[]{:S(2)}) copy-start(bf16[2,2,256,256]{3,2,1,0:T(8,128)(2,1)} %param.16) | copy-start | bytes 1572868
  171.5 5.9 %copy-start.38 = (bf16[2,256,256]{2,1,0:T(8,128)(2,1)S(1)}, bf16[2,256,256]{2,1,0:T(8,128)(2,1)}, u32[]{:S(2)}) copy-start(bf16[2,256,256]{2,1,0:T(8,128)(2,1)} %param.17) | copy-start | bytes 786436
  173.4 3.9 %collective-permute-start.4 = (bf16[256,128]{0,1:T(8,128)(2,1)S(1)}, bf16[256,128]{0,1:T(8,128)(2,1)S(1)}, u32[]{:S(2)}, u32[]{:S(2)}) collective-permute-start(bf16[256,128]{0,1:T(8,128)(2,1)S(1)} %get-tuple-element.42), channel_id=1, source_target_pairs={{0,8},{8,16},{16,24},{24,32},{32,40},{40,48},{48,56},{56,64},{64,7... | collective-permute-start | bytes 196616 | tf_op jit(solution)/shard_map/ppermute | solution.py:189

commit v2 on v0

v2 whole, which is shorter than its diff:
```python
import functools

import jax
import jax.numpy as jnp
from jax import lax
from jax.experimental import pallas as pl
from jax.experimental.pallas import tpu as pltpu
from jax.sharding import Mesh
from jax.sharding import PartitionSpec as P

Z, X, C, Y = "z", "x", "c", "y"
F32, F16, BF16 = jnp.float32, jnp.float16, jnp.bfloat16
EXTRA = 8


def split(values):
    high = values.astype(BF16)
    return high, (values - high.astype(F32)).astype(BF16)


def product(left_side, right_side):
    left_high, left_low = split(left_side)
    right_high, right_low = split(right_side)
    rows = left_side.shape[0]
    dot = functools.partial(jnp.dot, preferred_element_type=F32)
    high = dot(jnp.concatenate([left_high, left_low], axis=0), right_high)
    return high[:rows] + (high[rows:] + dot(left_high, right_low))


def exponent(values, axis):
    largest = jnp.max(jnp.abs(values), axis=axis, keepdims=True)
    return jnp.clip(jnp.floor(jnp.log2(jnp.maximum(largest, 1e-36))), -120.0, 120.0)


def choose(condition, one, other):
    flags = jnp.zeros(one.shape, jnp.int32) + condition.astype(jnp.int32)
    return jnp.where(flags != 0, one, other)


def kernel(body, out_shapes, *operands, flops=0):
    moved = sum(o.size * o.dtype.itemsize for o in operands)
    moved += sum(o.size * o.dtype.itemsize for o in out_shapes)
    return pl.pallas_call(
        body,
        out_shape=out_shapes,
        in_specs=[
            pl.BlockSpec(memory_space=pltpu.SMEM if o.dtype == jnp.int32 else pltpu.VMEM)
            for o in operands
        ],
        out_specs=[pl.BlockSpec(memory_space=pltpu.VMEM) for _ in out_shapes],
        compiler_params=pltpu.CompilerParams(vmem_limit_bytes=16 * 2**20),
        cost_estimate=pl.CostEstimate(flops=flops, bytes_accessed=moved, transcendentals=0),
    )(*operands)


def shape(*dims, dtype=F32):
    return jax.ShapeDtypeStruct(dims, dtype)


def half_rows(core, values):
    rows = values.shape[0] // 2
    return choose(core == 0, values[:rows], values[rows:])


def half_columns(core, values):
    columns = values.shape[1] // 2
    return choose(core == 0, values[:, :columns], values[:, columns:])


def encode(wire_ref, index, values):
    rows, columns = values.shape
    k = exponent(values, 0)
    wire_ref[index + (slice(0, rows), slice(None))] = values * jnp.exp2(-k)
    wire_ref[index + (slice(rows, rows + EXTRA), slice(None))] = jnp.broadcast_to(
        k, (EXTRA, columns)
    )


def decode(ref, i, columns):
    rows = ref.shape[1] - EXTRA
    return ref[i, 0:rows, columns] * jnp.exp2(ref[i, rows : rows + 1, columns])


class Wires:
    def __init__(self, core, mine_ref, other_ref):
        self.core, self.refs = core, (mine_ref, other_ref)
        self.count = mine_ref.shape[0]
        self.width = 2 * (mine_ref.shape[1] - EXTRA)

    def in_order(self, i, columns):
        mine, other = (decode(ref, i, columns) for ref in self.refs)
        return [choose(self.core == 0, mine, other), choose(self.core == 0, other, mine)]

    def matrix(self, i, columns=None):
        columns = slice(0, self.width) if columns is None else columns
        return jnp.concatenate(self.in_order(i, columns), axis=0)

    def values(self, i, columns):
        return jnp.concatenate(self.in_order(i, columns), axis=1)

    def part(self, i, columns):
        return decode(self.refs[0], i, columns)


def pair_columns(width):
    part = width // 2
    starts = [0, width, 2 * width, 3 * width, 3 * width + part, 3 * width + 2 * part]
    return [slice(a, b) for a, b in zip(starts[:-1], starts[1:])]


def encode_rows_kernel(blocks_ref, wire_ref):
    rows, columns = blocks_ref.shape
    width = columns // 4
    exponents = []
    for i in range(4):
        values = blocks_ref[:, width * i : width * (i + 1)]
        k = exponent(values, 1)
        wire_ref[:, width * i : width * (i + 1)] = values * jnp.exp2(-k)
        exponents.append(jnp.broadcast_to(k, (rows, 128 // 4)))
    wire_ref[:, columns:] = jnp.concatenate(exponents, axis=1)


def factors_kernel(wire_ref, rhs_ref, own_ref, right_ref, out_ref, next_ref):
    width = rhs_ref.shape[0]
    room = 128 // 4

    def block(i):
        start = 4 * width + room * i
        k = wire_ref[:, start : start + 1]
        return (wire_ref[:, width * i : width * (i + 1)] * jnp.exp2(k)).T

    source = (rhs_ref[...] - own_ref[...] - right_ref[...]).T
    both = product(jnp.concatenate([-block(1), source], axis=0), block(0))
    upper_inverse = block(2)
    out_ref[0:width] = both[:width]
    backward = product(-block(3), upper_inverse)
    out_ref[width : 2 * width] = backward
    out_ref[2 * width : 3 * width] = upper_inverse
    encode(next_ref, (), jnp.concatenate([backward, upper_inverse], axis=1))
    out_ref[3 * width :] = both[width:]


def both_cores(core, mine_ref, other_ref, start, end):
    mine, other = mine_ref[start:end], other_ref[start:end]
    return choose(core == 0, mine, other), choose(core == 0, other, mine)


def pair_kernel(place_ref, mine_ref, other_ref, wire_ref):
    core = place_ref[0]
    width = mine_ref.shape[1]
    both = functools.partial(both_cores, core, mine_ref, other_ref)
    forward_first, forward_second = both(0, width)
    backward_first, backward_second = both(width, 2 * width)
    inverse_first, inverse_second = both(2 * width, 3 * width)
    offset_first, offset_second = both(3 * width, mine_ref.shape[0])
    part = width // 2
    start = jnp.concatenate([half_rows(core, forward_first), offset_first], axis=0)
    end = product(start, forward_second)
    forward, value = end[:part], end[part:] + offset_second
    back = product(jnp.concatenate([forward, value], axis=0), inverse_second)
    back = jnp.concatenate([back, half_rows(core, backward_second)], axis=0)
    back = product(back, backward_first)
    rows = start.shape[0]
    through = product(start, inverse_first) + back[:rows]
    whole = [
        forward,
        back[rows:],
        through[:part],
        half_columns(core, value),
        half_columns(core, through[part:]),
    ]
    encode(wire_ref, (), jnp.concatenate(whole, axis=1))


def plane_kernel(place_ref, first_ref, second_ref, wire_ref):
    core = place_ref[0]
    pairs = Wires(core, first_ref, second_ref)
    part = pairs.width // 2
    forward, backward, _, value, _ = pair_columns(pairs.width)
    last = pairs.count - 1
    ahead = pairs.part(0, forward)
    ahead = jnp.concatenate([ahead, pairs.values(0, value)], axis=0)
    behind = pairs.part(last, backward)
    for i in range(1, pairs.count):
        ahead = product(ahead, pairs.matrix(i, forward))
        further = ahead[part:] + pairs.values(i, value)
        ahead = jnp.concatenate([ahead[:part], further], axis=0)
        behind = product(behind, pairs.matrix(last - i, backward))
    further = half_columns(core, ahead[part:])
    encode(wire_ref, (0,), jnp.concatenate([ahead[:part], further], axis=1))
    encode(wire_ref, (1,), jnp.concatenate([behind, further], axis=1))


def forward_kernel(
    place_ref, plane_first, plane_second, pair_first, pair_second, wire_ref, through_ref, start_ref
):
    core, x, z = place_ref[0], place_ref[1], place_ref[2]
    planes, pairs = Wires(core, plane_first, plane_second), Wires(core, pair_first, pair_second)
    width = pairs.width
    forward, backward, through, value, back_value = pair_columns(width)
    received = jnp.zeros(start_ref.shape, F32)
    for i in range(planes.count - 1):
        further = planes.values(i, slice(width, None)) + product(received, planes.matrix(i))
        received = choose(z > i, further, received)
    ahead = []
    for i in range(pairs.count):
        ahead.append(received)
        if i < pairs.count - 1:
            received = pairs.values(i, value) + product(received, pairs.matrix(i, forward))
    behind = None
    for i in range(pairs.count - 1, -1, -1):
        own = pairs.values(i, back_value) + product(ahead[i], pairs.matrix(i, through))
        through_ref[i] = own
        if behind is not None:
            own = own + product(behind, pairs.matrix(i, backward))
        behind = own
    encode(wire_ref, (), half_columns(core, behind))
    start = ahead[0]
    for i in range(1, pairs.count):
        start = choose(x == i, ahead[i], start)
    start_ref[...] = start


def values_kernel(
    place_ref, start_ref, mine_ref, other_ref, previous_ref, first_ref, second_ref, before_ref
):
    core = place_ref[0]
    width = mine_ref.shape[1]
    start = start_ref[...]
    both = functools.partial(both_cores, core, mine_ref, other_ref)
    factor_first, factor_second = both(0, width)
    inverse_first, inverse_second = both(2 * width, 3 * width)
    offset_first, offset_second = both(3 * width, mine_ref.shape[0])
    forward_first = offset_first + product(start, factor_first)
    forward_second = offset_second + product(forward_first, factor_second)
    first_ref[...] = product(forward_first, inverse_first)
    second_ref[...] = product(forward_second, inverse_second)
    before_ref[...] = product(start, decode_previous(previous_ref, slice(width, None)))


def decode_previous(ref, columns):
    rows = ref.shape[0] - EXTRA
    return ref[0:rows, columns] * jnp.exp2(ref[rows : rows + 1, columns])


def backward_kernel(
    place_ref, size_ref, value_first, value_second, plane_first, plane_second,
    pair_first, pair_second, through_ref, mine_ref, other_ref, first_ref, second_ref, before_ref,
    previous_ref, leaf_forward_ref, leaf_upper_ref, leaf_upper_inv_ref, leaf_ref, sep_ref,
):
    core, x, z = place_ref[0], place_ref[1], place_ref[2]
    planes, pairs = Wires(core, plane_first, plane_second), Wires(core, pair_first, pair_second)
    values = Wires(core, value_first, value_second)
    width = pairs.width
    backward = pair_columns(width)[1]
    received = jnp.zeros(first_ref.shape, F32)
    for i in range(planes.count - 1, 0, -1):
        further = values.values(i, slice(None)) + product(received, planes.matrix(i))
        received = choose(z < i, further, received)
    chip = received
    for i in range(pairs.count - 1, 0, -1):
        received = through_ref[i] + product(received, pairs.matrix(i, backward))
        chip = choose(x < i, received, chip)
    factor_first, factor_second = both_cores(core, mine_ref, other_ref, width, 2 * width)
    second = second_ref[...] + product(chip, factor_second)
    first = first_ref[...] + product(second, factor_first)
    before = before_ref[...] + product(first, decode_previous(previous_ref, slice(0, width)))
    sep = choose(core == 0, first, second).T
    before = choose(core == 0, before, first).T.astype(BF16)
    sep_ref[...] = sep
    sep = sep.astype(BF16)
    dot = functools.partial(jnp.dot, preferred_element_type=F32)
    rows = lax.broadcasted_iota(jnp.int32, sep.shape, 0)
    for leaf in range(leaf_ref.shape[0]):
        back = leaf_forward_ref[leaf] - dot(leaf_upper_ref[leaf, 0], before)
        back = back - dot(leaf_upper_ref[leaf, 1], sep)
        result = dot(leaf_upper_inv_ref[leaf], back.astype(BF16))
        leaf_ref[leaf] = jnp.where(rows < size_ref[leaf], result, 0.0)


def to_all(block, axis):
    size = lax.axis_size(axis)
    slots = jnp.broadcast_to(block.astype(F16)[None], (size,) + block.shape)
    return lax.all_to_all(slots, axis, 0, 0, tiled=True)


def swap_cores(block):
    return lax.ppermute(block, C, [(0, 1), (1, 0)])


def in_order(core, block):
    other = swap_cores(block)
    return block.astype(F32), other.astype(F32)


def per_device(
    leaf_rhs,
    sep_rhs,
    leaf_size,
    leaf_lower_inv,
    leaf_lower,
    leaf_upper,
    leaf_upper_inv,
    sep_lower_inv,
    sep_lower,
    sep_upper_inv,
    sep_upper,
):
    panel = (Z, X, C)
    panels = lax.axis_size(panel)
    planes, chips = lax.axis_size(Z), lax.axis_size(X)
    z, x, core = lax.axis_index(Z), lax.axis_index(X), lax.axis_index(C)
    place = jnp.stack([core, x, z]).astype(jnp.int32)
    leaves, width, samples = leaf_rhs.shape

    blocks = [sep_lower_inv[0], sep_lower[0], sep_upper_inv[0], sep_upper[0]]
    blocks = jnp.concatenate(blocks, axis=1)
    (wire,) = kernel(
        encode_rows_kernel, [shape(blocks.shape[0], blocks.shape[1] + 128)], blocks
    )
    wire = to_all(wire, Y).reshape(width, -1).astype(F32)

    active_rows = (jnp.arange(width, dtype=jnp.int32)[None, :] < leaf_size[:, None]).astype(F32)[
        :, :, None
    ]
    leaf_rounded = (active_rows * leaf_rhs).astype(BF16)
    leaf_forward = active_rows * jnp.einsum(
        "lij,ljs->lis", leaf_lower_inv, leaf_rounded, preferred_element_type=F32
    )
    forward_rounded = leaf_forward.astype(BF16)
    left_terms = jnp.einsum(
        "lij,ljs->is", leaf_lower[:, 0], forward_rounded, preferred_element_type=F32
    )
    from_right = lax.ppermute(left_terms, panel, [(i + 1, i) for i in range(panels - 1)])
    own_terms = jnp.einsum(
        "lij,ljs->is", leaf_lower[:, 1], forward_rounded, preferred_element_type=F32
    )

    mine, previous = kernel(
        factors_kernel,
        [shape(3 * width + samples, width), shape(width + EXTRA, 2 * width)],
        wire,
        sep_rhs[0],
        own_terms,
        from_right,
    )
    other = swap_cores(mine)
    to_next_chip = [(i, i + 1) for i in range(1, panels - 1, 2)]
    previous = lax.ppermute(previous.astype(F16), panel, to_next_chip)
    rows = width // 2 + EXTRA
    (wire,) = kernel(pair_kernel, [shape(rows, 4 * width)], place, mine, other)

    wire, previous = lax.optimization_barrier((wire.astype(F16), previous))
    pairs = in_order(core, to_all(wire, X))
    previous = previous.astype(F32)
    (wire,) = kernel(plane_kernel, [shape(2, rows, width + width // 2)], place, *pairs)

    wire = wire.astype(F16)
    index = jnp.arange(planes, dtype=jnp.int32)[:, None, None]
    slots = jnp.where(index > z, wire[0][None], wire[1][None])
    between = in_order(core, lax.all_to_all(slots, Z, 0, 0, tiled=True))
    block = shape(samples, width)
    wire, through, start = kernel(
        forward_kernel,
        [shape(rows, width // 2), shape(chips, samples, width), block],
        place,
        *between,
        *pairs,
    )
    values = in_order(core, to_all(wire, Z))
    first, second, before = kernel(
        values_kernel, [block, block, block], place, start, mine, other, previous
    )

    leaf_correction, sep_correction = kernel(
        backward_kernel,
        [shape(leaves, width, samples), shape(width, samples)],
        place,
        leaf_size,
        *values,
        *between,
        *pairs,
        through,
        mine,
        other,
        first,
        second,
        before,
        previous,
        leaf_forward,
        leaf_upper,
        leaf_upper_inv,
    )
    return (leaf_correction, sep_correction[None])


def solution(mesh):
    cut = Mesh(mesh.devices.reshape(8, 4, 2, 8), (Z, X, C, Y))
    panel = (Z, X, C)
    return jax.shard_map(
        per_device,
        mesh=cut,
        in_specs=(
            P(panel, None, Y),
            P(panel, None, Y),
            P(panel),
            P(panel, None, None),
            P(panel, None, None, None),
            P(panel, None, None, None),
            P(panel, None, None),
            P(panel, Y, None),
            P(panel, Y, None),
            P(panel, Y, None),
            P(panel, Y, None),
        ),
        out_specs=(P(panel, None, Y), P(panel, None, Y)),
        check_vma=False,
    )
```

time: 1380 us -> 134 us (0.10)
  the two profiles are of different devices: /device:TPU:272 before, /device:TPU:1 now
where the time goes in v2:
time: 134 us; the launch traced here: 133 us
  blocking collectives  66.6 us (50%)
  starting transfers between devices  30.7 us (23%)
  waiting for transfers between devices  16.4 us (12%)
  Pallas kernels  13.3 us (10%)
  other arithmetic  2.29 us (2%)
  local copies, waits for them, and re-layouts  2.1 us (2%)
    all_to_all x2, blocking collectives, to_all(): return lax.all_to_all(slots, axis, 0, 0, tiled=True)  33.9 us
    all_to_all x1, blocking collectives, per_device(): between = in_order(core, lax.all_to_all(slots, Z, 0, 0, tiled=True))  32.7 us
    ppermute x4, starting transfers between devices, swap_cores(): return lax.ppermute(block, C, [(0, 1), (1, 0)])  15.2 us
    pallas_call x7, Pallas kernels, kernel(): pl.pallas_call(body, out_shape=out_shapes, in_specs=[pl.BlockSpec(memory_...  13.3 us
    all_to_all x1, waiting for transfers between devices, to_all(): return lax.all_to_all(slots, axis, 0, 0, tiled=True)  10.8 us
    all_to_all x1, starting transfers between devices, to_all(): return lax.all_to_all(slots, axis, 0, 0, tiled=True)  7.65 us
    ppermute x1, starting transfers between devices, per_device(): lax.ppermute(left_terms, panel, [(i + 1, i) for i in range(panels - 1)])  4.82 us
    ppermute x4, waiting for transfers between devices, swap_cores(): return lax.ppermute(block, C, [(0, 1), (1, 0)])  3.97 us
  transfers between devices with their start and end apart: 7, of which 4 were waited for; matrix products, arithmetic and copies ran while one was open for 1% of the time, Pallas kernels for 2%

profile of v2, /device:TPU:1, one launch (start us, length us, event | category | flops | bytes accessed | tf_op | source)
XLA Modules:
  0.0 133.1 jit_solution(1051134047028319109)
XLA Ops:
  0.6 0.0 copy-start
  0.6 0.9 pad_maximum_fusion.blocks_ref
  1.5 0.0 copy-start.4
  1.5 0.0 copy-start.6
  1.5 0.1 shard_map.122
  1.7 0.0 copy-start.5
  1.7 0.9 broadcast_in_dim.54
  2.6 7.7 %all-to-all-start = ((f16[8,32,1152]{2,1,0:T(8,128)(2,1)}), f16[8,32,1152]{2,1,0:T(8,128)(2,1)S(1)}, u32[]{:S(2)}, u32[]{:S(2)}) async-start(f16[8,32,1152]{2,1,0:T(8,128)(2,1)} %broadcast_in_dim.54), calls=%async_computation | async-start | bytes 1179648 | tf_op jit(solution)/shard_map/all_to_all | solution.py:284
  10.2 0.1 compare_convert_fusion
  10.3 0.3 fusion.leaf_forward_ref
  10.6 0.2 convolution_bitcast_fusion
  10.9 0.0 copy-start.3
  10.9 4.8 %collective-permute-start = (f32[256,128]{1,0:T(8,128)S(1)}, f32[256,128]{1,0:T(8,128)S(1)}, u32[]{:S(2)}, u32[]{:S(2)}) collective-permute-start(f32[256,128]{1,0:T(8,128)S(1)} %convolution_bitcast_fusion), channel_id=1, source_target_pairs={{8,0},{16,8},{24,16},{32,24},{40,32},{48,40},{56,48},{64,56},{72,6... | collective-permute-start | bytes 393224 | tf_op jit(solution)/shard_map/ppermute | solution.py:334
  15.7 0.2 convolution_bitcast_fusion.1.own_ref
  15.9 10.8 %all-to-all-done = f16[8,32,1152]{2,1,0:T(8,128)(2,1)S(1)} async-done(((f16[8,32,1152]{2,1,0:T(8,128)(2,1)}), f16[8,32,1152]{2,1,0:T(8,128)(2,1)S(1)}, u32[]{:S(2)}, u32[]{:S(2)}) %all-to-all-start) | async-done | bytes 589856 | tf_op jit(solution)/shard_map/all_to_all | solution.py:284
  26.7 0.1 bitcast_convert_fusion.wire_ref
  26.8 0.0 collective-permute-done.right_ref
  26.8 0.9 shard_map.123
  27.7 5.3 %collective-permute-start.1 = (f32[896,256]{1,0:T(8,128)S(1)}, f32[896,256]{1,0:T(8,128)S(1)}, u32[]{:S(2)}, u32[]{:S(2)}) collective-permute-start(f32[896,256]{1,0:T(8,128)S(1)} %get-tuple-element.14.mine_ref), channel_id=1, source_target_pairs={{0,8},{8,0},{1,9},{9,1},{2,10},{10,2},{3,11},{11,3},{4,12},{12,4},... | collective-permute-start | bytes 2752520 | tf_op jit(solution)/shard_map/ppermute | solution.py:288
  33.1 3.0 %collective-permute-start.2 = (f16[264,512]{1,0:T(8,128)(2,1)S(1)}, f16[264,512]{1,0:T(8,128)(2,1)S(1)}, u32[]{:S(2)}, u32[]{:S(2)}) collective-permute-start(f16[264,512]{1,0:T(8,128)(2,1)S(1)} %convert_element_type.61), channel_id=1, source_target_pairs={{8,16},{24,32},{40,48},{56,64},{72,80},{88,96},{104,112},{120,128}... | collective-permute-start | bytes 811016 | tf_op jit(solution)/shard_map/ppermute | solution.py:349
  36.1 0.1 pad_add_fusion.place_ref
  36.2 0.0 collective-permute-done.1.other_ref
  36.2 1.6 %shard_map.124 = f32[136,1024]{1,0:T(8,128)S(1)} custom-call(s32[3]{0:T(128)S(1)} %pad_add_fusion.place_ref, f32[896,256]{1,0:T(8,128)S(1)} %get-tuple-element.14.mine_ref, f32[896,256]{1,0:T(8,128)S(1)} %collective-permute-done.1.other_ref), custom_call_target="tpu_custom_call" | custom-call | bytes 2392076 | tf_op jit(solution)/shard_map/pallas_call | solution.py:43
  37.8 1.7 %collective-permute-done.2 = f16[264,512]{1,0:T(8,128)(2,1)S(1)} collective-permute-done((f16[264,512]{1,0:T(8,128)(2,1)S(1)}, f16[264,512]{1,0:T(8,128)(2,1)S(1)}, u32[]{:S(2)}, u32[]{:S(2)}) %collective-permute-start.2) | collective-permute-done | bytes 270368 | tf_op jit(solution)/shard_map/ppermute | solution.py:349
  39.5 0.1 broadcast_in_dim.55
  39.6 18.8 %all_to_all.20 = f16[4,136,1024]{2,1,0:T(8,128)(2,1)S(1)} all-to-all(f16[4,136,1024]{2,1,0:T(8,128)(2,1)S(1)} %broadcast_in_dim.55), channel_id=1, replica_groups=mesh['z'=8,'x'=4,'c'=2,'y'=8] {'x'}, dimensions={0} | all-to-all | bytes 2228224 | tf_op jit(solution)/shard_map/all_to_all | solution.py:284
  58.5 4.1 %collective-permute-start.3 = (f16[4,136,1024]{2,1,0:T(8,128)(2,1)S(1)}, f16[4,136,1024]{2,1,0:T(8,128)(2,1)S(1)}, u32[]{:S(2)}, u32[]{:S(2)}) collective-permute-start(f16[4,136,1024]{2,1,0:T(8,128)(2,1)S(1)} %all_to_all.20), channel_id=1, source_target_pairs={{0,8},{8,0},{1,9},{9,1},{2,10},{10,2},{3,11},{11,3},{4,12},{12,4},... | collective-permute-start | bytes 3342344 | tf_op jit(solution)/shard_map/ppermute | solution.py:288
  62.6 0.2 convert_element_type.62.first_ref.pair_first
  62.9 2.1 %collective-permute-done.3 = f16[4,136,1024]{2,1,0:T(8,128)(2,1)S(1)} collective-permute-done((f16[4,136,1024]{2,1,0:T(8,128)(2,1)S(1)}, f16[4,136,1024]{2,1,0:T(8,128)(2,1)S(1)}, u32[]{:S(2)}, u32[]{:S(2)}) %collective-permute-start.3) | collective-permute-done | bytes 1114144 | tf_op jit(solution)/shard_map/ppermute | solution.py:288
  65.0 0.2 convert_element_type.63.second_ref.pair_second
  65.2 1.5 %shard_map.125 = f32[2,136,384]{2,1,0:T(8,128)S(1)} custom-call(s32[3]{0:T(128)S(1)} %pad_add_fusion.place_ref, f32[4,136,1024]{2,1,0:T(8,128)S(1)} %convert_element_type.62.first_ref.pair_first, f32[4,136,1024]{2,1,0:T(8,128)S(1)} %convert_element_type.63.second_ref.pair_second), custom_call_target="tpu_custom_call" | custom-call | bytes 4874252 | tf_op jit(solution)/shard_map/pallas_call | solution.py:43
  66.8 0.2 broadcast_select_fusion
  67.0 32.7 %all_to_all.21 = f16[8,136,384]{2,1,0:T(8,128)(2,1)S(1)} all-to-all(f16[8,136,384]{2,1,0:T(8,128)(2,1)S(1)} %broadcast_select_fusion), channel_id=1, replica_groups=mesh['z'=8,'x'=4,'c'=2,'y'=8] {'z'}, dimensions={0} | all-to-all | bytes 1671168 | tf_op jit(solution)/shard_map/all_to_all | solution.py:361
  99.7 3.3 %collective-permute-start.4 = (f16[8,136,384]{2,1,0:T(8,128)(2,1)S(1)}, f16[8,136,384]{2,1,0:T(8,128)(2,1)S(1)}, u32[]{:S(2)}, u32[]{:S(2)}) collective-permute-start(f16[8,136,384]{2,1,0:T(8,128)(2,1)S(1)} %all_to_all.21), channel_id=1, source_target_pairs={{0,8},{8,0},{1,9},{9,1},{2,10},{10,2},{3,11},{11,3},{4,12},{12,4},... | collective-permute-start | bytes 2506760 | tf_op jit(solution)/shard_map/ppermute | solution.py:288
  103.0 0.1 convert_element_type.65.plane_first
  103.2 1.8 %collective-permute-done.4 = f16[8,136,384]{2,1,0:T(8,128)(2,1)S(1)} collective-permute-done((f16[8,136,384]{2,1,0:T(8,128)(2,1)S(1)}, f16[8,136,384]{2,1,0:T(8,128)(2,1)S(1)}, u32[]{:S(2)}, u32[]{:S(2)}) %collective-permute-start.4) | collective-permute-done | bytes 835616 | tf_op jit(solution)/shard_map/ppermute | solution.py:288
  105.0 0.1 convert_element_type.66.plane_second
  105.1 3.4 %shard_map.126 = (f32[136,128]{1,0:T(8,128)S(1)}, f32[4,128,256]{2,1,0:T(8,128)S(1)}, f32[128,256]{1,0:T(8,128)S(1)}) custom-call(s32[3]{0:T(128)S(1)} %pad_add_fusion.place_ref, f32[8,136,384]{2,1,0:T(8,128)S(1)} %convert_element_type.65.plane_first, f32[8,136,384]{2,1,0:T(8,128)S(1)} %convert_element_type.66.plane_second, ...), custom_call_target="tpu_custom_call" | custom-call | bytes 8523788 | tf_op jit(solution)/shard_map/pallas_call | solution.py:43
  108.6 15.1 %all_to_all.22 = f16[8,136,128]{2,1,0:T(8,128)(2,1)S(1)} all-to-all(f16[8,136,128]{2,1,0:T(8,128)(2,1)S(1)} %broadcast_in_dim.60), channel_id=1, replica_groups=mesh['z'=8,'x'=4,'c'=2,'y'=8] {'z'}, dimensions={0} | all-to-all | bytes 557056 | tf_op jit(solution)/shard_map/all_to_all | solution.py:284
  123.7 2.4 %collective-permute-start.5 = (f16[8,136,128]{2,1,0:T(8,128)(2,1)S(1)}, f16[8,136,128]{2,1,0:T(8,128)(2,1)S(1)}, u32[]{:S(2)}, u32[]{:S(2)}) collective-permute-start(f16[8,136,128]{2,1,0:T(8,128)(2,1)S(1)} %all_to_all.22), channel_id=1, source_target_pairs={{0,8},{8,0},{1,9},{9,1},{2,10},{10,2},{3,11},{11,3},{4,12},{12,4},... | collective-permute-start | bytes 835592 | tf_op jit(solution)/shard_map/ppermute | solution.py:288
  126.1 0.1 convert_element_type.70.previous_ref
  126.2 1.2 shard_map.127
  127.4 0.0 copy-start.1
  127.4 0.0 copy-start.2
  127.5 0.0 collective-permute-done.5
  127.5 0.9 copy-done.1
  128.4 0.1 copy-done.2
  128.5 4.6 %shard_map.128 = (f32[2,256,128]{2,1,0:T(8,128)}, f32[256,128]{1,0:T(8,128)}) custom-call(s32[3]{0:T(128)S(1)} %pad_add_fusion.place_ref, s32[2]{0:T(128)S(1)} %copy-done.4, f32[8,136,128]{2,1,0:T(8,128)S(1)} %convert_element_type.68.value_first, f32[8,136,128]{2,1,0:T(8,128)S(1)} %convert_element_type.69.value_second, ...), custom_call_target="tpu_custom_call" | custom-call | bytes 13647892 | tf_op jit(solution)/shard_map/pallas_call | solution.py:43
  (15 shorter events, 0.3 us)
Async XLA Ops:
  0.6 9.7 %copy-start = (bf16[2,256,256]{2,1,0:T(8,128)(2,1)S(1)}, bf16[2,256,256]{2,1,0:T(8,128)(2,1)}, u32[]{:S(2)}) copy-start(bf16[2,256,256]{2,1,0:T(8,128)(2,1)} %param.14) | copy-start | bytes 786436
  1.5 8.7 %copy-start.4 = (s32[2]{0:T(128)S(1)}, s32[2]{0:T(128)}, u32[]{:S(2)}) copy-start(s32[2]{0:T(128)} %size_ref.1) | copy-start | bytes 28
  1.5 8.8 %copy-start.6 = (f32[2,256,128]{2,1,0:T(8,128)S(1)}, f32[2,256,128]{2,1,0:T(8,128)}, u32[]{:S(2)}) copy-start(f32[2,256,128]{2,1,0:T(8,128)} %param.11) | copy-start | bytes 786436
  1.7 9.0 %copy-start.5 = (bf16[2,2,256,256]{3,2,1,0:T(8,128)(2,1)S(1)}, bf16[2,2,256,256]{3,2,1,0:T(8,128)(2,1)}, u32[]{:S(2)}) copy-start(bf16[2,2,256,256]{3,2,1,0:T(8,128)(2,1)} %param.15) | copy-start | bytes 1572868
  2.6 24.1 %all-to-all-start = ((f16[8,32,1152]{2,1,0:T(8,128)(2,1)}), f16[8,32,1152]{2,1,0:T(8,128)(2,1)S(1)}, u32[]{:S(2)}, u32[]{:S(2)}) async-start(f16[8,32,1152]{2,1,0:T(8,128)(2,1)} %broadcast_in_dim.54), calls=%async_computation | async-start | bytes 1179648 | tf_op jit(solution)/shard_map/all_to_all | solution.py:284
  10.9 16.0 %copy-start.3 = (f32[1,256,128]{2,1,0:T(8,128)S(1)}, f32[1,256,128]{2,1,0:T(8,128)}, u32[]{:S(2)}) copy-start(f32[1,256,128]{2,1,0:T(8,128)} %param.12) | copy-start | bytes 393220
  10.9 15.9 %collective-permute-start = (f32[256,128]{1,0:T(8,128)S(1)}, f32[256,128]{1,0:T(8,128)S(1)}, u32[]{:S(2)}, u32[]{:S(2)}) collective-permute-start(f32[256,128]{1,0:T(8,128)S(1)} %convolution_bitcast_fusion), channel_id=1, source_target_pairs={{8,0},{16,8},{24,16},{32,24},{40,32},{48,40},{56,48},{64,56},{72,6... | collective-permute-start | bytes 393224 | tf_op jit(solution)/shard_map/ppermute | solution.py:334
  27.7 8.5 %collective-permute-start.1 = (f32[896,256]{1,0:T(8,128)S(1)}, f32[896,256]{1,0:T(8,128)S(1)}, u32[]{:S(2)}, u32[]{:S(2)}) collective-permute-start(f32[896,256]{1,0:T(8,128)S(1)} %get-tuple-element.14.mine_ref), channel_id=1, source_target_pairs={{0,8},{8,0},{1,9},{9,1},{2,10},{10,2},{3,11},{11,3},{4,12},{12,4},... | collective-permute-start | bytes 2752520 | tf_op jit(solution)/shard_map/ppermute | solution.py:288
  33.1 6.4 %collective-permute-start.2 = (f16[264,512]{1,0:T(8,128)(2,1)S(1)}, f16[264,512]{1,0:T(8,128)(2,1)S(1)}, u32[]{:S(2)}, u32[]{:S(2)}) collective-permute-start(f16[264,512]{1,0:T(8,128)(2,1)S(1)} %convert_element_type.61), channel_id=1, source_target_pairs={{8,16},{24,32},{40,48},{56,64},{72,80},{88,96},{104,112},{120,128}... | collective-permute-start | bytes 811016 | tf_op jit(solution)/shard_map/ppermute | solution.py:349
  58.5 6.5 %collective-permute-start.3 = (f16[4,136,1024]{2,1,0:T(8,128)(2,1)S(1)}, f16[4,136,1024]{2,1,0:T(8,128)(2,1)S(1)}, u32[]{:S(2)}, u32[]{:S(2)}) collective-permute-start(f16[4,136,1024]{2,1,0:T(8,128)(2,1)S(1)} %all_to_all.20), channel_id=1, source_target_pairs={{0,8},{8,0},{1,9},{9,1},{2,10},{10,2},{3,11},{11,3},{4,12},{12,4},... | collective-permute-start | bytes 3342344 | tf_op jit(solution)/shard_map/ppermute | solution.py:288
  99.7 5.3 %collective-permute-start.4 = (f16[8,136,384]{2,1,0:T(8,128)(2,1)S(1)}, f16[8,136,384]{2,1,0:T(8,128)(2,1)S(1)}, u32[]{:S(2)}, u32[]{:S(2)}) collective-permute-start(f16[8,136,384]{2,1,0:T(8,128)(2,1)S(1)} %all_to_all.21), channel_id=1, source_target_pairs={{0,8},{8,0},{1,9},{9,1},{2,10},{10,2},{3,11},{11,3},{4,12},{12,4},... | collective-permute-start | bytes 2506760 | tf_op jit(solution)/shard_map/ppermute | solution.py:288
  123.7 3.8 %collective-permute-start.5 = (f16[8,136,128]{2,1,0:T(8,128)(2,1)S(1)}, f16[8,136,128]{2,1,0:T(8,128)(2,1)S(1)}, u32[]{:S(2)}, u32[]{:S(2)}) collective-permute-start(f16[8,136,128]{2,1,0:T(8,128)(2,1)S(1)} %all_to_all.22), channel_id=1, source_target_pairs={{0,8},{8,0},{1,9},{9,1},{2,10},{10,2},{3,11},{11,3},{4,12},{12,4},... | collective-permute-start | bytes 835592 | tf_op jit(solution)/shard_map/ppermute | solution.py:288
  127.4 1.0 copy-start.1
  127.4 1.1 copy-start.2

commit v3 on v2

--- a/solution.py
+++ b/solution.py
@@ -10,7 +10,7 @@
 
 Z, X, C, Y = "z", "x", "c", "y"
 F32, F16, BF16 = jnp.float32, jnp.float16, jnp.bfloat16
-EXTRA = 8
+LANES, EXTRA = 128, 8
 
 
 def split(values):
@@ -67,28 +67,40 @@
     return choose(core == 0, values[:, :columns], values[:, columns:])
 
 
+def wire_shape(*dims):
+    *outer, rows, columns = dims
+    return shape(*outer, columns // LANES * rows + EXTRA, LANES)
+
+
 def encode(wire_ref, index, values):
     rows, columns = values.shape
     k = exponent(values, 0)
-    wire_ref[index + (slice(0, rows), slice(None))] = values * jnp.exp2(-k)
-    wire_ref[index + (slice(rows, rows + EXTRA), slice(None))] = jnp.broadcast_to(
-        k, (EXTRA, columns)
-    )
-
-
-def decode(ref, i, columns):
-    rows = ref.shape[1] - EXTRA
-    return ref[i, 0:rows, columns] * jnp.exp2(ref[i, rows : rows + 1, columns])
+    scaled = values * jnp.exp2(-k)
+    count = columns // LANES
+    wire_ref[index + (slice(count * rows, None),)] = jnp.zeros((EXTRA, LANES), F32)
+    for b in range(count):
+        block = slice(LANES * b, LANES * (b + 1))
+        wire_ref[index + (slice(rows * b, rows * (b + 1)),)] = scaled[:, block]
+        wire_ref[index + (slice(count * rows + b, count * rows + b + 1),)] = k[:, block]
+
+
+def decode(ref, index, rows, columns):
+    count = (ref.shape[-2] - EXTRA) // rows
+    blocks = []
+    for b in range(columns.start // LANES, columns.stop // LANES):
+        k = ref[index + (slice(count * rows + b, count * rows + b + 1),)]
+        blocks.append(ref[index + (slice(rows * b, rows * (b + 1)),)] * jnp.exp2(k))
+    return jnp.concatenate(blocks, axis=1)
 
 
 class Wires:
     def __init__(self, core, mine_ref, other_ref):
         self.core, self.refs = core, (mine_ref, other_ref)
-        self.count = mine_ref.shape[0]
-        self.width = 2 * (mine_ref.shape[1] - EXTRA)
+        self.count, self.part = mine_ref.shape[0], mine_ref.shape[2]
+        self.width = 2 * self.part
 
     def in_order(self, i, columns):
-        mine, other = (decode(ref, i, columns) for ref in self.refs)
+        mine, other = (decode(ref, (i,), self.part, columns) for ref in self.refs)
         return [choose(self.core == 0, mine, other), choose(self.core == 0, other, mine)]
 
     def matrix(self, i, columns=None):
@@ -98,8 +110,8 @@
     def values(self, i, columns):
         return jnp.concatenate(self.in_order(i, columns), axis=1)
 
-    def part(self, i, columns):
-        return decode(self.refs[0], i, columns)
+    def own_part(self, i, columns):
+        return decode(self.refs[0], (i,), self.part, columns)
 
 
 def pair_columns(width):
@@ -109,25 +121,17 @@
 
 
 def encode_rows_kernel(blocks_ref, wire_ref):
-    rows, columns = blocks_ref.shape
-    width = columns // 4
-    exponents = []
-    for i in range(4):
-        values = blocks_ref[:, width * i : width * (i + 1)]
-        k = exponent(values, 1)
-        wire_ref[:, width * i : width * (i + 1)] = values * jnp.exp2(-k)
-        exponents.append(jnp.broadcast_to(k, (rows, 128 // 4)))
-    wire_ref[:, columns:] = jnp.concatenate(exponents, axis=1)
+    encode(wire_ref, (), blocks_ref[...])
 
 
 def factors_kernel(wire_ref, rhs_ref, own_ref, right_ref, out_ref, next_ref):
     width = rhs_ref.shape[0]
-    room = 128 // 4
+    senders = wire_ref.shape[0]
 
     def block(i):
-        start = 4 * width + room * i
-        k = wire_ref[:, start : start + 1]
-        return (wire_ref[:, width * i : width * (i + 1)] * jnp.exp2(k)).T
+        columns = slice(width * i, width * (i + 1))
+        rows = [decode(wire_ref, (j,), width // senders, columns) for j in range(senders)]
+        return jnp.concatenate(rows, axis=0).T
 
     source = (rhs_ref[...] - own_ref[...] - right_ref[...]).T
     both = product(jnp.concatenate([-block(1), source], axis=0), block(0))
@@ -178,9 +182,9 @@
     part = pairs.width // 2
     forward, backward, _, value, _ = pair_columns(pairs.width)
     last = pairs.count - 1
-    ahead = pairs.part(0, forward)
+    ahead = pairs.own_part(0, forward)
     ahead = jnp.concatenate([ahead, pairs.values(0, value)], axis=0)
-    behind = pairs.part(last, backward)
+    behind = pairs.own_part(last, backward)
     for i in range(1, pairs.count):
         ahead = product(ahead, pairs.matrix(i, forward))
         further = ahead[part:] + pairs.values(i, value)
@@ -191,42 +195,59 @@
     encode(wire_ref, (1,), jnp.concatenate([behind, further], axis=1))
 
 
-def forward_kernel(
-    place_ref, plane_first, plane_second, pair_first, pair_second, wire_ref, through_ref, start_ref
-):
-    core, x, z = place_ref[0], place_ref[1], place_ref[2]
-    planes, pairs = Wires(core, plane_first, plane_second), Wires(core, pair_first, pair_second)
+def through_kernel(place_ref, mine_ref, other_ref, factor_ref, value_ref):
+    pairs = Wires(place_ref[0], mine_ref, other_ref)
     width = pairs.width
     forward, backward, through, value, back_value = pair_columns(width)
-    received = jnp.zeros(start_ref.shape, F32)
+
+    def add_value(block, further):
+        return jnp.concatenate([block[:width], block[width:] + further], axis=0)
+
+    ahead = jnp.concatenate([pairs.matrix(0, forward), pairs.values(0, value)], axis=0)
+    own = [jnp.concatenate([pairs.matrix(0, through), pairs.values(0, back_value)], axis=0)]
+    for i in range(1, pairs.count):
+        further = product(ahead, pairs.matrix(i, through))
+        own.append(add_value(further, pairs.values(i, back_value)))
+        if i < pairs.count - 1:
+            further = product(ahead, pairs.matrix(i, forward))
+            ahead = add_value(further, pairs.values(i, value))
+    behind = own[-1]
+    for i in range(pairs.count - 2, -1, -1):
+        behind = own[i] + product(behind, pairs.matrix(i, backward))
+    factor_ref[...] = behind[:width]
+    value_ref[...] = behind[width:]
+
+
+def forward_kernel(
+    place_ref, plane_mine, plane_other, factor_ref, value_ref, wire_ref, ahead_ref
+):
+    core, z = place_ref[0], place_ref[2]
+    planes = Wires(core, plane_mine, plane_other)
+    width = planes.width
+    received = jnp.zeros(ahead_ref.shape, F32)
     for i in range(planes.count - 1):
-        further = planes.values(i, slice(width, None)) + product(received, planes.matrix(i))
-        received = choose(z > i, further, received)
-    ahead = []
-    for i in range(pairs.count):
-        ahead.append(received)
-        if i < pairs.count - 1:
-            received = pairs.values(i, value) + product(received, pairs.matrix(i, forward))
-    behind = None
-    for i in range(pairs.count - 1, -1, -1):
-        own = pairs.values(i, back_value) + product(ahead[i], pairs.matrix(i, through))
-        through_ref[i] = own
-        if behind is not None:
-            own = own + product(behind, pairs.matrix(i, backward))
-        behind = own
+        offset = planes.values(i, slice(width, width + planes.part))
+        received = choose(z > i, offset + product(received, planes.matrix(i)), received)
+    ahead_ref[...] = received
+    behind = value_ref[...] + product(received, factor_ref[...])
     encode(wire_ref, (), half_columns(core, behind))
-    start = ahead[0]
+
+
+def values_kernel(
+    place_ref, ahead_ref, pair_mine, pair_other, mine_ref, other_ref, previous_ref,
+    through_ref, first_ref, second_ref, before_ref,
+):
+    core, x = place_ref[0], place_ref[1]
+    pairs = Wires(core, pair_mine, pair_other)
+    width = pairs.width
+    forward, _, through, value, back_value = pair_columns(width)
+    ahead = ahead_ref[...]
+    start = ahead
+    through_ref[0] = jnp.zeros(ahead.shape, F32)
     for i in range(1, pairs.count):
-        start = choose(x == i, ahead[i], start)
-    start_ref[...] = start
-
-
-def values_kernel(
-    place_ref, start_ref, mine_ref, other_ref, previous_ref, first_ref, second_ref, before_ref
-):
-    core = place_ref[0]
-    width = mine_ref.shape[1]
-    start = start_ref[...]
+        ahead = pairs.values(i - 1, value) + product(ahead, pairs.matrix(i - 1, forward))
+        start = choose(x == i, ahead, start)
+        through_ref[i] = pairs.values(i, back_value) + product(ahead, pairs.matrix(i, through))
     both = functools.partial(both_cores, core, mine_ref, other_ref)
     factor_first, factor_second = both(0, width)
     inverse_first, inverse_second = both(2 * width, 3 * width)
@@ -235,12 +256,8 @@
     forward_second = offset_second + product(forward_first, factor_second)
     first_ref[...] = product(forward_first, inverse_first)
     second_ref[...] = product(forward_second, inverse_second)
-    before_ref[...] = product(start, decode_previous(previous_ref, slice(width, None)))
-
-
-def decode_previous(ref, columns):
-    rows = ref.shape[0] - EXTRA
-    return ref[0:rows, columns] * jnp.exp2(ref[rows : rows + 1, columns])
+    previous = decode(previous_ref, (), width, slice(width, 2 * width))
+    before_ref[...] = product(start, previous)
 
 
 def backward_kernel(
@@ -255,7 +272,7 @@
     backward = pair_columns(width)[1]
     received = jnp.zeros(first_ref.shape, F32)
     for i in range(planes.count - 1, 0, -1):
-        further = values.values(i, slice(None)) + product(received, planes.matrix(i))
+        further = values.values(i, slice(0, values.part)) + product(received, planes.matrix(i))
         received = choose(z < i, further, received)
     chip = received
     for i in range(pairs.count - 1, 0, -1):
@@ -264,7 +281,8 @@
     factor_first, factor_second = both_cores(core, mine_ref, other_ref, width, 2 * width)
     second = second_ref[...] + product(chip, factor_second)
     first = first_ref[...] + product(second, factor_first)
-    before = before_ref[...] + product(first, decode_previous(previous_ref, slice(0, width)))
+    previous = decode(previous_ref, (), width, slice(0, width))
+    before = before_ref[...] + product(first, previous)
     sep = choose(core == 0, first, second).T
     before = choose(core == 0, before, first).T.astype(BF16)
     sep_ref[...] = sep
@@ -316,9 +334,9 @@
     blocks = [sep_lower_inv[0], sep_lower[0], sep_upper_inv[0], sep_upper[0]]
     blocks = jnp.concatenate(blocks, axis=1)
     (wire,) = kernel(
-        encode_rows_kernel, [shape(blocks.shape[0], blocks.shape[1] + 128)], blocks
-    )
-    wire = to_all(wire, Y).reshape(width, -1).astype(F32)
+        encode_rows_kernel, [wire_shape(*blocks.shape)], blocks
+    )
+    wire = to_all(wire, Y).astype(F32)
 
     active_rows = (jnp.arange(width, dtype=jnp.int32)[None, :] < leaf_size[:, None]).astype(F32)[
         :, :, None
@@ -338,7 +356,7 @@
 
     mine, previous = kernel(
         factors_kernel,
-        [shape(3 * width + samples, width), shape(width + EXTRA, 2 * width)],
+        [shape(3 * width + samples, width), wire_shape(width, 2 * width)],
         wire,
         sep_rhs[0],
         own_terms,
@@ -347,29 +365,35 @@
     other = swap_cores(mine)
     to_next_chip = [(i, i + 1) for i in range(1, panels - 1, 2)]
     previous = lax.ppermute(previous.astype(F16), panel, to_next_chip)
-    rows = width // 2 + EXTRA
-    (wire,) = kernel(pair_kernel, [shape(rows, 4 * width)], place, mine, other)
+    part = width // 2
+    (wire,) = kernel(pair_kernel, [wire_shape(part, 4 * width)], place, mine, other)
 
     wire, previous = lax.optimization_barrier((wire.astype(F16), previous))
     pairs = in_order(core, to_all(wire, X))
     previous = previous.astype(F32)
-    (wire,) = kernel(plane_kernel, [shape(2, rows, width + width // 2)], place, *pairs)
+    (wire,) = kernel(plane_kernel, [wire_shape(2, part, width + part)], place, *pairs)
 
     wire = wire.astype(F16)
     index = jnp.arange(planes, dtype=jnp.int32)[:, None, None]
     slots = jnp.where(index > z, wire[0][None], wire[1][None])
     between = in_order(core, lax.all_to_all(slots, Z, 0, 0, tiled=True))
     block = shape(samples, width)
-    wire, through, start = kernel(
-        forward_kernel,
-        [shape(rows, width // 2), shape(chips, samples, width), block],
+    through = kernel(
+        through_kernel, [shape(width, width), shape(samples, width)], place, *pairs
+    )
+    wire, ahead = kernel(
+        forward_kernel, [wire_shape(part, part), block], place, *between, *through
+    )
+    values = in_order(core, to_all(wire, Z))
+    through, first, second, before = kernel(
+        values_kernel,
+        [shape(chips, samples, width), block, block, block],
         place,
-        *between,
+        ahead,
         *pairs,
-    )
-    values = in_order(core, to_all(wire, Z))
-    first, second, before = kernel(
-        values_kernel, [block, block, block], place, start, mine, other, previous
+        mine,
+        other,
+        previous,
     )
 
     leaf_correction, sep_correction = kernel(

time: 134 us -> 131 us (0.978)
  waiting for transfers between devices: 16.4 us -> 13.3 us
  Pallas kernels: 13.3 us -> 15.5 us
    pallas_call x7 -> x8, Pallas kernels: 13.3 us -> 15.5 us  [kernel(): pl.pallas_call(body, out_shape=out_shapes, in_specs=[pl.BlockSpec(memory_...]
    ppermute x4, waiting for transfers between devices: 3.97 us -> 2.12 us  [swap_cores(): return lax.ppermute(block, C, [(0, 1), (1, 0)])]
  transfers between devices with their start and end apart: 7 -> 7, of which waited for: 4 -> 3; matrix products, arithmetic and copies ran while one was open for 1% -> 1% of each run, Pallas kernels for 2% -> 5%
where the time goes in v3:
time: 131 us
  blocking collectives  65.5 us (50%)
  starting transfers between devices  30.6 us (23%)
  Pallas kernels  15.5 us (12%)
  waiting for transfers between devices  13.3 us (10%)
  local copies, waits for them, and re-layouts  2.12 us (2%)
  other arithmetic  2.11 us (2%)
    all_to_all x2, blocking collectives, to_all(): return lax.all_to_all(slots, axis, 0, 0, tiled=True)  33.4 us
    all_to_all x1, blocking collectives, per_device(): between = in_order(core, lax.all_to_all(slots, Z, 0, 0, tiled=True))  32.1 us
    pallas_call x8, Pallas kernels, kernel(): pl.pallas_call(body, out_shape=out_shapes, in_specs=[pl.BlockSpec(memory_...  15.5 us
    ppermute x4, starting transfers between devices, swap_cores(): return lax.ppermute(block, C, [(0, 1), (1, 0)])  15.3 us
    all_to_all x1, waiting for transfers between devices, to_all(): return lax.all_to_all(slots, axis, 0, 0, tiled=True)  9.57 us
    all_to_all x1, starting transfers between devices, to_all(): return lax.all_to_all(slots, axis, 0, 0, tiled=True)  7.65 us
    ppermute x1, starting transfers between devices, per_device(): lax.ppermute(left_terms, panel, [(i + 1, i) for i in range(panels - 1)])  4.68 us
    ppermute x1, starting transfers between devices, per_device(): previous = lax.ppermute(previous.astype(F16), panel, to_next_chip)  3.03 us
  transfers between devices with their start and end apart: 7, of which 3 were waited for; matrix products, arithmetic and copies ran while one was open for 1% of the time, Pallas kernels for 5%

profile of v3, /device:TPU:1, one launch (start us, length us, event | category | flops | bytes accessed | tf_op | source)
XLA Modules:
  0.0 130.9 jit_solution(11236910552511324962)
XLA Ops:
  0.6 0.0 copy-start
  0.6 0.0 copy-start.4
  0.7 0.0 copy-start.6
  0.7 0.9 pad_maximum_fusion.blocks_ref
  1.6 0.9 broadcast_in_dim.54
  2.5 7.7 %all-to-all-start = ((f16[8,264,128]{2,1,0:T(8,128)(2,1)}), f16[8,264,128]{2,1,0:T(8,128)(2,1)S(1)}, u32[]{:S(2)}, u32[]{:S(2)}) async-start(f16[8,264,128]{2,1,0:T(8,128)(2,1)} %broadcast_in_dim.54), calls=%async_computation | async-start | bytes 1081344 | tf_op jit(solution)/shard_map/all_to_all | solution.py:302
  10.2 0.0 copy-done.4
  10.2 0.1 compare_convert_fusion
  10.3 0.0 copy-done
  10.3 0.3 fusion.leaf_forward_ref
  10.6 0.0 copy-start.3
  10.6 0.2 convolution_bitcast_fusion
  10.8 4.7 %collective-permute-start = (f32[256,128]{1,0:T(8,128)S(1)}, f32[256,128]{1,0:T(8,128)S(1)}, u32[]{:S(2)}, u32[]{:S(2)}) collective-permute-start(f32[256,128]{1,0:T(8,128)S(1)} %convolution_bitcast_fusion), channel_id=1, source_target_pairs={{8,0},{16,8},{24,16},{32,24},{40,32},{48,40},{56,48},{64,56},{72,6... | collective-permute-start | bytes 393224 | tf_op jit(solution)/shard_map/ppermute | solution.py:352
  15.5 0.2 convolution_bitcast_fusion.1.own_ref
  15.8 9.6 %all-to-all-done = f16[8,264,128]{2,1,0:T(8,128)(2,1)S(1)} async-done(((f16[8,264,128]{2,1,0:T(8,128)(2,1)}), f16[8,264,128]{2,1,0:T(8,128)(2,1)S(1)}, u32[]{:S(2)}, u32[]{:S(2)}) %all-to-all-start) | async-done | bytes 540704 | tf_op jit(solution)/shard_map/all_to_all | solution.py:302
  25.3 0.1 convert_element_type.53.wire_ref
  25.4 0.0 collective-permute-done.right_ref
  25.4 0.7 shard_map.123
  26.1 5.6 %collective-permute-start.1 = (f32[896,256]{1,0:T(8,128)S(1)}, f32[896,256]{1,0:T(8,128)S(1)}, u32[]{:S(2)}, u32[]{:S(2)}) collective-permute-start(f32[896,256]{1,0:T(8,128)S(1)} %get-tuple-element.16.mine_ref), channel_id=1, source_target_pairs={{0,8},{8,0},{1,9},{9,1},{2,10},{10,2},{3,11},{11,3},{4,12},{12,4},... | collective-permute-start | bytes 2752520 | tf_op jit(solution)/shard_map/ppermute | solution.py:306
  31.8 3.0 %collective-permute-start.2 = (f16[1032,128]{1,0:T(8,128)(2,1)S(1)}, f16[1032,128]{1,0:T(8,128)(2,1)S(1)}, u32[]{:S(2)}, u32[]{:S(2)}) collective-permute-start(f16[1032,128]{1,0:T(8,128)(2,1)S(1)} %convert_element_type.58), channel_id=1, source_target_pairs={{8,16},{24,32},{40,48},{56,64},{72,80},{88,96},{104,112},{120,128}... | collective-permute-start | bytes 792584 | tf_op jit(solution)/shard_map/ppermute | solution.py:367
  34.8 0.1 pad_add_fusion.place_ref
  34.9 0.0 collective-permute-done.1.other_ref
  34.9 1.6 %shard_map.124 = f32[1032,128]{1,0:T(8,128)S(1)} custom-call(s32[3]{0:T(128)S(1)} %pad_add_fusion.place_ref, f32[896,256]{1,0:T(8,128)S(1)} %get-tuple-element.16.mine_ref, f32[896,256]{1,0:T(8,128)S(1)} %collective-permute-done.1.other_ref), custom_call_target="tpu_custom_call" | custom-call | bytes 2363404 | tf_op jit(solution)/shard_map/pallas_call | solution.py:43
  36.5 1.6 %collective-permute-done.2 = f16[1032,128]{1,0:T(8,128)(2,1)S(1)} collective-permute-done((f16[1032,128]{1,0:T(8,128)(2,1)S(1)}, f16[1032,128]{1,0:T(8,128)(2,1)S(1)}, u32[]{:S(2)}, u32[]{:S(2)}) %collective-permute-start.2) | collective-permute-done | bytes 264224 | tf_op jit(solution)/shard_map/ppermute | solution.py:367
  38.1 0.1 broadcast_in_dim.55
  38.2 18.4 %all_to_all.20 = f16[4,1032,128]{2,1,0:T(8,128)(2,1)S(1)} all-to-all(f16[4,1032,128]{2,1,0:T(8,128)(2,1)S(1)} %broadcast_in_dim.55), channel_id=1, replica_groups=mesh['z'=8,'x'=4,'c'=2,'y'=8] {'x'}, dimensions={0} | all-to-all | bytes 2113536 | tf_op jit(solution)/shard_map/all_to_all | solution.py:302
  56.7 4.0 %collective-permute-start.3 = (f16[4,1032,128]{2,1,0:T(8,128)(2,1)S(1)}, f16[4,1032,128]{2,1,0:T(8,128)(2,1)S(1)}, u32[]{:S(2)}, u32[]{:S(2)}) collective-permute-start(f16[4,1032,128]{2,1,0:T(8,128)(2,1)S(1)} %all_to_all.20), channel_id=1, source_target_pairs={{0,8},{8,0},{1,9},{9,1},{2,10},{10,2},{3,11},{11,3},{4,12},{12,4},... | collective-permute-start | bytes 3170312 | tf_op jit(solution)/shard_map/ppermute | solution.py:306
  60.7 0.1 convert_element_type.59.first_ref.mine_ref.pair_mine.pair_first
  60.8 2.1 %collective-permute-done.3 = f16[4,1032,128]{2,1,0:T(8,128)(2,1)S(1)} collective-permute-done((f16[4,1032,128]{2,1,0:T(8,128)(2,1)S(1)}, f16[4,1032,128]{2,1,0:T(8,128)(2,1)S(1)}, u32[]{:S(2)}, u32[]{:S(2)}) %collective-permute-start.3) | collective-permute-done | bytes 1056800 | tf_op jit(solution)/shard_map/ppermute | solution.py:306
  62.9 0.1 convert_element_type.60.second_ref.other_ref.pair_other.pair_second
  63.1 1.5 %shard_map.125 = f32[2,392,128]{2,1,0:T(8,128)S(1)} custom-call(s32[3]{0:T(128)S(1)} %pad_add_fusion.place_ref, f32[4,1032,128]{2,1,0:T(8,128)S(1)} %convert_element_type.59.first_ref.mine_ref.pair_mine.pair_first, f32[4,1032,128]{2,1,0:T(8,128)S(1)} %convert_element_type.60.second_ref.other_ref.pair_other.pair_second), custom_call_target="tpu_custom_call" | custom-call | bytes 4628492 | tf_op jit(solution)/shard_map/pallas_call | solution.py:43
  64.6 0.2 broadcast_select_fusion
  64.9 32.1 %all_to_all.21 = f16[8,392,128]{2,1,0:T(8,128)(2,1)S(1)} all-to-all(f16[8,392,128]{2,1,0:T(8,128)(2,1)S(1)} %broadcast_select_fusion), channel_id=1, replica_groups=mesh['z'=8,'x'=4,'c'=2,'y'=8] {'z'}, dimensions={0} | all-to-all | bytes 1605632 | tf_op jit(solution)/shard_map/all_to_all | solution.py:379
  96.9 3.3 %collective-permute-start.4 = (f16[8,392,128]{2,1,0:T(8,128)(2,1)S(1)}, f16[8,392,128]{2,1,0:T(8,128)(2,1)S(1)}, u32[]{:S(2)}, u32[]{:S(2)}) collective-permute-start(f16[8,392,128]{2,1,0:T(8,128)(2,1)S(1)} %all_to_all.21), channel_id=1, source_target_pairs={{0,8},{8,0},{1,9},{9,1},{2,10},{10,2},{3,11},{11,3},{4,12},{12,4},... | collective-permute-start | bytes 2408456 | tf_op jit(solution)/shard_map/ppermute | solution.py:306
  100.2 3.0 %shard_map.126 = (f32[256,256]{1,0:T(8,128)S(1)}, f32[128,256]{1,0:T(8,128)S(1)}) custom-call(s32[3]{0:T(128)S(1)} %pad_add_fusion.place_ref, f32[4,1032,128]{2,1,0:T(8,128)S(1)} %convert_element_type.59.first_ref.mine_ref.pair_mine.pair_first, f32[4,1032,128]{2,1,0:T(8,128)S(1)} %convert_element_type.60.second_ref.other_ref.pair_other.pair_second), custom_call_target="tpu_custom_call" | custom-call | bytes 4620300 | tf_op jit(solution)/shard_map/pallas_call | solution.py:43
  103.2 0.1 convert_element_type.62.plane_mine.plane_first
  103.3 0.0 collective-permute-done.4
  103.3 0.1 convert_element_type.63.plane_other.plane_second
  103.4 2.2 %shard_map.127 = (f32[136,128]{1,0:T(8,128)S(1)}, f32[128,256]{1,0:T(8,128)S(1)}) custom-call(s32[3]{0:T(128)S(1)} %pad_add_fusion.place_ref, f32[8,392,128]{2,1,0:T(8,128)S(1)} %convert_element_type.62.plane_mine.plane_first, f32[8,392,128]{2,1,0:T(8,128)S(1)} %convert_element_type.63.plane_other.plane_second, f32[256,256]{1,0:T(8,128)S(1)} %get-tuple-element.19.factor_ref, ...), custom_call_target="tpu_custom_call" | custom-call | bytes 3805196 | tf_op jit(solution)/shard_map/pallas_call | solution.py:43
  105.7 15.0 %all_to_all.22 = f16[8,136,128]{2,1,0:T(8,128)(2,1)S(1)} all-to-all(f16[8,136,128]{2,1,0:T(8,128)(2,1)S(1)} %broadcast_in_dim.60), channel_id=1, replica_groups=mesh['z'=8,'x'=4,'c'=2,'y'=8] {'z'}, dimensions={0} | all-to-all | bytes 557056 | tf_op jit(solution)/shard_map/all_to_all | solution.py:302
  120.7 2.5 %collective-permute-start.5 = (f16[8,136,128]{2,1,0:T(8,128)(2,1)S(1)}, f16[8,136,128]{2,1,0:T(8,128)(2,1)S(1)}, u32[]{:S(2)}, u32[]{:S(2)}) collective-permute-start(f16[8,136,128]{2,1,0:T(8,128)(2,1)S(1)} %all_to_all.22), channel_id=1, source_target_pairs={{0,8},{8,0},{1,9},{9,1},{2,10},{10,2},{3,11},{11,3},{4,12},{12,4},... | collective-permute-start | bytes 835592 | tf_op jit(solution)/shard_map/ppermute | solution.py:306
  123.2 1.9 %shard_map.128 = (f32[4,128,256]{2,1,0:T(8,128)S(1)}, f32[128,256]{1,0:T(8,128)S(1)}, f32[128,256]{1,0:T(8,128)S(1)}, f32[128,256]{1,0:T(8,128)S(1)}) custom-call(s32[3]{0:T(128)S(1)} %pad_add_fusion.place_ref, f32[128,256]{1,0:T(8,128)S(1)} %get-tuple-element.22.ahead_ref, f32[4,1032,128]{2,1,0:T(8,128)S(1)} %convert_element_type.59.first_ref.mine_ref.pair_mine.pair_first, ...), custom_call_target="tpu_custom_call" | custom-call | bytes 7639052 | tf_op jit(solution)/shard_map/pallas_call | solution.py:43
  125.1 0.0 copy-start.1
  125.1 0.0 copy-start.2
  125.2 0.0 collective-permute-done.5
  125.2 0.9 copy-done.1
  126.2 0.1 copy-done.2
  126.2 4.6 %shard_map.129 = (f32[2,256,128]{2,1,0:T(8,128)}, f32[256,128]{1,0:T(8,128)}) custom-call(s32[3]{0:T(128)S(1)} %pad_add_fusion.place_ref, s32[2]{0:T(128)S(1)} %copy-done.4, f32[8,136,128]{2,1,0:T(8,128)S(1)} %convert_element_type.65.value_first, f32[8,136,128]{2,1,0:T(8,128)S(1)} %convert_element_type.66.value_second, ...), custom_call_target="tpu_custom_call" | custom-call | bytes 13275156 | tf_op jit(solution)/shard_map/pallas_call | solution.py:43
  (16 shorter events, 0.4 us)
Async XLA Ops:
  0.6 9.6 %copy-start = (bf16[2,256,256]{2,1,0:T(8,128)(2,1)S(1)}, bf16[2,256,256]{2,1,0:T(8,128)(2,1)}, u32[]{:S(2)}) copy-start(bf16[2,256,256]{2,1,0:T(8,128)(2,1)} %param.14) | copy-start | bytes 786436
  0.6 9.5 %copy-start.4 = (s32[2]{0:T(128)S(1)}, s32[2]{0:T(128)}, u32[]{:S(2)}) copy-start(s32[2]{0:T(128)} %size_ref.1) | copy-start | bytes 28
  0.7 9.6 %copy-start.6 = (f32[2,256,128]{2,1,0:T(8,128)S(1)}, f32[2,256,128]{2,1,0:T(8,128)}, u32[]{:S(2)}) copy-start(f32[2,256,128]{2,1,0:T(8,128)} %param.11) | copy-start | bytes 786436
  0.7 9.9 %copy-start.5 = (bf16[2,2,256,256]{3,2,1,0:T(8,128)(2,1)S(1)}, bf16[2,2,256,256]{3,2,1,0:T(8,128)(2,1)}, u32[]{:S(2)}) copy-start(bf16[2,2,256,256]{3,2,1,0:T(8,128)(2,1)} %param.15) | copy-start | bytes 1572868
  2.5 22.8 %all-to-all-start = ((f16[8,264,128]{2,1,0:T(8,128)(2,1)}), f16[8,264,128]{2,1,0:T(8,128)(2,1)S(1)}, u32[]{:S(2)}, u32[]{:S(2)}) async-start(f16[8,264,128]{2,1,0:T(8,128)(2,1)} %broadcast_in_dim.54), calls=%async_computation | async-start | bytes 1081344 | tf_op jit(solution)/shard_map/all_to_all | solution.py:302
  10.6 14.8 %copy-start.3 = (f32[1,256,128]{2,1,0:T(8,128)S(1)}, f32[1,256,128]{2,1,0:T(8,128)}, u32[]{:S(2)}) copy-start(f32[1,256,128]{2,1,0:T(8,128)} %param.12) | copy-start | bytes 393220
  10.8 14.6 %collective-permute-start = (f32[256,128]{1,0:T(8,128)S(1)}, f32[256,128]{1,0:T(8,128)S(1)}, u32[]{:S(2)}, u32[]{:S(2)}) collective-permute-start(f32[256,128]{1,0:T(8,128)S(1)} %convolution_bitcast_fusion), channel_id=1, source_target_pairs={{8,0},{16,8},{24,16},{32,24},{40,32},{48,40},{56,48},{64,56},{72,6... | collective-permute-start | bytes 393224 | tf_op jit(solution)/shard_map/ppermute | solution.py:352
  26.1 8.7 %collective-permute-start.1 = (f32[896,256]{1,0:T(8,128)S(1)}, f32[896,256]{1,0:T(8,128)S(1)}, u32[]{:S(2)}, u32[]{:S(2)}) collective-permute-start(f32[896,256]{1,0:T(8,128)S(1)} %get-tuple-element.16.mine_ref), channel_id=1, source_target_pairs={{0,8},{8,0},{1,9},{9,1},{2,10},{10,2},{3,11},{11,3},{4,12},{12,4},... | collective-permute-start | bytes 2752520 | tf_op jit(solution)/shard_map/ppermute | solution.py:306
  31.8 6.3 %collective-permute-start.2 = (f16[1032,128]{1,0:T(8,128)(2,1)S(1)}, f16[1032,128]{1,0:T(8,128)(2,1)S(1)}, u32[]{:S(2)}, u32[]{:S(2)}) collective-permute-start(f16[1032,128]{1,0:T(8,128)(2,1)S(1)} %convert_element_type.58), channel_id=1, source_target_pairs={{8,16},{24,32},{40,48},{56,64},{72,80},{88,96},{104,112},{120,128}... | collective-permute-start | bytes 792584 | tf_op jit(solution)/shard_map/ppermute | solution.py:367
  56.7 6.2 %collective-permute-start.3 = (f16[4,1032,128]{2,1,0:T(8,128)(2,1)S(1)}, f16[4,1032,128]{2,1,0:T(8,128)(2,1)S(1)}, u32[]{:S(2)}, u32[]{:S(2)}) collective-permute-start(f16[4,1032,128]{2,1,0:T(8,128)(2,1)S(1)} %all_to_all.20), channel_id=1, source_target_pairs={{0,8},{8,0},{1,9},{9,1},{2,10},{10,2},{3,11},{11,3},{4,12},{12,4},... | collective-permute-start | bytes 3170312 | tf_op jit(solution)/shard_map/ppermute | solution.py:306
  96.9 6.4 %collective-permute-start.4 = (f16[8,392,128]{2,1,0:T(8,128)(2,1)S(1)}, f16[8,392,128]{2,1,0:T(8,128)(2,1)S(1)}, u32[]{:S(2)}, u32[]{:S(2)}) collective-permute-start(f16[8,392,128]{2,1,0:T(8,128)(2,1)S(1)} %all_to_all.21), channel_id=1, source_target_pairs={{0,8},{8,0},{1,9},{9,1},{2,10},{10,2},{3,11},{11,3},{4,12},{12,4},... | collective-permute-start | bytes 2408456 | tf_op jit(solution)/shard_map/ppermute | solution.py:306
  120.7 4.5 %collective-permute-start.5 = (f16[8,136,128]{2,1,0:T(8,128)(2,1)S(1)}, f16[8,136,128]{2,1,0:T(8,128)(2,1)S(1)}, u32[]{:S(2)}, u32[]{:S(2)}) collective-permute-start(f16[8,136,128]{2,1,0:T(8,128)(2,1)S(1)} %all_to_all.22), channel_id=1, source_target_pairs={{0,8},{8,0},{1,9},{9,1},{2,10},{10,2},{3,11},{11,3},{4,12},{12,4},... | collective-permute-start | bytes 835592 | tf_op jit(solution)/shard_map/ppermute | solution.py:306
  125.1 1.0 copy-start.1
  125.1 1.1 copy-start.2

commit v4 on v3

--- a/solution.py
+++ b/solution.py
@@ -37,7 +37,7 @@
     return jnp.where(flags != 0, one, other)
 
 
-def kernel(body, out_shapes, *operands, flops=0):
+def kernel(body, out_shapes, *operands, left_in_hbm=(), scratch=(), flops=0):
     moved = sum(o.size * o.dtype.itemsize for o in operands)
     moved += sum(o.size * o.dtype.itemsize for o in out_shapes)
     return pl.pallas_call(
@@ -46,11 +46,13 @@
         in_specs=[
             pl.BlockSpec(memory_space=pltpu.SMEM if o.dtype == jnp.int32 else pltpu.VMEM)
             for o in operands
-        ],
+        ]
+        + [pl.BlockSpec(memory_space=pltpu.HBM) for _ in left_in_hbm],
         out_specs=[pl.BlockSpec(memory_space=pltpu.VMEM) for _ in out_shapes],
+        scratch_shapes=scratch,
         compiler_params=pltpu.CompilerParams(vmem_limit_bytes=16 * 2**20),
         cost_estimate=pl.CostEstimate(flops=flops, bytes_accessed=moved, transcendentals=0),
-    )(*operands)
+    )(*operands, *left_in_hbm)
 
 
 def shape(*dims, dtype=F32):
@@ -195,7 +197,8 @@
     encode(wire_ref, (1,), jnp.concatenate([behind, further], axis=1))
 
 
-def through_kernel(place_ref, mine_ref, other_ref, factor_ref, value_ref):
+def through_kernel(place_ref, mine_ref, other_ref, factor_ref, value_ref, start_ref, own_ref):
+    x = place_ref[1]
     pairs = Wires(place_ref[0], mine_ref, other_ref)
     width = pairs.width
     forward, backward, through, value, back_value = pair_columns(width)
@@ -205,15 +208,23 @@
 
     ahead = jnp.concatenate([pairs.matrix(0, forward), pairs.values(0, value)], axis=0)
     own = [jnp.concatenate([pairs.matrix(0, through), pairs.values(0, back_value)], axis=0)]
+    start = ahead
     for i in range(1, pairs.count):
+        start = choose(x == i, ahead, start)
         further = product(ahead, pairs.matrix(i, through))
         own.append(add_value(further, pairs.values(i, back_value)))
         if i < pairs.count - 1:
             further = product(ahead, pairs.matrix(i, forward))
             ahead = add_value(further, pairs.values(i, value))
+    start_ref[...] = start
+    for i in range(pairs.count):
+        own_ref[i] = own[i]
     behind = own[-1]
     for i in range(pairs.count - 2, -1, -1):
-        behind = own[i] + product(behind, pairs.matrix(i, backward))
+        factor, offset = pairs.matrix(i, backward), own[i]
+        if i == 0:
+            factor, offset = half_columns(pairs.core, factor), half_columns(pairs.core, offset)
+        behind = offset + product(behind, factor)
     factor_ref[...] = behind[:width]
     value_ref[...] = behind[width:]
 
@@ -226,28 +237,27 @@
     width = planes.width
     received = jnp.zeros(ahead_ref.shape, F32)
     for i in range(planes.count - 1):
-        offset = planes.values(i, slice(width, width + planes.part))
-        received = choose(z > i, offset + product(received, planes.matrix(i)), received)
+        further = planes.values(i, slice(width, width + planes.part))
+        if i > 0:
+            further = further + product(received, planes.matrix(i))
+        received = choose(z > i, further, received)
     ahead_ref[...] = received
     behind = value_ref[...] + product(received, factor_ref[...])
-    encode(wire_ref, (), half_columns(core, behind))
+    wire_ref[...] = behind.astype(BF16)
 
 
 def values_kernel(
-    place_ref, ahead_ref, pair_mine, pair_other, mine_ref, other_ref, previous_ref,
+    place_ref, ahead_ref, start_factor_ref, own_ref, mine_ref, other_ref, previous_ref,
     through_ref, first_ref, second_ref, before_ref,
 ):
     core, x = place_ref[0], place_ref[1]
-    pairs = Wires(core, pair_mine, pair_other)
-    width = pairs.width
-    forward, _, through, value, back_value = pair_columns(width)
+    width = mine_ref.shape[1]
     ahead = ahead_ref[...]
-    start = ahead
+    start = start_factor_ref[width:] + product(ahead, start_factor_ref[:width])
+    start = choose(x == 0, ahead, start)
     through_ref[0] = jnp.zeros(ahead.shape, F32)
-    for i in range(1, pairs.count):
-        ahead = pairs.values(i - 1, value) + product(ahead, pairs.matrix(i - 1, forward))
-        start = choose(x == i, ahead, start)
-        through_ref[i] = pairs.values(i, back_value) + product(ahead, pairs.matrix(i, through))
+    for i in range(1, own_ref.shape[0]):
+        through_ref[i] = own_ref[i, width:] + product(ahead, own_ref[i, :width])
     both = functools.partial(both_cores, core, mine_ref, other_ref)
     factor_first, factor_second = both(0, width)
     inverse_first, inverse_second = both(2 * width, 3 * width)
@@ -263,16 +273,26 @@
 def backward_kernel(
     place_ref, size_ref, value_first, value_second, plane_first, plane_second,
     pair_first, pair_second, through_ref, mine_ref, other_ref, first_ref, second_ref, before_ref,
-    previous_ref, leaf_forward_ref, leaf_upper_ref, leaf_upper_inv_ref, leaf_ref, sep_ref,
+    previous_ref, leaf_forward_ref, far_upper_ref, far_upper_inv_ref, leaf_ref, sep_ref,
+    leaf_upper_ref, leaf_upper_inv_ref, arrived,
 ):
+    copies = [
+        pltpu.make_async_copy(far_upper_ref, leaf_upper_ref, arrived.at[0]),
+        pltpu.make_async_copy(far_upper_inv_ref, leaf_upper_inv_ref, arrived.at[1]),
+    ]
+    for copy in copies:
+        copy.start()
     core, x, z = place_ref[0], place_ref[1], place_ref[2]
     planes, pairs = Wires(core, plane_first, plane_second), Wires(core, pair_first, pair_second)
-    values = Wires(core, value_first, value_second)
     width = pairs.width
     backward = pair_columns(width)[1]
     received = jnp.zeros(first_ref.shape, F32)
     for i in range(planes.count - 1, 0, -1):
-        further = values.values(i, slice(0, values.part)) + product(received, planes.matrix(i))
+        mine, other = value_first[i].astype(F32), value_second[i].astype(F32)
+        offset = [choose(core == 0, mine, other), choose(core == 0, other, mine)]
+        further = jnp.concatenate(offset, axis=1)
+        if i < planes.count - 1:
+            further = further + product(received, planes.matrix(i))
         received = choose(z < i, further, received)
     chip = received
     for i in range(pairs.count - 1, 0, -1):
@@ -289,6 +309,8 @@
     sep = sep.astype(BF16)
     dot = functools.partial(jnp.dot, preferred_element_type=F32)
     rows = lax.broadcasted_iota(jnp.int32, sep.shape, 0)
+    for copy in copies:
+        copy.wait()
     for leaf in range(leaf_ref.shape[0]):
         back = leaf_forward_ref[leaf] - dot(leaf_upper_ref[leaf, 0], before)
         back = back - dot(leaf_upper_ref[leaf, 1], sep)
@@ -296,9 +318,9 @@
         leaf_ref[leaf] = jnp.where(rows < size_ref[leaf], result, 0.0)
 
 
-def to_all(block, axis):
+def to_all(block, axis, dtype=F16):
     size = lax.axis_size(axis)
-    slots = jnp.broadcast_to(block.astype(F16)[None], (size,) + block.shape)
+    slots = jnp.broadcast_to(block.astype(dtype)[None], (size,) + block.shape)
     return lax.all_to_all(slots, axis, 0, 0, tiled=True)
 
 
@@ -378,19 +400,29 @@
     slots = jnp.where(index > z, wire[0][None], wire[1][None])
     between = in_order(core, lax.all_to_all(slots, Z, 0, 0, tiled=True))
     block = shape(samples, width)
-    through = kernel(
-        through_kernel, [shape(width, width), shape(samples, width)], place, *pairs
+    *through, start, own = kernel(
+        through_kernel,
+        [
+            shape(width, part),
+            shape(samples, part),
+            shape(width + samples, width),
+            shape(chips, width + samples, width),
+        ],
+        place,
+        *pairs,
     )
     wire, ahead = kernel(
-        forward_kernel, [wire_shape(part, part), block], place, *between, *through
-    )
-    values = in_order(core, to_all(wire, Z))
+        forward_kernel, [shape(samples, part, dtype=BF16), block], place, *between, *through
+    )
+    values = to_all(wire, Z, BF16)
+    values = values, swap_cores(values)
     through, first, second, before = kernel(
         values_kernel,
         [shape(chips, samples, width), block, block, block],
         place,
         ahead,
-        *pairs,
+        start,
+        own,
         mine,
         other,
         previous,
@@ -412,8 +444,12 @@
         before,
         previous,
         leaf_forward,
-        leaf_upper,
-        leaf_upper_inv,
+        left_in_hbm=[leaf_upper, leaf_upper_inv],
+        scratch=[
+            pltpu.VMEM(leaf_upper.shape, BF16),
+            pltpu.VMEM(leaf_upper_inv.shape, BF16),
+            pltpu.SemaphoreType.DMA((2,)),
+        ],
     )
     return (leaf_correction, sep_correction[None])
 

time: 131 us -> 129 us (0.985)
  no operation moved by 1% of the time
where the time goes in v4:
time: 129 us; the launch traced here: 128 us
  blocking collectives  65.3 us (51%)
  starting transfers between devices  30.5 us (24%)
  Pallas kernels  14.5 us (11%)
  waiting for transfers between devices  13.3 us (10%)
  other arithmetic  2.02 us (2%)
    all_to_all x2, blocking collectives, to_all(): return lax.all_to_all(slots, axis, 0, 0, tiled=True)  33.2 us
    all_to_all x1, blocking collectives, per_device(): between = in_order(core, lax.all_to_all(slots, Z, 0, 0, tiled=True))  32.1 us
    ppermute x4, starting transfers between devices, swap_cores(): return lax.ppermute(block, C, [(0, 1), (1, 0)])  15.1 us
    pallas_call x8, Pallas kernels, kernel(): pl.pallas_call(body, out_shape=out_shapes, in_specs=[pl.BlockSpec(memory_...  14.5 us
    all_to_all x1, waiting for transfers between devices, to_all(): return lax.all_to_all(slots, axis, 0, 0, tiled=True)  9.57 us
    all_to_all x1, starting transfers between devices, to_all(): return lax.all_to_all(slots, axis, 0, 0, tiled=True)  7.65 us
    ppermute x1, starting transfers between devices, per_device(): lax.ppermute(left_terms, panel, [(i + 1, i) for i in range(panels - 1)])  4.68 us
    ppermute x1, starting transfers between devices, per_device(): previous = lax.ppermute(previous.astype(F16), panel, to_next_chip)  3.03 us
  transfers between devices with their start and end apart: 7, of which 3 were waited for; matrix products, arithmetic and copies ran while one was open for 1% of the time, Pallas kernels for 5%

profile of v4, /device:TPU:1, one launch (start us, length us, event | category | flops | bytes accessed | tf_op | source)
XLA Modules:
  0.0 128.4 jit_solution(507242662233517956)
XLA Ops:
  0.6 0.0 copy-start
  0.6 0.0 copy-start.4
  0.7 0.0 copy-start.6
  0.7 0.0 copy-start.5
  0.7 0.9 pad_maximum_fusion.blocks_ref
  1.6 0.9 broadcast_in_dim.54
  2.5 7.7 %all-to-all-start = ((f16[8,264,128]{2,1,0:T(8,128)(2,1)}), f16[8,264,128]{2,1,0:T(8,128)(2,1)S(1)}, u32[]{:S(2)}, u32[]{:S(2)}) async-start(f16[8,264,128]{2,1,0:T(8,128)(2,1)} %broadcast_in_dim.54), calls=%async_computation | async-start | bytes 1081344 | tf_op jit(solution)/shard_map/all_to_all | solution.py:324
  10.2 0.0 copy-done.4
  10.2 0.1 compare_convert_fusion
  10.3 0.0 copy-done
  10.3 0.0 copy-done.6
  10.3 0.3 fusion.leaf_forward_ref
  10.6 0.0 copy-start.3
  10.6 0.2 convolution_bitcast_fusion
  10.8 4.7 %collective-permute-start = (f32[256,128]{1,0:T(8,128)S(1)}, f32[256,128]{1,0:T(8,128)S(1)}, u32[]{:S(2)}, u32[]{:S(2)}) collective-permute-start(f32[256,128]{1,0:T(8,128)S(1)} %convolution_bitcast_fusion), channel_id=1, source_target_pairs={{8,0},{16,8},{24,16},{32,24},{40,32},{48,40},{56,48},{64,56},{72,6... | collective-permute-start | bytes 393224 | tf_op jit(solution)/shard_map/ppermute | solution.py:374
  15.5 0.2 convolution_bitcast_fusion.1.own_ref
  15.8 9.6 %all-to-all-done = f16[8,264,128]{2,1,0:T(8,128)(2,1)S(1)} async-done(((f16[8,264,128]{2,1,0:T(8,128)(2,1)}), f16[8,264,128]{2,1,0:T(8,128)(2,1)S(1)}, u32[]{:S(2)}, u32[]{:S(2)}) %all-to-all-start) | async-done | bytes 540704 | tf_op jit(solution)/shard_map/all_to_all | solution.py:324
  25.3 0.1 convert_element_type.44.wire_ref
  25.4 0.0 collective-permute-done.right_ref
  25.4 0.7 shard_map.123
  26.1 5.6 %collective-permute-start.1 = (f32[896,256]{1,0:T(8,128)S(1)}, f32[896,256]{1,0:T(8,128)S(1)}, u32[]{:S(2)}, u32[]{:S(2)}) collective-permute-start(f32[896,256]{1,0:T(8,128)S(1)} %get-tuple-element.18.mine_ref), channel_id=1, source_target_pairs={{0,8},{8,0},{1,9},{9,1},{2,10},{10,2},{3,11},{11,3},{4,12},{12,4},... | collective-permute-start | bytes 2752520 | tf_op jit(solution)/shard_map/ppermute | solution.py:328
  31.8 3.0 %collective-permute-start.2 = (f16[1032,128]{1,0:T(8,128)(2,1)S(1)}, f16[1032,128]{1,0:T(8,128)(2,1)S(1)}, u32[]{:S(2)}, u32[]{:S(2)}) collective-permute-start(f16[1032,128]{1,0:T(8,128)(2,1)S(1)} %convert_element_type.49), channel_id=1, source_target_pairs={{8,16},{24,32},{40,48},{56,64},{72,80},{88,96},{104,112},{120,128}... | collective-permute-start | bytes 792584 | tf_op jit(solution)/shard_map/ppermute | solution.py:389
  34.8 0.1 pad_add_fusion.place_ref
  34.9 0.0 collective-permute-done.1.other_ref
  34.9 1.6 %shard_map.124 = f32[1032,128]{1,0:T(8,128)S(1)} custom-call(s32[3]{0:T(128)S(1)} %pad_add_fusion.place_ref, f32[896,256]{1,0:T(8,128)S(1)} %get-tuple-element.18.mine_ref, f32[896,256]{1,0:T(8,128)S(1)} %collective-permute-done.1.other_ref), custom_call_target="tpu_custom_call" | custom-call | bytes 2363404 | tf_op jit(solution)/shard_map/pallas_call | solution.py:43
  36.5 1.6 %collective-permute-done.2 = f16[1032,128]{1,0:T(8,128)(2,1)S(1)} collective-permute-done((f16[1032,128]{1,0:T(8,128)(2,1)S(1)}, f16[1032,128]{1,0:T(8,128)(2,1)S(1)}, u32[]{:S(2)}, u32[]{:S(2)}) %collective-permute-start.2) | collective-permute-done | bytes 264224 | tf_op jit(solution)/shard_map/ppermute | solution.py:389
  38.1 0.1 broadcast_in_dim.55
  38.2 18.4 %all_to_all.20 = f16[4,1032,128]{2,1,0:T(8,128)(2,1)S(1)} all-to-all(f16[4,1032,128]{2,1,0:T(8,128)(2,1)S(1)} %broadcast_in_dim.55), channel_id=1, replica_groups=mesh['z'=8,'x'=4,'c'=2,'y'=8] {'x'}, dimensions={0} | all-to-all | bytes 2113536 | tf_op jit(solution)/shard_map/all_to_all | solution.py:324
  56.7 4.0 %collective-permute-start.3 = (f16[4,1032,128]{2,1,0:T(8,128)(2,1)S(1)}, f16[4,1032,128]{2,1,0:T(8,128)(2,1)S(1)}, u32[]{:S(2)}, u32[]{:S(2)}) collective-permute-start(f16[4,1032,128]{2,1,0:T(8,128)(2,1)S(1)} %all_to_all.20), channel_id=1, source_target_pairs={{0,8},{8,0},{1,9},{9,1},{2,10},{10,2},{3,11},{11,3},{4,12},{12,4},... | collective-permute-start | bytes 3170312 | tf_op jit(solution)/shard_map/ppermute | solution.py:328
  60.7 0.1 convert_element_type.50.first_ref.mine_ref.pair_first
  60.8 2.1 %collective-permute-done.3 = f16[4,1032,128]{2,1,0:T(8,128)(2,1)S(1)} collective-permute-done((f16[4,1032,128]{2,1,0:T(8,128)(2,1)S(1)}, f16[4,1032,128]{2,1,0:T(8,128)(2,1)S(1)}, u32[]{:S(2)}, u32[]{:S(2)}) %collective-permute-start.3) | collective-permute-done | bytes 1056800 | tf_op jit(solution)/shard_map/ppermute | solution.py:328
  62.9 0.1 convert_element_type.51.second_ref.other_ref.pair_second
  63.1 1.5 %shard_map.125 = f32[2,392,128]{2,1,0:T(8,128)S(1)} custom-call(s32[3]{0:T(128)S(1)} %pad_add_fusion.place_ref, f32[4,1032,128]{2,1,0:T(8,128)S(1)} %convert_element_type.50.first_ref.mine_ref.pair_first, f32[4,1032,128]{2,1,0:T(8,128)S(1)} %convert_element_type.51.second_ref.other_ref.pair_second), custom_call_target="tpu_custom_call" | custom-call | bytes 4628492 | tf_op jit(solution)/shard_map/pallas_call | solution.py:43
  64.6 0.2 broadcast_select_fusion
  64.9 32.1 %all_to_all.21 = f16[8,392,128]{2,1,0:T(8,128)(2,1)S(1)} all-to-all(f16[8,392,128]{2,1,0:T(8,128)(2,1)S(1)} %broadcast_select_fusion), channel_id=1, replica_groups=mesh['z'=8,'x'=4,'c'=2,'y'=8] {'z'}, dimensions={0} | all-to-all | bytes 1605632 | tf_op jit(solution)/shard_map/all_to_all | solution.py:401
  96.9 3.3 %collective-permute-start.4 = (f16[8,392,128]{2,1,0:T(8,128)(2,1)S(1)}, f16[8,392,128]{2,1,0:T(8,128)(2,1)S(1)}, u32[]{:S(2)}, u32[]{:S(2)}) collective-permute-start(f16[8,392,128]{2,1,0:T(8,128)(2,1)S(1)} %all_to_all.21), channel_id=1, source_target_pairs={{0,8},{8,0},{1,9},{9,1},{2,10},{10,2},{3,11},{11,3},{4,12},{12,4},... | collective-permute-start | bytes 2408456 | tf_op jit(solution)/shard_map/ppermute | solution.py:328
  100.2 2.8 %shard_map.126 = (f32[256,128]{1,0:T(8,128)S(1)}, f32[128,128]{1,0:T(8,128)S(1)}, f32[384,256]{1,0:T(8,128)S(1)}, f32[4,384,256]{2,1,0:T(8,128)S(1)}) custom-call(s32[3]{0:T(128)S(1)} %pad_add_fusion.place_ref, f32[4,1032,128]{2,1,0:T(8,128)S(1)} %convert_element_type.50.first_ref.mine_ref.pair_first, ...), custom_call_target="tpu_custom_call" | custom-call | bytes 6389772 | tf_op jit(solution)/shard_map/pallas_call | solution.py:43
  103.0 0.1 convert_element_type.53.plane_mine.plane_first
  103.1 0.0 collective-permute-done.4
  103.1 0.1 convert_element_type.54.plane_other.plane_second
  103.2 2.0 %shard_map.127 = (bf16[128,128]{1,0:T(8,128)(2,1)S(1)}, f32[128,256]{1,0:T(8,128)S(1)}) custom-call(s32[3]{0:T(128)S(1)} %pad_add_fusion.place_ref, f32[8,392,128]{2,1,0:T(8,128)S(1)} %convert_element_type.53.plane_mine.plane_first, f32[8,392,128]{2,1,0:T(8,128)S(1)} %convert_element_type.54.plane_other.plane_second, ...), custom_call_target="tpu_custom_call" | custom-call | bytes 3571724 | tf_op jit(solution)/shard_map/pallas_call | solution.py:43
  105.3 14.8 %all_to_all.22.value_first = bf16[8,128,128]{2,1,0:T(8,128)(2,1)S(1)} all-to-all(bf16[8,128,128]{2,1,0:T(8,128)(2,1)S(1)} %broadcast_in_dim.60), channel_id=1, replica_groups=mesh['z'=8,'x'=4,'c'=2,'y'=8] {'z'}, dimensions={0} | all-to-all | bytes 524288 | tf_op jit(solution)/shard_map/all_to_all | solution.py:324
  120.0 2.3 %collective-permute-start.5 = (bf16[8,128,128]{2,1,0:T(8,128)(2,1)S(1)}, bf16[8,128,128]{2,1,0:T(8,128)(2,1)S(1)}, u32[]{:S(2)}, u32[]{:S(2)}) collective-permute-start(bf16[8,128,128]{2,1,0:T(8,128)(2,1)S(1)} %all_to_all.22.value_first), channel_id=1, source_target_pairs={{0,8},{8,0},{1,9},{9,1},{2,10},{10,2},{3,11},{11,3},{4,12},{12,4},... | collective-permute-start | bytes 786440 | tf_op jit(solution)/shard_map/ppermute | solution.py:328
  122.4 0.0 copy-start.1
  122.4 0.0 copy-start.2
  122.5 1.5 %shard_map.128 = (f32[4,128,256]{2,1,0:T(8,128)S(1)}, f32[128,256]{1,0:T(8,128)S(1)}, f32[128,256]{1,0:T(8,128)S(1)}, f32[128,256]{1,0:T(8,128)S(1)}) custom-call(s32[3]{0:T(128)S(1)} %pad_add_fusion.place_ref, f32[128,256]{1,0:T(8,128)S(1)} %get-tuple-element.24.ahead_ref, f32[384,256]{1,0:T(8,128)S(1)} %get-tuple-element.25.start_factor_ref, ...), custom_call_target="tpu_custom_call" | custom-call | bytes 5378060 | tf_op jit(solution)/shard_map/pallas_call | solution.py:43
  123.9 0.0 collective-permute-done.5.value_second
  124.0 4.5 %shard_map.129 = (f32[2,256,128]{2,1,0:T(8,128)}, f32[256,128]{1,0:T(8,128)}) custom-call(s32[3]{0:T(128)S(1)} %pad_add_fusion.place_ref, s32[2]{0:T(128)S(1)} %copy-done.4, bf16[8,128,128]{2,1,0:T(8,128)(2,1)S(1)} %all_to_all.22.value_first, bf16[8,128,128]{2,1,0:T(8,128)(2,1)S(1)} %collective-permute-done.5.value_second, ...), custom_call_target="tpu_custom_call" | custom-call | bytes 11898900 | tf_op jit(solution)/shard_map/pallas_call | solution.py:43
  (13 shorter events, 0.3 us)
Async XLA Ops:
  0.6 9.6 %copy-start = (bf16[2,256,256]{2,1,0:T(8,128)(2,1)S(1)}, bf16[2,256,256]{2,1,0:T(8,128)(2,1)}, u32[]{:S(2)}) copy-start(bf16[2,256,256]{2,1,0:T(8,128)(2,1)} %param.14) | copy-start | bytes 786436
  0.6 9.5 %copy-start.4 = (s32[2]{0:T(128)S(1)}, s32[2]{0:T(128)}, u32[]{:S(2)}) copy-start(s32[2]{0:T(128)} %size_ref.1) | copy-start | bytes 28
  0.7 9.6 %copy-start.6 = (f32[2,256,128]{2,1,0:T(8,128)S(1)}, f32[2,256,128]{2,1,0:T(8,128)}, u32[]{:S(2)}) copy-start(f32[2,256,128]{2,1,0:T(8,128)} %param.11) | copy-start | bytes 786436
  0.7 9.9 %copy-start.5 = (bf16[2,2,256,256]{3,2,1,0:T(8,128)(2,1)S(1)}, bf16[2,2,256,256]{3,2,1,0:T(8,128)(2,1)}, u32[]{:S(2)}) copy-start(bf16[2,2,256,256]{3,2,1,0:T(8,128)(2,1)} %param.15) | copy-start | bytes 1572868
  2.5 22.8 %all-to-all-start = ((f16[8,264,128]{2,1,0:T(8,128)(2,1)}), f16[8,264,128]{2,1,0:T(8,128)(2,1)S(1)}, u32[]{:S(2)}, u32[]{:S(2)}) async-start(f16[8,264,128]{2,1,0:T(8,128)(2,1)} %broadcast_in_dim.54), calls=%async_computation | async-start | bytes 1081344 | tf_op jit(solution)/shard_map/all_to_all | solution.py:324
  10.6 14.8 %copy-start.3 = (f32[1,256,128]{2,1,0:T(8,128)S(1)}, f32[1,256,128]{2,1,0:T(8,128)}, u32[]{:S(2)}) copy-start(f32[1,256,128]{2,1,0:T(8,128)} %param.12) | copy-start | bytes 393220
  10.8 14.6 %collective-permute-start = (f32[256,128]{1,0:T(8,128)S(1)}, f32[256,128]{1,0:T(8,128)S(1)}, u32[]{:S(2)}, u32[]{:S(2)}) collective-permute-start(f32[256,128]{1,0:T(8,128)S(1)} %convolution_bitcast_fusion), channel_id=1, source_target_pairs={{8,0},{16,8},{24,16},{32,24},{40,32},{48,40},{56,48},{64,56},{72,6... | collective-permute-start | bytes 393224 | tf_op jit(solution)/shard_map/ppermute | solution.py:374
  26.1 8.7 %collective-permute-start.1 = (f32[896,256]{1,0:T(8,128)S(1)}, f32[896,256]{1,0:T(8,128)S(1)}, u32[]{:S(2)}, u32[]{:S(2)}) collective-permute-start(f32[896,256]{1,0:T(8,128)S(1)} %get-tuple-element.18.mine_ref), channel_id=1, source_target_pairs={{0,8},{8,0},{1,9},{9,1},{2,10},{10,2},{3,11},{11,3},{4,12},{12,4},... | collective-permute-start | bytes 2752520 | tf_op jit(solution)/shard_map/ppermute | solution.py:328
  31.8 6.3 %collective-permute-start.2 = (f16[1032,128]{1,0:T(8,128)(2,1)S(1)}, f16[1032,128]{1,0:T(8,128)(2,1)S(1)}, u32[]{:S(2)}, u32[]{:S(2)}) collective-permute-start(f16[1032,128]{1,0:T(8,128)(2,1)S(1)} %convert_element_type.49), channel_id=1, source_target_pairs={{8,16},{24,32},{40,48},{56,64},{72,80},{88,96},{104,112},{120,128}... | collective-permute-start | bytes 792584 | tf_op jit(solution)/shard_map/ppermute | solution.py:389
  56.7 6.2 %collective-permute-start.3 = (f16[4,1032,128]{2,1,0:T(8,128)(2,1)S(1)}, f16[4,1032,128]{2,1,0:T(8,128)(2,1)S(1)}, u32[]{:S(2)}, u32[]{:S(2)}) collective-permute-start(f16[4,1032,128]{2,1,0:T(8,128)(2,1)S(1)} %all_to_all.20), channel_id=1, source_target_pairs={{0,8},{8,0},{1,9},{9,1},{2,10},{10,2},{3,11},{11,3},{4,12},{12,4},... | collective-permute-start | bytes 3170312 | tf_op jit(solution)/shard_map/ppermute | solution.py:328
  96.9 6.2 %collective-permute-start.4 = (f16[8,392,128]{2,1,0:T(8,128)(2,1)S(1)}, f16[8,392,128]{2,1,0:T(8,128)(2,1)S(1)}, u32[]{:S(2)}, u32[]{:S(2)}) collective-permute-start(f16[8,392,128]{2,1,0:T(8,128)(2,1)S(1)} %all_to_all.21), channel_id=1, source_target_pairs={{0,8},{8,0},{1,9},{9,1},{2,10},{10,2},{3,11},{11,3},{4,12},{12,4},... | collective-permute-start | bytes 2408456 | tf_op jit(solution)/shard_map/ppermute | solution.py:328
  120.0 3.9 %collective-permute-start.5 = (bf16[8,128,128]{2,1,0:T(8,128)(2,1)S(1)}, bf16[8,128,128]{2,1,0:T(8,128)(2,1)S(1)}, u32[]{:S(2)}, u32[]{:S(2)}) collective-permute-start(bf16[8,128,128]{2,1,0:T(8,128)(2,1)S(1)} %all_to_all.22.value_first), channel_id=1, source_target_pairs={{0,8},{8,0},{1,9},{9,1},{2,10},{10,2},{3,11},{11,3},{4,12},{12,4},... | collective-permute-start | bytes 786440 | tf_op jit(solution)/shard_map/ppermute | solution.py:328
  122.4 1.5 %copy-start.1 = (bf16[2,2,256,256]{3,2,1,0:T(8,128)(2,1)S(1)}, bf16[2,2,256,256]{3,2,1,0:T(8,128)(2,1)}, u32[]{:S(2)}) copy-start(bf16[2,2,256,256]{3,2,1,0:T(8,128)(2,1)} %far_upper_ref.1) | copy-start | bytes 1572868
  122.4 1.5 %copy-start.2 = (bf16[2,256,256]{2,1,0:T(8,128)(2,1)S(1)}, bf16[2,256,256]{2,1,0:T(8,128)(2,1)}, u32[]{:S(2)}) copy-start(bf16[2,256,256]{2,1,0:T(8,128)(2,1)} %far_upper_inv_ref.1) | copy-start | bytes 786436

commit v5 on v4

--- a/solution.py
+++ b/solution.py
@@ -390,12 +390,11 @@
     part = width // 2
     (wire,) = kernel(pair_kernel, [wire_shape(part, 4 * width)], place, mine, other)
 
+    pairs = in_order(core, to_all(wire, X))
+    (wire,) = kernel(plane_kernel, [wire_shape(2, part, width + part)], place, *pairs)
+
     wire, previous = lax.optimization_barrier((wire.astype(F16), previous))
-    pairs = in_order(core, to_all(wire, X))
     previous = previous.astype(F32)
-    (wire,) = kernel(plane_kernel, [wire_shape(2, part, width + part)], place, *pairs)
-
-    wire = wire.astype(F16)
     index = jnp.arange(planes, dtype=jnp.int32)[:, None, None]
     slots = jnp.where(index > z, wire[0][None], wire[1][None])
     between = in_order(core, lax.all_to_all(slots, Z, 0, 0, tiled=True))

time: 129 us -> 128 us (level)
  blocking collectives: 65.3 us -> 59.5 us
  starting transfers between devices: 30.5 us -> 35.7 us
    ppermute x4, starting transfers between devices: 15.1 us -> 21.2 us  [swap_cores(): return lax.ppermute(block, C, [(0, 1), (1, 0)])]
    all_to_all x1, blocking collectives: 32.1 us -> 26.5 us  [per_device(): between = in_order(core, lax.all_to_all(slots, Z, 0, 0, tiled=True))]
  transfers between devices with their start and end apart: 7 -> 7, of which waited for: 3 -> 3; matrix products, arithmetic and copies ran while one was open for 1% -> 1% of each run, Pallas kernels for 5% -> 4%
where the time goes in v5:
time: 128 us
  blocking collectives  59.5 us (46%)
  starting transfers between devices  35.7 us (28%)
  Pallas kernels  14.5 us (11%)
  waiting for transfers between devices  13 us (10%)
  other arithmetic  2.02 us (2%)
    all_to_all x2, blocking collectives, to_all(): return lax.all_to_all(slots, axis, 0, 0, tiled=True)  32.9 us
    all_to_all x1, blocking collectives, per_device(): between = in_order(core, lax.all_to_all(slots, Z, 0, 0, tiled=True))  26.5 us
    ppermute x4, starting transfers between devices, swap_cores(): return lax.ppermute(block, C, [(0, 1), (1, 0)])  21.2 us
    pallas_call x8, Pallas kernels, kernel(): pl.pallas_call(body, out_shape=out_shapes, in_specs=[pl.BlockSpec(memory_...  14.5 us
    all_to_all x1, waiting for transfers between devices, to_all(): return lax.all_to_all(slots, axis, 0, 0, tiled=True)  9.57 us
    all_to_all x1, starting transfers between devices, to_all(): return lax.all_to_all(slots, axis, 0, 0, tiled=True)  7.65 us
    ppermute x1, starting transfers between devices, per_device(): lax.ppermute(left_terms, panel, [(i + 1, i) for i in range(panels - 1)])  4.68 us
  transfers between devices with their start and end apart: 7, of which 3 were waited for; matrix products, arithmetic and copies ran while one was open for 1% of the time, Pallas kernels for 4%

profile of v5, /device:TPU:1, one launch (start us, length us, event | category | flops | bytes accessed | tf_op | source)
XLA Modules:
  0.0 127.6 jit_solution(16128779714640765027)
XLA Ops:
  0.6 0.0 copy-start
  0.6 0.0 copy-start.4
  0.7 0.0 copy-start.6
  0.7 0.0 copy-start.5
  0.7 0.9 pad_maximum_fusion.blocks_ref
  1.6 0.9 broadcast_in_dim.54
  2.5 7.7 %all-to-all-start = ((f16[8,264,128]{2,1,0:T(8,128)(2,1)}), f16[8,264,128]{2,1,0:T(8,128)(2,1)S(1)}, u32[]{:S(2)}, u32[]{:S(2)}) async-start(f16[8,264,128]{2,1,0:T(8,128)(2,1)} %broadcast_in_dim.54), calls=%async_computation | async-start | bytes 1081344 | tf_op jit(solution)/shard_map/all_to_all | solution.py:324
  10.2 0.0 copy-done.4
  10.2 0.1 compare_convert_fusion
  10.3 0.0 copy-done
  10.3 0.0 copy-done.6
  10.3 0.3 fusion.leaf_forward_ref
  10.6 0.0 copy-start.3
  10.6 0.2 convolution_bitcast_fusion
  10.8 4.7 %collective-permute-start = (f32[256,128]{1,0:T(8,128)S(1)}, f32[256,128]{1,0:T(8,128)S(1)}, u32[]{:S(2)}, u32[]{:S(2)}) collective-permute-start(f32[256,128]{1,0:T(8,128)S(1)} %convolution_bitcast_fusion), channel_id=1, source_target_pairs={{8,0},{16,8},{24,16},{32,24},{40,32},{48,40},{56,48},{64,56},{72,6... | collective-permute-start | bytes 393224 | tf_op jit(solution)/shard_map/ppermute | solution.py:374
  15.5 0.2 convolution_bitcast_fusion.1.own_ref
  15.8 9.6 %all-to-all-done = f16[8,264,128]{2,1,0:T(8,128)(2,1)S(1)} async-done(((f16[8,264,128]{2,1,0:T(8,128)(2,1)}), f16[8,264,128]{2,1,0:T(8,128)(2,1)S(1)}, u32[]{:S(2)}, u32[]{:S(2)}) %all-to-all-start) | async-done | bytes 540704 | tf_op jit(solution)/shard_map/all_to_all | solution.py:324
  25.3 0.1 convert_element_type.44.wire_ref
  25.4 0.0 collective-permute-done.right_ref
  25.4 0.7 shard_map.123
  26.1 5.6 %collective-permute-start.1 = (f32[896,256]{1,0:T(8,128)S(1)}, f32[896,256]{1,0:T(8,128)S(1)}, u32[]{:S(2)}, u32[]{:S(2)}) collective-permute-start(f32[896,256]{1,0:T(8,128)S(1)} %get-tuple-element.18.mine_ref), channel_id=1, source_target_pairs={{0,8},{8,0},{1,9},{9,1},{2,10},{10,2},{3,11},{11,3},{4,12},{12,4},... | collective-permute-start | bytes 2752520 | tf_op jit(solution)/shard_map/ppermute | solution.py:328
  31.7 0.1 pad_add_fusion.place_ref
  31.8 2.0 %collective-permute-done.1.other_ref = f32[896,256]{1,0:T(8,128)S(1)} collective-permute-done((f32[896,256]{1,0:T(8,128)S(1)}, f32[896,256]{1,0:T(8,128)S(1)}, u32[]{:S(2)}, u32[]{:S(2)}) %collective-permute-start.1) | collective-permute-done | bytes 917536 | tf_op jit(solution)/shard_map/ppermute | solution.py:328
  33.8 1.5 %shard_map.124 = f32[1032,128]{1,0:T(8,128)S(1)} custom-call(s32[3]{0:T(128)S(1)} %pad_add_fusion.place_ref, f32[896,256]{1,0:T(8,128)S(1)} %get-tuple-element.18.mine_ref, f32[896,256]{1,0:T(8,128)S(1)} %collective-permute-done.1.other_ref), custom_call_target="tpu_custom_call" | custom-call | bytes 2363404 | tf_op jit(solution)/shard_map/pallas_call | solution.py:43
  35.4 0.1 broadcast_in_dim.55
  35.5 18.2 %all_to_all.20 = f16[4,1032,128]{2,1,0:T(8,128)(2,1)S(1)} all-to-all(f16[4,1032,128]{2,1,0:T(8,128)(2,1)S(1)} %broadcast_in_dim.55), channel_id=1, replica_groups=mesh['z'=8,'x'=4,'c'=2,'y'=8] {'x'}, dimensions={0} | all-to-all | bytes 2113536 | tf_op jit(solution)/shard_map/all_to_all | solution.py:324
  53.7 3.7 %collective-permute-start.2 = (f16[4,1032,128]{2,1,0:T(8,128)(2,1)S(1)}, f16[4,1032,128]{2,1,0:T(8,128)(2,1)S(1)}, u32[]{:S(2)}, u32[]{:S(2)}) collective-permute-start(f16[4,1032,128]{2,1,0:T(8,128)(2,1)S(1)} %all_to_all.20), channel_id=1, source_target_pairs={{0,8},{8,0},{1,9},{9,1},{2,10},{10,2},{3,11},{11,3},{4,12},{12,4},... | collective-permute-start | bytes 3170312 | tf_op jit(solution)/shard_map/ppermute | solution.py:328
  57.4 2.1 %collective-permute-start.3 = (f16[1032,128]{1,0:T(8,128)(2,1)S(1)}, f16[1032,128]{1,0:T(8,128)(2,1)S(1)}, u32[]{:S(2)}, u32[]{:S(2)}) collective-permute-start(f16[1032,128]{1,0:T(8,128)(2,1)S(1)} %convert_element_type.52), channel_id=1, source_target_pairs={{8,16},{24,32},{40,48},{56,64},{72,80},{88,96},{104,112},{120,128}... | collective-permute-start | bytes 792584 | tf_op jit(solution)/shard_map/ppermute | solution.py:389
  59.6 0.1 convert_element_type.49.first_ref.mine_ref.pair_first
  59.7 0.0 collective-permute-done.2
  59.7 0.1 convert_element_type.50.second_ref.other_ref.pair_second
  59.9 1.5 %shard_map.125 = f32[2,392,128]{2,1,0:T(8,128)S(1)} custom-call(s32[3]{0:T(128)S(1)} %pad_add_fusion.place_ref, f32[4,1032,128]{2,1,0:T(8,128)S(1)} %convert_element_type.49.first_ref.mine_ref.pair_first, f32[4,1032,128]{2,1,0:T(8,128)S(1)} %convert_element_type.50.second_ref.other_ref.pair_second), custom_call_target="tpu_custom_call" | custom-call | bytes 4628492 | tf_op jit(solution)/shard_map/pallas_call | solution.py:43
  61.4 1.5 %collective-permute-done.3 = f16[1032,128]{1,0:T(8,128)(2,1)S(1)} collective-permute-done((f16[1032,128]{1,0:T(8,128)(2,1)S(1)}, f16[1032,128]{1,0:T(8,128)(2,1)S(1)}, u32[]{:S(2)}, u32[]{:S(2)}) %collective-permute-start.3) | collective-permute-done | bytes 264224 | tf_op jit(solution)/shard_map/ppermute | solution.py:389
  62.9 0.2 broadcast_select_fusion
  63.2 26.5 %all_to_all.21 = f16[8,392,128]{2,1,0:T(8,128)(2,1)S(1)} all-to-all(f16[8,392,128]{2,1,0:T(8,128)(2,1)S(1)} %broadcast_select_fusion), channel_id=1, replica_groups=mesh['z'=8,'x'=4,'c'=2,'y'=8] {'z'}, dimensions={0} | all-to-all | bytes 1605632 | tf_op jit(solution)/shard_map/all_to_all | solution.py:400
  89.7 9.6 %collective-permute-start.4 = (f16[8,392,128]{2,1,0:T(8,128)(2,1)S(1)}, f16[8,392,128]{2,1,0:T(8,128)(2,1)S(1)}, u32[]{:S(2)}, u32[]{:S(2)}) collective-permute-start(f16[8,392,128]{2,1,0:T(8,128)(2,1)S(1)} %all_to_all.21), channel_id=1, source_target_pairs={{0,8},{8,0},{1,9},{9,1},{2,10},{10,2},{3,11},{11,3},{4,12},{12,4},... | collective-permute-start | bytes 2408456 | tf_op jit(solution)/shard_map/ppermute | solution.py:328
  99.3 2.8 %shard_map.126 = (f32[256,128]{1,0:T(8,128)S(1)}, f32[128,128]{1,0:T(8,128)S(1)}, f32[384,256]{1,0:T(8,128)S(1)}, f32[4,384,256]{2,1,0:T(8,128)S(1)}) custom-call(s32[3]{0:T(128)S(1)} %pad_add_fusion.place_ref, f32[4,1032,128]{2,1,0:T(8,128)S(1)} %convert_element_type.49.first_ref.mine_ref.pair_first, ...), custom_call_target="tpu_custom_call" | custom-call | bytes 6389772 | tf_op jit(solution)/shard_map/pallas_call | solution.py:43
  102.1 0.1 convert_element_type.53.plane_mine.plane_first
  102.2 0.0 collective-permute-done.4
  102.2 0.1 convert_element_type.54.plane_other.plane_second
  102.3 2.0 %shard_map.127 = (bf16[128,128]{1,0:T(8,128)(2,1)S(1)}, f32[128,256]{1,0:T(8,128)S(1)}) custom-call(s32[3]{0:T(128)S(1)} %pad_add_fusion.place_ref, f32[8,392,128]{2,1,0:T(8,128)S(1)} %convert_element_type.53.plane_mine.plane_first, f32[8,392,128]{2,1,0:T(8,128)S(1)} %convert_element_type.54.plane_other.plane_second, ...), custom_call_target="tpu_custom_call" | custom-call | bytes 3571724 | tf_op jit(solution)/shard_map/pallas_call | solution.py:43
  104.4 14.8 %all_to_all.22.value_first = bf16[8,128,128]{2,1,0:T(8,128)(2,1)S(1)} all-to-all(bf16[8,128,128]{2,1,0:T(8,128)(2,1)S(1)} %broadcast_in_dim.60), channel_id=1, replica_groups=mesh['z'=8,'x'=4,'c'=2,'y'=8] {'z'}, dimensions={0} | all-to-all | bytes 524288 | tf_op jit(solution)/shard_map/all_to_all | solution.py:324
  119.2 2.3 %collective-permute-start.5 = (bf16[8,128,128]{2,1,0:T(8,128)(2,1)S(1)}, bf16[8,128,128]{2,1,0:T(8,128)(2,1)S(1)}, u32[]{:S(2)}, u32[]{:S(2)}) collective-permute-start(bf16[8,128,128]{2,1,0:T(8,128)(2,1)S(1)} %all_to_all.22.value_first), channel_id=1, source_target_pairs={{0,8},{8,0},{1,9},{9,1},{2,10},{10,2},{3,11},{11,3},{4,12},{12,4},... | collective-permute-start | bytes 786440 | tf_op jit(solution)/shard_map/ppermute | solution.py:328
  121.5 0.0 copy-start.1
  121.6 0.0 copy-start.2
  121.6 1.5 %shard_map.128 = (f32[4,128,256]{2,1,0:T(8,128)S(1)}, f32[128,256]{1,0:T(8,128)S(1)}, f32[128,256]{1,0:T(8,128)S(1)}, f32[128,256]{1,0:T(8,128)S(1)}) custom-call(s32[3]{0:T(128)S(1)} %pad_add_fusion.place_ref, f32[128,256]{1,0:T(8,128)S(1)} %get-tuple-element.24.ahead_ref, f32[384,256]{1,0:T(8,128)S(1)} %get-tuple-element.25.start_factor_ref, ...), custom_call_target="tpu_custom_call" | custom-call | bytes 5378060 | tf_op jit(solution)/shard_map/pallas_call | solution.py:43
  123.0 0.0 collective-permute-done.5.value_second
  123.1 4.5 %shard_map.129 = (f32[2,256,128]{2,1,0:T(8,128)}, f32[256,128]{1,0:T(8,128)}) custom-call(s32[3]{0:T(128)S(1)} %pad_add_fusion.place_ref, s32[2]{0:T(128)S(1)} %copy-done.4, bf16[8,128,128]{2,1,0:T(8,128)(2,1)S(1)} %all_to_all.22.value_first, bf16[8,128,128]{2,1,0:T(8,128)(2,1)S(1)} %collective-permute-done.5.value_second, ...), custom_call_target="tpu_custom_call" | custom-call | bytes 11898900 | tf_op jit(solution)/shard_map/pallas_call | solution.py:43
  (13 shorter events, 0.3 us)
Async XLA Ops:
  0.6 9.6 %copy-start = (bf16[2,256,256]{2,1,0:T(8,128)(2,1)S(1)}, bf16[2,256,256]{2,1,0:T(8,128)(2,1)}, u32[]{:S(2)}) copy-start(bf16[2,256,256]{2,1,0:T(8,128)(2,1)} %param.14) | copy-start | bytes 786436
  0.6 9.5 %copy-start.4 = (s32[2]{0:T(128)S(1)}, s32[2]{0:T(128)}, u32[]{:S(2)}) copy-start(s32[2]{0:T(128)} %size_ref.1) | copy-start | bytes 28
  0.7 9.6 %copy-start.6 = (f32[2,256,128]{2,1,0:T(8,128)S(1)}, f32[2,256,128]{2,1,0:T(8,128)}, u32[]{:S(2)}) copy-start(f32[2,256,128]{2,1,0:T(8,128)} %param.11) | copy-start | bytes 786436
  0.7 9.9 %copy-start.5 = (bf16[2,2,256,256]{3,2,1,0:T(8,128)(2,1)S(1)}, bf16[2,2,256,256]{3,2,1,0:T(8,128)(2,1)}, u32[]{:S(2)}) copy-start(bf16[2,2,256,256]{3,2,1,0:T(8,128)(2,1)} %param.15) | copy-start | bytes 1572868
  2.5 22.8 %all-to-all-start = ((f16[8,264,128]{2,1,0:T(8,128)(2,1)}), f16[8,264,128]{2,1,0:T(8,128)(2,1)S(1)}, u32[]{:S(2)}, u32[]{:S(2)}) async-start(f16[8,264,128]{2,1,0:T(8,128)(2,1)} %broadcast_in_dim.54), calls=%async_computation | async-start | bytes 1081344 | tf_op jit(solution)/shard_map/all_to_all | solution.py:324
  10.6 14.8 %copy-start.3 = (f32[1,256,128]{2,1,0:T(8,128)S(1)}, f32[1,256,128]{2,1,0:T(8,128)}, u32[]{:S(2)}) copy-start(f32[1,256,128]{2,1,0:T(8,128)} %param.12) | copy-start | bytes 393220
  10.8 14.6 %collective-permute-start = (f32[256,128]{1,0:T(8,128)S(1)}, f32[256,128]{1,0:T(8,128)S(1)}, u32[]{:S(2)}, u32[]{:S(2)}) collective-permute-start(f32[256,128]{1,0:T(8,128)S(1)} %convolution_bitcast_fusion), channel_id=1, source_target_pairs={{8,0},{16,8},{24,16},{32,24},{40,32},{48,40},{56,48},{64,56},{72,6... | collective-permute-start | bytes 393224 | tf_op jit(solution)/shard_map/ppermute | solution.py:374
  26.1 7.7 %collective-permute-start.1 = (f32[896,256]{1,0:T(8,128)S(1)}, f32[896,256]{1,0:T(8,128)S(1)}, u32[]{:S(2)}, u32[]{:S(2)}) collective-permute-start(f32[896,256]{1,0:T(8,128)S(1)} %get-tuple-element.18.mine_ref), channel_id=1, source_target_pairs={{0,8},{8,0},{1,9},{9,1},{2,10},{10,2},{3,11},{11,3},{4,12},{12,4},... | collective-permute-start | bytes 2752520 | tf_op jit(solution)/shard_map/ppermute | solution.py:328
  53.7 6.0 %collective-permute-start.2 = (f16[4,1032,128]{2,1,0:T(8,128)(2,1)S(1)}, f16[4,1032,128]{2,1,0:T(8,128)(2,1)S(1)}, u32[]{:S(2)}, u32[]{:S(2)}) collective-permute-start(f16[4,1032,128]{2,1,0:T(8,128)(2,1)S(1)} %all_to_all.20), channel_id=1, source_target_pairs={{0,8},{8,0},{1,9},{9,1},{2,10},{10,2},{3,11},{11,3},{4,12},{12,4},... | collective-permute-start | bytes 3170312 | tf_op jit(solution)/shard_map/ppermute | solution.py:328
  57.4 5.4 %collective-permute-start.3 = (f16[1032,128]{1,0:T(8,128)(2,1)S(1)}, f16[1032,128]{1,0:T(8,128)(2,1)S(1)}, u32[]{:S(2)}, u32[]{:S(2)}) collective-permute-start(f16[1032,128]{1,0:T(8,128)(2,1)S(1)} %convert_element_type.52), channel_id=1, source_target_pairs={{8,16},{24,32},{40,48},{56,64},{72,80},{88,96},{104,112},{120,128}... | collective-permute-start | bytes 792584 | tf_op jit(solution)/shard_map/ppermute | solution.py:389
  89.7 12.5 %collective-permute-start.4 = (f16[8,392,128]{2,1,0:T(8,128)(2,1)S(1)}, f16[8,392,128]{2,1,0:T(8,128)(2,1)S(1)}, u32[]{:S(2)}, u32[]{:S(2)}) collective-permute-start(f16[8,392,128]{2,1,0:T(8,128)(2,1)S(1)} %all_to_all.21), channel_id=1, source_target_pairs={{0,8},{8,0},{1,9},{9,1},{2,10},{10,2},{3,11},{11,3},{4,12},{12,4},... | collective-permute-start | bytes 2408456 | tf_op jit(solution)/shard_map/ppermute | solution.py:328
  119.2 3.9 %collective-permute-start.5 = (bf16[8,128,128]{2,1,0:T(8,128)(2,1)S(1)}, bf16[8,128,128]{2,1,0:T(8,128)(2,1)S(1)}, u32[]{:S(2)}, u32[]{:S(2)}) collective-permute-start(bf16[8,128,128]{2,1,0:T(8,128)(2,1)S(1)} %all_to_all.22.value_first), channel_id=1, source_target_pairs={{0,8},{8,0},{1,9},{9,1},{2,10},{10,2},{3,11},{11,3},{4,12},{12,4},... | collective-permute-start | bytes 786440 | tf_op jit(solution)/shard_map/ppermute | solution.py:328
  121.5 1.5 %copy-start.1 = (bf16[2,2,256,256]{3,2,1,0:T(8,128)(2,1)S(1)}, bf16[2,2,256,256]{3,2,1,0:T(8,128)(2,1)}, u32[]{:S(2)}) copy-start(bf16[2,2,256,256]{3,2,1,0:T(8,128)(2,1)} %far_upper_ref.1) | copy-start | bytes 1572868
  121.6 1.5 %copy-start.2 = (bf16[2,256,256]{2,1,0:T(8,128)(2,1)S(1)}, bf16[2,256,256]{2,1,0:T(8,128)(2,1)}, u32[]{:S(2)}) copy-start(bf16[2,256,256]{2,1,0:T(8,128)(2,1)} %far_upper_inv_ref.1) | copy-start | bytes 786436

commit v6 on v5

--- a/solution.py
+++ b/solution.py
@@ -197,11 +197,11 @@
     encode(wire_ref, (1,), jnp.concatenate([behind, further], axis=1))
 
 
-def through_kernel(place_ref, mine_ref, other_ref, factor_ref, value_ref, start_ref, own_ref):
+def through_kernel(place_ref, mine_ref, other_ref, start_ref, own_ref):
     x = place_ref[1]
     pairs = Wires(place_ref[0], mine_ref, other_ref)
     width = pairs.width
-    forward, backward, through, value, back_value = pair_columns(width)
+    forward, _, through, value, back_value = pair_columns(width)
 
     def add_value(block, further):
         return jnp.concatenate([block[:width], block[width:] + further], axis=0)
@@ -219,9 +219,15 @@
     start_ref[...] = start
     for i in range(pairs.count):
         own_ref[i] = own[i]
-    behind = own[-1]
+
+
+def compose_kernel(place_ref, mine_ref, other_ref, own_ref, factor_ref, value_ref):
+    pairs = Wires(place_ref[0], mine_ref, other_ref)
+    width = pairs.width
+    backward = pair_columns(width)[1]
+    behind = own_ref[pairs.count - 1]
     for i in range(pairs.count - 2, -1, -1):
-        factor, offset = pairs.matrix(i, backward), own[i]
+        factor, offset = pairs.matrix(i, backward), own_ref[i]
         if i == 0:
             factor, offset = half_columns(pairs.core, factor), half_columns(pairs.core, offset)
         behind = offset + product(behind, factor)
@@ -393,22 +399,22 @@
     pairs = in_order(core, to_all(wire, X))
     (wire,) = kernel(plane_kernel, [wire_shape(2, part, width + part)], place, *pairs)
 
-    wire, previous = lax.optimization_barrier((wire.astype(F16), previous))
+    start, own = kernel(
+        through_kernel,
+        [shape(width + samples, width), shape(chips, width + samples, width)],
+        place,
+        *pairs,
+    )
+    wire, previous, start, own = lax.optimization_barrier(
+        (wire.astype(F16), previous, start, own)
+    )
     previous = previous.astype(F32)
     index = jnp.arange(planes, dtype=jnp.int32)[:, None, None]
     slots = jnp.where(index > z, wire[0][None], wire[1][None])
     between = in_order(core, lax.all_to_all(slots, Z, 0, 0, tiled=True))
     block = shape(samples, width)
-    *through, start, own = kernel(
-        through_kernel,
-        [
-            shape(width, part),
-            shape(samples, part),
-            shape(width + samples, width),
-            shape(chips, width + samples, width),
-        ],
-        place,
-        *pairs,
+    through = kernel(
+        compose_kernel, [shape(width, part), shape(samples, part)], place, *pairs, own
     )
     wire, ahead = kernel(
         forward_kernel, [shape(samples, part, dtype=BF16), block], place, *between, *through

time: 128 us -> 128 us (level)
    ppermute x1, waiting for transfers between devices: 1.46 us -> 0.01 us  [per_device(): previous = lax.ppermute(previous.astype(F16), panel, to_next_chip)]
    pallas_call x8 -> x9, Pallas kernels: 14.5 us -> 15.2 us  [kernel(): pl.pallas_call(body, out_shape=out_shapes, in_specs=[pl.BlockSpec(memory_...]
  transfers between devices with their start and end apart: 7 -> 7, of which waited for: 3 -> 3; matrix products, arithmetic and copies ran while one was open for 1% -> 1% of each run, Pallas kernels for 4% -> 5%
where the time goes in v6:
time: 128 us; the launch traced here: 127 us
  blocking collectives  60.2 us (47%)
  starting transfers between devices  35 us (27%)
  Pallas kernels  15.2 us (12%)
  waiting for transfers between devices  11.8 us (9%)
  other arithmetic  2.02 us (2%)
    all_to_all x2, blocking collectives, to_all(): return lax.all_to_all(slots, axis, 0, 0, tiled=True)  32.9 us
    all_to_all x1, blocking collectives, per_device(): between = in_order(core, lax.all_to_all(slots, Z, 0, 0, tiled=True))  27.3 us
    ppermute x4, starting transfers between devices, swap_cores(): return lax.ppermute(block, C, [(0, 1), (1, 0)])  20.5 us
    pallas_call x9, Pallas kernels, kernel(): pl.pallas_call(body, out_shape=out_shapes, in_specs=[pl.BlockSpec(memory_...  15.2 us
    all_to_all x1, waiting for transfers between devices, to_all(): return lax.all_to_all(slots, axis, 0, 0, tiled=True)  9.56 us
    all_to_all x1, starting transfers between devices, to_all(): return lax.all_to_all(slots, axis, 0, 0, tiled=True)  7.65 us
    ppermute x1, starting transfers between devices, per_device(): lax.ppermute(left_terms, panel, [(i + 1, i) for i in range(panels - 1)])  4.68 us
  transfers between devices with their start and end apart: 7, of which 3 were waited for; matrix products, arithmetic and copies ran while one was open for 1% of the time, Pallas kernels for 5%

profile of v6, /device:TPU:1, one launch (start us, length us, event | category | flops | bytes accessed | tf_op | source)
XLA Modules:
  0.0 127.1 jit_solution(2117506326793500325)
XLA Ops:
  0.6 0.0 copy-start
  0.6 0.0 copy-start.4
  0.7 0.0 copy-start.6
  0.7 0.0 copy-start.5
  0.7 0.9 pad_maximum_fusion.blocks_ref
  1.6 0.9 broadcast_in_dim.54
  2.5 7.7 %all-to-all-start = ((f16[8,264,128]{2,1,0:T(8,128)(2,1)}), f16[8,264,128]{2,1,0:T(8,128)(2,1)S(1)}, u32[]{:S(2)}, u32[]{:S(2)}) async-start(f16[8,264,128]{2,1,0:T(8,128)(2,1)} %broadcast_in_dim.54), calls=%async_computation | async-start | bytes 1081344 | tf_op jit(solution)/shard_map/all_to_all | solution.py:330
  10.2 0.0 copy-done.4
  10.2 0.1 compare_convert_fusion
  10.3 0.3 fusion.leaf_forward_ref
  10.6 0.0 copy-done.5
  10.6 0.0 copy-start.3
  10.6 0.2 convolution_bitcast_fusion
  10.8 4.7 %collective-permute-start = (f32[256,128]{1,0:T(8,128)S(1)}, f32[256,128]{1,0:T(8,128)S(1)}, u32[]{:S(2)}, u32[]{:S(2)}) collective-permute-start(f32[256,128]{1,0:T(8,128)S(1)} %convolution_bitcast_fusion), channel_id=1, source_target_pairs={{8,0},{16,8},{24,16},{32,24},{40,32},{48,40},{56,48},{64,56},{72,6... | collective-permute-start | bytes 393224 | tf_op jit(solution)/shard_map/ppermute | solution.py:380
  15.5 0.2 convolution_bitcast_fusion.1.own_ref
  15.8 9.6 %all-to-all-done = f16[8,264,128]{2,1,0:T(8,128)(2,1)S(1)} async-done(((f16[8,264,128]{2,1,0:T(8,128)(2,1)}), f16[8,264,128]{2,1,0:T(8,128)(2,1)S(1)}, u32[]{:S(2)}, u32[]{:S(2)}) %all-to-all-start) | async-done | bytes 540704 | tf_op jit(solution)/shard_map/all_to_all | solution.py:330
  25.3 0.1 convert_element_type.44.wire_ref
  25.4 0.0 collective-permute-done.right_ref
  25.4 0.7 shard_map.123
  26.1 5.6 %collective-permute-start.1 = (f32[896,256]{1,0:T(8,128)S(1)}, f32[896,256]{1,0:T(8,128)S(1)}, u32[]{:S(2)}, u32[]{:S(2)}) collective-permute-start(f32[896,256]{1,0:T(8,128)S(1)} %get-tuple-element.20.mine_ref), channel_id=1, source_target_pairs={{0,8},{8,0},{1,9},{9,1},{2,10},{10,2},{3,11},{11,3},{4,12},{12,4},... | collective-permute-start | bytes 2752520 | tf_op jit(solution)/shard_map/ppermute | solution.py:334
  31.7 0.1 pad_add_fusion.place_ref
  31.8 2.0 %collective-permute-done.1.other_ref = f32[896,256]{1,0:T(8,128)S(1)} collective-permute-done((f32[896,256]{1,0:T(8,128)S(1)}, f32[896,256]{1,0:T(8,128)S(1)}, u32[]{:S(2)}, u32[]{:S(2)}) %collective-permute-start.1) | collective-permute-done | bytes 917536 | tf_op jit(solution)/shard_map/ppermute | solution.py:334
  33.8 1.5 %shard_map.124 = f32[1032,128]{1,0:T(8,128)S(1)} custom-call(s32[3]{0:T(128)S(1)} %pad_add_fusion.place_ref, f32[896,256]{1,0:T(8,128)S(1)} %get-tuple-element.20.mine_ref, f32[896,256]{1,0:T(8,128)S(1)} %collective-permute-done.1.other_ref), custom_call_target="tpu_custom_call" | custom-call | bytes 2363404 | tf_op jit(solution)/shard_map/pallas_call | solution.py:43
  35.4 0.1 broadcast_in_dim.55
  35.5 18.1 %all_to_all.20 = f16[4,1032,128]{2,1,0:T(8,128)(2,1)S(1)} all-to-all(f16[4,1032,128]{2,1,0:T(8,128)(2,1)S(1)} %broadcast_in_dim.55), channel_id=1, replica_groups=mesh['z'=8,'x'=4,'c'=2,'y'=8] {'x'}, dimensions={0} | all-to-all | bytes 2113536 | tf_op jit(solution)/shard_map/all_to_all | solution.py:330
  53.7 3.7 %collective-permute-start.2 = (f16[4,1032,128]{2,1,0:T(8,128)(2,1)S(1)}, f16[4,1032,128]{2,1,0:T(8,128)(2,1)S(1)}, u32[]{:S(2)}, u32[]{:S(2)}) collective-permute-start(f16[4,1032,128]{2,1,0:T(8,128)(2,1)S(1)} %all_to_all.20), channel_id=1, source_target_pairs={{0,8},{8,0},{1,9},{9,1},{2,10},{10,2},{3,11},{11,3},{4,12},{12,4},... | collective-permute-start | bytes 3170312 | tf_op jit(solution)/shard_map/ppermute | solution.py:334
  57.4 2.1 %collective-permute-start.3 = (f16[1032,128]{1,0:T(8,128)(2,1)S(1)}, f16[1032,128]{1,0:T(8,128)(2,1)S(1)}, u32[]{:S(2)}, u32[]{:S(2)}) collective-permute-start(f16[1032,128]{1,0:T(8,128)(2,1)S(1)} %convert_element_type.52), channel_id=1, source_target_pairs={{8,16},{24,32},{40,48},{56,64},{72,80},{88,96},{104,112},{120,128}... | collective-permute-start | bytes 792584 | tf_op jit(solution)/shard_map/ppermute | solution.py:395
  59.6 0.1 convert_element_type.49.first_ref.mine_ref.pair_first
  59.7 0.0 collective-permute-done.2
  59.7 0.1 convert_element_type.50.second_ref.other_ref.pair_second
  59.9 1.5 %shard_map.125 = f32[2,392,128]{2,1,0:T(8,128)S(1)} custom-call(s32[3]{0:T(128)S(1)} %pad_add_fusion.place_ref, f32[4,1032,128]{2,1,0:T(8,128)S(1)} %convert_element_type.49.first_ref.mine_ref.pair_first, f32[4,1032,128]{2,1,0:T(8,128)S(1)} %convert_element_type.50.second_ref.other_ref.pair_second), custom_call_target="tpu_custom_call" | custom-call | bytes 4628492 | tf_op jit(solution)/shard_map/pallas_call | solution.py:43
  61.4 2.0 %shard_map.126 = (f32[384,256]{1,0:T(8,128)S(1)}, f32[4,384,256]{2,1,0:T(8,128)S(1)}) custom-call(s32[3]{0:T(128)S(1)} %pad_add_fusion.place_ref, f32[4,1032,128]{2,1,0:T(8,128)S(1)} %convert_element_type.49.first_ref.mine_ref.pair_first, f32[4,1032,128]{2,1,0:T(8,128)S(1)} %convert_element_type.50.second_ref.other_ref.pair_second), custom_call_target="tpu_custom_call" | custom-call | bytes 6193164 | tf_op jit(solution)/shard_map/pallas_call | solution.py:43
  63.4 0.0 collective-permute-done.3
  63.4 0.2 broadcast_select_fusion
  63.7 27.3 %all_to_all.21 = f16[8,392,128]{2,1,0:T(8,128)(2,1)S(1)} all-to-all(f16[8,392,128]{2,1,0:T(8,128)(2,1)S(1)} %broadcast_select_fusion), channel_id=1, replica_groups=mesh['z'=8,'x'=4,'c'=2,'y'=8] {'z'}, dimensions={0} | all-to-all | bytes 1605632 | tf_op jit(solution)/shard_map/all_to_all | solution.py:414
  91.0 8.8 %collective-permute-start.4 = (f16[8,392,128]{2,1,0:T(8,128)(2,1)S(1)}, f16[8,392,128]{2,1,0:T(8,128)(2,1)S(1)}, u32[]{:S(2)}, u32[]{:S(2)}) collective-permute-start(f16[8,392,128]{2,1,0:T(8,128)(2,1)S(1)} %all_to_all.21), channel_id=1, source_target_pairs={{0,8},{8,0},{1,9},{9,1},{2,10},{10,2},{3,11},{11,3},{4,12},{12,4},... | collective-permute-start | bytes 2408456 | tf_op jit(solution)/shard_map/ppermute | solution.py:334
  99.8 1.6 %shard_map.127 = (f32[256,128]{1,0:T(8,128)S(1)}, f32[128,128]{1,0:T(8,128)S(1)}) custom-call(s32[3]{0:T(128)S(1)} %pad_add_fusion.place_ref, f32[4,1032,128]{2,1,0:T(8,128)S(1)} %convert_element_type.49.first_ref.mine_ref.pair_first, f32[4,1032,128]{2,1,0:T(8,128)S(1)} %convert_element_type.50.second_ref.other_ref.pair_second, ...), custom_call_target="tpu_custom_call" | custom-call | bytes 5996556 | tf_op jit(solution)/shard_map/pallas_call | solution.py:43
  101.4 0.1 convert_element_type.53.plane_mine.plane_first
  101.5 0.2 collective-permute-done.4
  101.8 0.1 convert_element_type.54.plane_other.plane_second
  101.9 2.0 %shard_map.128 = (bf16[128,128]{1,0:T(8,128)(2,1)S(1)}, f32[128,256]{1,0:T(8,128)S(1)}) custom-call(s32[3]{0:T(128)S(1)} %pad_add_fusion.place_ref, f32[8,392,128]{2,1,0:T(8,128)S(1)} %convert_element_type.53.plane_mine.plane_first, f32[8,392,128]{2,1,0:T(8,128)S(1)} %convert_element_type.54.plane_other.plane_second, ...), custom_call_target="tpu_custom_call" | custom-call | bytes 3571724 | tf_op jit(solution)/shard_map/pallas_call | solution.py:43
  103.9 14.8 %all_to_all.22.value_first = bf16[8,128,128]{2,1,0:T(8,128)(2,1)S(1)} all-to-all(bf16[8,128,128]{2,1,0:T(8,128)(2,1)S(1)} %broadcast_in_dim.60), channel_id=1, replica_groups=mesh['z'=8,'x'=4,'c'=2,'y'=8] {'z'}, dimensions={0} | all-to-all | bytes 524288 | tf_op jit(solution)/shard_map/all_to_all | solution.py:330
  118.6 2.4 %collective-permute-start.5 = (bf16[8,128,128]{2,1,0:T(8,128)(2,1)S(1)}, bf16[8,128,128]{2,1,0:T(8,128)(2,1)S(1)}, u32[]{:S(2)}, u32[]{:S(2)}) collective-permute-start(bf16[8,128,128]{2,1,0:T(8,128)(2,1)S(1)} %all_to_all.22.value_first), channel_id=1, source_target_pairs={{0,8},{8,0},{1,9},{9,1},{2,10},{10,2},{3,11},{11,3},{4,12},{12,4},... | collective-permute-start | bytes 786440 | tf_op jit(solution)/shard_map/ppermute | solution.py:334
  121.1 0.0 copy-start.1
  121.1 0.0 copy-start.2
  121.1 1.5 %shard_map.129 = (f32[4,128,256]{2,1,0:T(8,128)S(1)}, f32[128,256]{1,0:T(8,128)S(1)}, f32[128,256]{1,0:T(8,128)S(1)}, f32[128,256]{1,0:T(8,128)S(1)}) custom-call(s32[3]{0:T(128)S(1)} %pad_add_fusion.place_ref, f32[128,256]{1,0:T(8,128)S(1)} %get-tuple-element.29.ahead_ref, f32[384,256]{1,0:T(8,128)S(1)} %get-tuple-element.30.start_factor_ref, ...), custom_call_target="tpu_custom_call" | custom-call | bytes 5378060 | tf_op jit(solution)/shard_map/pallas_call | solution.py:43
  122.6 0.0 collective-permute-done.5.value_second
  122.6 4.5 %shard_map.130 = (f32[2,256,128]{2,1,0:T(8,128)}, f32[256,128]{1,0:T(8,128)}) custom-call(s32[3]{0:T(128)S(1)} %pad_add_fusion.place_ref, s32[2]{0:T(128)S(1)} %copy-done.4, bf16[8,128,128]{2,1,0:T(8,128)(2,1)S(1)} %all_to_all.22.value_first, bf16[8,128,128]{2,1,0:T(8,128)(2,1)S(1)} %collective-permute-done.5.value_second, ...), custom_call_target="tpu_custom_call" | custom-call | bytes 11898900 | tf_op jit(solution)/shard_map/pallas_call | solution.py:43
  (14 shorter events, 0.3 us)
Async XLA Ops:
  0.6 9.6 %copy-start = (bf16[2,256,256]{2,1,0:T(8,128)(2,1)S(1)}, bf16[2,256,256]{2,1,0:T(8,128)(2,1)}, u32[]{:S(2)}) copy-start(bf16[2,256,256]{2,1,0:T(8,128)(2,1)} %param.14) | copy-start | bytes 786436
  0.6 9.5 %copy-start.4 = (s32[2]{0:T(128)S(1)}, s32[2]{0:T(128)}, u32[]{:S(2)}) copy-start(s32[2]{0:T(128)} %size_ref.1) | copy-start | bytes 28
  0.7 9.6 %copy-start.6 = (f32[2,256,128]{2,1,0:T(8,128)S(1)}, f32[2,256,128]{2,1,0:T(8,128)}, u32[]{:S(2)}) copy-start(f32[2,256,128]{2,1,0:T(8,128)} %param.11) | copy-start | bytes 786436
  0.7 9.9 %copy-start.5 = (bf16[2,2,256,256]{3,2,1,0:T(8,128)(2,1)S(1)}, bf16[2,2,256,256]{3,2,1,0:T(8,128)(2,1)}, u32[]{:S(2)}) copy-start(bf16[2,2,256,256]{3,2,1,0:T(8,128)(2,1)} %param.15) | copy-start | bytes 1572868
  2.5 22.8 %all-to-all-start = ((f16[8,264,128]{2,1,0:T(8,128)(2,1)}), f16[8,264,128]{2,1,0:T(8,128)(2,1)S(1)}, u32[]{:S(2)}, u32[]{:S(2)}) async-start(f16[8,264,128]{2,1,0:T(8,128)(2,1)} %broadcast_in_dim.54), calls=%async_computation | async-start | bytes 1081344 | tf_op jit(solution)/shard_map/all_to_all | solution.py:330
  10.6 14.8 %copy-start.3 = (f32[1,256,128]{2,1,0:T(8,128)S(1)}, f32[1,256,128]{2,1,0:T(8,128)}, u32[]{:S(2)}) copy-start(f32[1,256,128]{2,1,0:T(8,128)} %param.12) | copy-start | bytes 393220
  10.8 14.6 %collective-permute-start = (f32[256,128]{1,0:T(8,128)S(1)}, f32[256,128]{1,0:T(8,128)S(1)}, u32[]{:S(2)}, u32[]{:S(2)}) collective-permute-start(f32[256,128]{1,0:T(8,128)S(1)} %convolution_bitcast_fusion), channel_id=1, source_target_pairs={{8,0},{16,8},{24,16},{32,24},{40,32},{48,40},{56,48},{64,56},{72,6... | collective-permute-start | bytes 393224 | tf_op jit(solution)/shard_map/ppermute | solution.py:380
  26.1 7.7 %collective-permute-start.1 = (f32[896,256]{1,0:T(8,128)S(1)}, f32[896,256]{1,0:T(8,128)S(1)}, u32[]{:S(2)}, u32[]{:S(2)}) collective-permute-start(f32[896,256]{1,0:T(8,128)S(1)} %get-tuple-element.20.mine_ref), channel_id=1, source_target_pairs={{0,8},{8,0},{1,9},{9,1},{2,10},{10,2},{3,11},{11,3},{4,12},{12,4},... | collective-permute-start | bytes 2752520 | tf_op jit(solution)/shard_map/ppermute | solution.py:334
  53.7 6.1 %collective-permute-start.2 = (f16[4,1032,128]{2,1,0:T(8,128)(2,1)S(1)}, f16[4,1032,128]{2,1,0:T(8,128)(2,1)S(1)}, u32[]{:S(2)}, u32[]{:S(2)}) collective-permute-start(f16[4,1032,128]{2,1,0:T(8,128)(2,1)S(1)} %all_to_all.20), channel_id=1, source_target_pairs={{0,8},{8,0},{1,9},{9,1},{2,10},{10,2},{3,11},{11,3},{4,12},{12,4},... | collective-permute-start | bytes 3170312 | tf_op jit(solution)/shard_map/ppermute | solution.py:334
  57.4 5.9 %collective-permute-start.3 = (f16[1032,128]{1,0:T(8,128)(2,1)S(1)}, f16[1032,128]{1,0:T(8,128)(2,1)S(1)}, u32[]{:S(2)}, u32[]{:S(2)}) collective-permute-start(f16[1032,128]{1,0:T(8,128)(2,1)S(1)} %convert_element_type.52), channel_id=1, source_target_pairs={{8,16},{24,32},{40,48},{56,64},{72,80},{88,96},{104,112},{120,128}... | collective-permute-start | bytes 792584 | tf_op jit(solution)/shard_map/ppermute | solution.py:395
  91.0 10.8 %collective-permute-start.4 = (f16[8,392,128]{2,1,0:T(8,128)(2,1)S(1)}, f16[8,392,128]{2,1,0:T(8,128)(2,1)S(1)}, u32[]{:S(2)}, u32[]{:S(2)}) collective-permute-start(f16[8,392,128]{2,1,0:T(8,128)(2,1)S(1)} %all_to_all.21), channel_id=1, source_target_pairs={{0,8},{8,0},{1,9},{9,1},{2,10},{10,2},{3,11},{11,3},{4,12},{12,4},... | collective-permute-start | bytes 2408456 | tf_op jit(solution)/shard_map/ppermute | solution.py:334
  118.6 3.9 %collective-permute-start.5 = (bf16[8,128,128]{2,1,0:T(8,128)(2,1)S(1)}, bf16[8,128,128]{2,1,0:T(8,128)(2,1)S(1)}, u32[]{:S(2)}, u32[]{:S(2)}) collective-permute-start(bf16[8,128,128]{2,1,0:T(8,128)(2,1)S(1)} %all_to_all.22.value_first), channel_id=1, source_target_pairs={{0,8},{8,0},{1,9},{9,1},{2,10},{10,2},{3,11},{11,3},{4,12},{12,4},... | collective-permute-start | bytes 786440 | tf_op jit(solution)/shard_map/ppermute | solution.py:334
  121.1 1.5 %copy-start.1 = (bf16[2,2,256,256]{3,2,1,0:T(8,128)(2,1)S(1)}, bf16[2,2,256,256]{3,2,1,0:T(8,128)(2,1)}, u32[]{:S(2)}) copy-start(bf16[2,2,256,256]{3,2,1,0:T(8,128)(2,1)} %far_upper_ref.1) | copy-start | bytes 1572868
  121.1 1.5 %copy-start.2 = (bf16[2,256,256]{2,1,0:T(8,128)(2,1)S(1)}, bf16[2,256,256]{2,1,0:T(8,128)(2,1)}, u32[]{:S(2)}) copy-start(bf16[2,256,256]{2,1,0:T(8,128)(2,1)} %far_upper_inv_ref.1) | copy-start | bytes 786436

commit v7 on v6

--- a/solution.py
+++ b/solution.py
@@ -37,7 +37,7 @@
     return jnp.where(flags != 0, one, other)
 
 
-def kernel(body, out_shapes, *operands, left_in_hbm=(), scratch=(), flops=0):
+def kernel(body, out_shapes, *operands, left_in_hbm=(), scratch=(), out=pltpu.VMEM, flops=0):
     moved = sum(o.size * o.dtype.itemsize for o in operands)
     moved += sum(o.size * o.dtype.itemsize for o in out_shapes)
     return pl.pallas_call(
@@ -48,7 +48,7 @@
             for o in operands
         ]
         + [pl.BlockSpec(memory_space=pltpu.HBM) for _ in left_in_hbm],
-        out_specs=[pl.BlockSpec(memory_space=pltpu.VMEM) for _ in out_shapes],
+        out_specs=[pl.BlockSpec(memory_space=out) for _ in out_shapes],
         scratch_shapes=scratch,
         compiler_params=pltpu.CompilerParams(vmem_limit_bytes=16 * 2**20),
         cost_estimate=pl.CostEstimate(flops=flops, bytes_accessed=moved, transcendentals=0),
@@ -279,8 +279,8 @@
 def backward_kernel(
     place_ref, size_ref, value_first, value_second, plane_first, plane_second,
     pair_first, pair_second, through_ref, mine_ref, other_ref, first_ref, second_ref, before_ref,
-    previous_ref, leaf_forward_ref, far_upper_ref, far_upper_inv_ref, leaf_ref, sep_ref,
-    leaf_upper_ref, leaf_upper_inv_ref, arrived,
+    previous_ref, leaf_forward_ref, far_upper_ref, far_upper_inv_ref, far_leaf_ref, far_sep_ref,
+    leaf_upper_ref, leaf_upper_inv_ref, leaf_ref, sep_ref, arrived, left,
 ):
     copies = [
         pltpu.make_async_copy(far_upper_ref, leaf_upper_ref, arrived.at[0]),
@@ -312,6 +312,8 @@
     sep = choose(core == 0, first, second).T
     before = choose(core == 0, before, first).T.astype(BF16)
     sep_ref[...] = sep
+    results = [pltpu.make_async_copy(sep_ref, far_sep_ref, left.at[0])]
+    results[0].start()
     sep = sep.astype(BF16)
     dot = functools.partial(jnp.dot, preferred_element_type=F32)
     rows = lax.broadcasted_iota(jnp.int32, sep.shape, 0)
@@ -322,6 +324,11 @@
         back = back - dot(leaf_upper_ref[leaf, 1], sep)
         result = dot(leaf_upper_inv_ref[leaf], back.astype(BF16))
         leaf_ref[leaf] = jnp.where(rows < size_ref[leaf], result, 0.0)
+        copy = pltpu.make_async_copy(leaf_ref.at[leaf], far_leaf_ref.at[leaf], left.at[leaf + 1])
+        copy.start()
+        results.append(copy)
+    for copy in results:
+        copy.wait()
 
 
 def to_all(block, axis, dtype=F16):
@@ -453,8 +460,12 @@
         scratch=[
             pltpu.VMEM(leaf_upper.shape, BF16),
             pltpu.VMEM(leaf_upper_inv.shape, BF16),
+            pltpu.VMEM((leaves, width, samples), F32),
+            pltpu.VMEM((width, samples), F32),
             pltpu.SemaphoreType.DMA((2,)),
+            pltpu.SemaphoreType.DMA((leaves + 1,)),
         ],
+        out=pltpu.HBM,
     )
     return (leaf_correction, sep_correction[None])
 

time: 128 us -> 128 us (level)
  no operation moved by 1% of the time
where the time goes in v7:
time: 128 us; the launch traced here: 127 us
  blocking collectives  60.2 us (47%)
  starting transfers between devices  35 us (27%)
  Pallas kernels  15.2 us (12%)
  waiting for transfers between devices  11.8 us (9%)
  other arithmetic  2.02 us (2%)
    all_to_all x2, blocking collectives, to_all(): return lax.all_to_all(slots, axis, 0, 0, tiled=True)  32.9 us
    all_to_all x1, blocking collectives, per_device(): between = in_order(core, lax.all_to_all(slots, Z, 0, 0, tiled=True))  27.3 us
    ppermute x4, starting transfers between devices, swap_cores(): return lax.ppermute(block, C, [(0, 1), (1, 0)])  20.5 us
    pallas_call x9, Pallas kernels, kernel(): pl.pallas_call(body, out_shape=out_shapes, in_specs=[pl.BlockSpec(memory_...  15.2 us
    all_to_all x1, waiting for transfers between devices, to_all(): return lax.all_to_all(slots, axis, 0, 0, tiled=True)  9.56 us
    all_to_all x1, starting transfers between devices, to_all(): return lax.all_to_all(slots, axis, 0, 0, tiled=True)  7.65 us
    ppermute x1, starting transfers between devices, per_device(): lax.ppermute(left_terms, panel, [(i + 1, i) for i in range(panels - 1)])  4.68 us
  transfers between devices with their start and end apart: 7, of which 3 were waited for; matrix products, arithmetic and copies ran while one was open for 1% of the time, Pallas kernels for 5%

profile of v7, /device:TPU:1, one launch (start us, length us, event | category | flops | bytes accessed | tf_op | source)
XLA Modules:
  0.0 127.1 jit_solution(324859538390880619)
XLA Ops:
  0.6 0.0 copy-start
  0.6 0.0 copy-start.4
  0.7 0.0 copy-start.6
  0.7 0.0 copy-start.5
  0.7 0.9 pad_maximum_fusion.blocks_ref
  1.6 0.9 broadcast_in_dim.54
  2.5 7.7 %all-to-all-start = ((f16[8,264,128]{2,1,0:T(8,128)(2,1)}), f16[8,264,128]{2,1,0:T(8,128)(2,1)S(1)}, u32[]{:S(2)}, u32[]{:S(2)}) async-start(f16[8,264,128]{2,1,0:T(8,128)(2,1)} %broadcast_in_dim.54), calls=%async_computation | async-start | bytes 1081344 | tf_op jit(solution)/shard_map/all_to_all | solution.py:337
  10.2 0.0 copy-done.4
  10.2 0.1 compare_convert_fusion
  10.3 0.0 copy-done
  10.3 0.3 fusion.leaf_forward_ref
  10.6 0.0 copy-start.3
  10.6 0.2 convolution_bitcast_fusion
  10.8 4.7 %collective-permute-start = (f32[256,128]{1,0:T(8,128)S(1)}, f32[256,128]{1,0:T(8,128)S(1)}, u32[]{:S(2)}, u32[]{:S(2)}) collective-permute-start(f32[256,128]{1,0:T(8,128)S(1)} %convolution_bitcast_fusion), channel_id=1, source_target_pairs={{8,0},{16,8},{24,16},{32,24},{40,32},{48,40},{56,48},{64,56},{72,6... | collective-permute-start | bytes 393224 | tf_op jit(solution)/shard_map/ppermute | solution.py:387
  15.5 0.2 convolution_bitcast_fusion.1.own_ref
  15.8 9.6 %all-to-all-done = f16[8,264,128]{2,1,0:T(8,128)(2,1)S(1)} async-done(((f16[8,264,128]{2,1,0:T(8,128)(2,1)}), f16[8,264,128]{2,1,0:T(8,128)(2,1)S(1)}, u32[]{:S(2)}, u32[]{:S(2)}) %all-to-all-start) | async-done | bytes 540704 | tf_op jit(solution)/shard_map/all_to_all | solution.py:337
  25.3 0.1 convert_element_type.44.wire_ref
  25.4 0.0 collective-permute-done.right_ref
  25.4 0.7 shard_map.123
  26.1 5.6 %collective-permute-start.1 = (f32[896,256]{1,0:T(8,128)S(1)}, f32[896,256]{1,0:T(8,128)S(1)}, u32[]{:S(2)}, u32[]{:S(2)}) collective-permute-start(f32[896,256]{1,0:T(8,128)S(1)} %get-tuple-element.20.mine_ref), channel_id=1, source_target_pairs={{0,8},{8,0},{1,9},{9,1},{2,10},{10,2},{3,11},{11,3},{4,12},{12,4},... | collective-permute-start | bytes 2752520 | tf_op jit(solution)/shard_map/ppermute | solution.py:341
  31.7 0.1 pad_add_fusion.place_ref
  31.8 2.0 %collective-permute-done.1.other_ref = f32[896,256]{1,0:T(8,128)S(1)} collective-permute-done((f32[896,256]{1,0:T(8,128)S(1)}, f32[896,256]{1,0:T(8,128)S(1)}, u32[]{:S(2)}, u32[]{:S(2)}) %collective-permute-start.1) | collective-permute-done | bytes 917536 | tf_op jit(solution)/shard_map/ppermute | solution.py:341
  33.8 1.5 %shard_map.124 = f32[1032,128]{1,0:T(8,128)S(1)} custom-call(s32[3]{0:T(128)S(1)} %pad_add_fusion.place_ref, f32[896,256]{1,0:T(8,128)S(1)} %get-tuple-element.20.mine_ref, f32[896,256]{1,0:T(8,128)S(1)} %collective-permute-done.1.other_ref), custom_call_target="tpu_custom_call" | custom-call | bytes 2363404 | tf_op jit(solution)/shard_map/pallas_call | solution.py:43
  35.4 0.1 broadcast_in_dim.55
  35.5 18.1 %all_to_all.20 = f16[4,1032,128]{2,1,0:T(8,128)(2,1)S(1)} all-to-all(f16[4,1032,128]{2,1,0:T(8,128)(2,1)S(1)} %broadcast_in_dim.55), channel_id=1, replica_groups=mesh['z'=8,'x'=4,'c'=2,'y'=8] {'x'}, dimensions={0} | all-to-all | bytes 2113536 | tf_op jit(solution)/shard_map/all_to_all | solution.py:337
  53.7 3.7 %collective-permute-start.2 = (f16[4,1032,128]{2,1,0:T(8,128)(2,1)S(1)}, f16[4,1032,128]{2,1,0:T(8,128)(2,1)S(1)}, u32[]{:S(2)}, u32[]{:S(2)}) collective-permute-start(f16[4,1032,128]{2,1,0:T(8,128)(2,1)S(1)} %all_to_all.20), channel_id=1, source_target_pairs={{0,8},{8,0},{1,9},{9,1},{2,10},{10,2},{3,11},{11,3},{4,12},{12,4},... | collective-permute-start | bytes 3170312 | tf_op jit(solution)/shard_map/ppermute | solution.py:341
  57.4 2.1 %collective-permute-start.3 = (f16[1032,128]{1,0:T(8,128)(2,1)S(1)}, f16[1032,128]{1,0:T(8,128)(2,1)S(1)}, u32[]{:S(2)}, u32[]{:S(2)}) collective-permute-start(f16[1032,128]{1,0:T(8,128)(2,1)S(1)} %convert_element_type.52), channel_id=1, source_target_pairs={{8,16},{24,32},{40,48},{56,64},{72,80},{88,96},{104,112},{120,128}... | collective-permute-start | bytes 792584 | tf_op jit(solution)/shard_map/ppermute | solution.py:402
  59.6 0.1 convert_element_type.49.first_ref.mine_ref.pair_first
  59.7 0.0 collective-permute-done.2
  59.7 0.1 convert_element_type.50.second_ref.other_ref.pair_second
  59.9 1.5 %shard_map.125 = f32[2,392,128]{2,1,0:T(8,128)S(1)} custom-call(s32[3]{0:T(128)S(1)} %pad_add_fusion.place_ref, f32[4,1032,128]{2,1,0:T(8,128)S(1)} %convert_element_type.49.first_ref.mine_ref.pair_first, f32[4,1032,128]{2,1,0:T(8,128)S(1)} %convert_element_type.50.second_ref.other_ref.pair_second), custom_call_target="tpu_custom_call" | custom-call | bytes 4628492 | tf_op jit(solution)/shard_map/pallas_call | solution.py:43
  61.4 2.0 %shard_map.126 = (f32[384,256]{1,0:T(8,128)S(1)}, f32[4,384,256]{2,1,0:T(8,128)S(1)}) custom-call(s32[3]{0:T(128)S(1)} %pad_add_fusion.place_ref, f32[4,1032,128]{2,1,0:T(8,128)S(1)} %convert_element_type.49.first_ref.mine_ref.pair_first, f32[4,1032,128]{2,1,0:T(8,128)S(1)} %convert_element_type.50.second_ref.other_ref.pair_second), custom_call_target="tpu_custom_call" | custom-call | bytes 6193164 | tf_op jit(solution)/shard_map/pallas_call | solution.py:43
  63.4 0.0 collective-permute-done.3
  63.4 0.2 broadcast_select_fusion
  63.7 27.3 %all_to_all.21 = f16[8,392,128]{2,1,0:T(8,128)(2,1)S(1)} all-to-all(f16[8,392,128]{2,1,0:T(8,128)(2,1)S(1)} %broadcast_select_fusion), channel_id=1, replica_groups=mesh['z'=8,'x'=4,'c'=2,'y'=8] {'z'}, dimensions={0} | all-to-all | bytes 1605632 | tf_op jit(solution)/shard_map/all_to_all | solution.py:421
  91.0 8.8 %collective-permute-start.4 = (f16[8,392,128]{2,1,0:T(8,128)(2,1)S(1)}, f16[8,392,128]{2,1,0:T(8,128)(2,1)S(1)}, u32[]{:S(2)}, u32[]{:S(2)}) collective-permute-start(f16[8,392,128]{2,1,0:T(8,128)(2,1)S(1)} %all_to_all.21), channel_id=1, source_target_pairs={{0,8},{8,0},{1,9},{9,1},{2,10},{10,2},{3,11},{11,3},{4,12},{12,4},... | collective-permute-start | bytes 2408456 | tf_op jit(solution)/shard_map/ppermute | solution.py:341
  99.8 1.6 %shard_map.127 = (f32[256,128]{1,0:T(8,128)S(1)}, f32[128,128]{1,0:T(8,128)S(1)}) custom-call(s32[3]{0:T(128)S(1)} %pad_add_fusion.place_ref, f32[4,1032,128]{2,1,0:T(8,128)S(1)} %convert_element_type.49.first_ref.mine_ref.pair_first, f32[4,1032,128]{2,1,0:T(8,128)S(1)} %convert_element_type.50.second_ref.other_ref.pair_second, ...), custom_call_target="tpu_custom_call" | custom-call | bytes 5996556 | tf_op jit(solution)/shard_map/pallas_call | solution.py:43
  101.4 0.1 convert_element_type.53.plane_mine.plane_first
  101.5 0.2 collective-permute-done.4
  101.8 0.1 convert_element_type.54.plane_other.plane_second
  101.9 2.0 %shard_map.128 = (bf16[128,128]{1,0:T(8,128)(2,1)S(1)}, f32[128,256]{1,0:T(8,128)S(1)}) custom-call(s32[3]{0:T(128)S(1)} %pad_add_fusion.place_ref, f32[8,392,128]{2,1,0:T(8,128)S(1)} %convert_element_type.53.plane_mine.plane_first, f32[8,392,128]{2,1,0:T(8,128)S(1)} %convert_element_type.54.plane_other.plane_second, ...), custom_call_target="tpu_custom_call" | custom-call | bytes 3571724 | tf_op jit(solution)/shard_map/pallas_call | solution.py:43
  103.9 14.8 %all_to_all.22.value_first = bf16[8,128,128]{2,1,0:T(8,128)(2,1)S(1)} all-to-all(bf16[8,128,128]{2,1,0:T(8,128)(2,1)S(1)} %broadcast_in_dim.60), channel_id=1, replica_groups=mesh['z'=8,'x'=4,'c'=2,'y'=8] {'z'}, dimensions={0} | all-to-all | bytes 524288 | tf_op jit(solution)/shard_map/all_to_all | solution.py:337
  118.6 2.4 %collective-permute-start.5 = (bf16[8,128,128]{2,1,0:T(8,128)(2,1)S(1)}, bf16[8,128,128]{2,1,0:T(8,128)(2,1)S(1)}, u32[]{:S(2)}, u32[]{:S(2)}) collective-permute-start(bf16[8,128,128]{2,1,0:T(8,128)(2,1)S(1)} %all_to_all.22.value_first), channel_id=1, source_target_pairs={{0,8},{8,0},{1,9},{9,1},{2,10},{10,2},{3,11},{11,3},{4,12},{12,4},... | collective-permute-start | bytes 786440 | tf_op jit(solution)/shard_map/ppermute | solution.py:341
  121.1 0.0 copy-start.1
  121.1 0.0 copy-start.2
  121.1 1.5 %shard_map.129 = (f32[4,128,256]{2,1,0:T(8,128)S(1)}, f32[128,256]{1,0:T(8,128)S(1)}, f32[128,256]{1,0:T(8,128)S(1)}, f32[128,256]{1,0:T(8,128)S(1)}) custom-call(s32[3]{0:T(128)S(1)} %pad_add_fusion.place_ref, f32[128,256]{1,0:T(8,128)S(1)} %get-tuple-element.29.ahead_ref, f32[384,256]{1,0:T(8,128)S(1)} %get-tuple-element.30.start_factor_ref, ...), custom_call_target="tpu_custom_call" | custom-call | bytes 5378060 | tf_op jit(solution)/shard_map/pallas_call | solution.py:43
  122.6 0.0 collective-permute-done.5.value_second
  122.6 4.5 %shard_map.130 = (f32[2,256,128]{2,1,0:T(8,128)}, f32[256,128]{1,0:T(8,128)}) custom-call(s32[3]{0:T(128)S(1)} %pad_add_fusion.place_ref, s32[2]{0:T(128)S(1)} %copy-done.4, bf16[8,128,128]{2,1,0:T(8,128)(2,1)S(1)} %all_to_all.22.value_first, bf16[8,128,128]{2,1,0:T(8,128)(2,1)S(1)} %collective-permute-done.5.value_second, ...), custom_call_target="tpu_custom_call" | custom-call | bytes 11898900 | tf_op jit(solution)/shard_map/pallas_call | solution.py:43
  (14 shorter events, 0.3 us)
Async XLA Ops:
  0.6 9.6 %copy-start = (bf16[2,256,256]{2,1,0:T(8,128)(2,1)S(1)}, bf16[2,256,256]{2,1,0:T(8,128)(2,1)}, u32[]{:S(2)}) copy-start(bf16[2,256,256]{2,1,0:T(8,128)(2,1)} %param.14) | copy-start | bytes 786436
  0.6 9.5 %copy-start.4 = (s32[2]{0:T(128)S(1)}, s32[2]{0:T(128)}, u32[]{:S(2)}) copy-start(s32[2]{0:T(128)} %size_ref.1) | copy-start | bytes 28
  0.7 9.6 %copy-start.6 = (f32[2,256,128]{2,1,0:T(8,128)S(1)}, f32[2,256,128]{2,1,0:T(8,128)}, u32[]{:S(2)}) copy-start(f32[2,256,128]{2,1,0:T(8,128)} %param.11) | copy-start | bytes 786436
  0.7 9.9 %copy-start.5 = (bf16[2,2,256,256]{3,2,1,0:T(8,128)(2,1)S(1)}, bf16[2,2,256,256]{3,2,1,0:T(8,128)(2,1)}, u32[]{:S(2)}) copy-start(bf16[2,2,256,256]{3,2,1,0:T(8,128)(2,1)} %param.15) | copy-start | bytes 1572868
  2.5 22.8 %all-to-all-start = ((f16[8,264,128]{2,1,0:T(8,128)(2,1)}), f16[8,264,128]{2,1,0:T(8,128)(2,1)S(1)}, u32[]{:S(2)}, u32[]{:S(2)}) async-start(f16[8,264,128]{2,1,0:T(8,128)(2,1)} %broadcast_in_dim.54), calls=%async_computation | async-start | bytes 1081344 | tf_op jit(solution)/shard_map/all_to_all | solution.py:337
  10.6 14.8 %copy-start.3 = (f32[1,256,128]{2,1,0:T(8,128)S(1)}, f32[1,256,128]{2,1,0:T(8,128)}, u32[]{:S(2)}) copy-start(f32[1,256,128]{2,1,0:T(8,128)} %param.12) | copy-start | bytes 393220
  10.8 14.6 %collective-permute-start = (f32[256,128]{1,0:T(8,128)S(1)}, f32[256,128]{1,0:T(8,128)S(1)}, u32[]{:S(2)}, u32[]{:S(2)}) collective-permute-start(f32[256,128]{1,0:T(8,128)S(1)} %convolution_bitcast_fusion), channel_id=1, source_target_pairs={{8,0},{16,8},{24,16},{32,24},{40,32},{48,40},{56,48},{64,56},{72,6... | collective-permute-start | bytes 393224 | tf_op jit(solution)/shard_map/ppermute | solution.py:387
  26.1 7.7 %collective-permute-start.1 = (f32[896,256]{1,0:T(8,128)S(1)}, f32[896,256]{1,0:T(8,128)S(1)}, u32[]{:S(2)}, u32[]{:S(2)}) collective-permute-start(f32[896,256]{1,0:T(8,128)S(1)} %get-tuple-element.20.mine_ref), channel_id=1, source_target_pairs={{0,8},{8,0},{1,9},{9,1},{2,10},{10,2},{3,11},{11,3},{4,12},{12,4},... | collective-permute-start | bytes 2752520 | tf_op jit(solution)/shard_map/ppermute | solution.py:341
  53.7 6.1 %collective-permute-start.2 = (f16[4,1032,128]{2,1,0:T(8,128)(2,1)S(1)}, f16[4,1032,128]{2,1,0:T(8,128)(2,1)S(1)}, u32[]{:S(2)}, u32[]{:S(2)}) collective-permute-start(f16[4,1032,128]{2,1,0:T(8,128)(2,1)S(1)} %all_to_all.20), channel_id=1, source_target_pairs={{0,8},{8,0},{1,9},{9,1},{2,10},{10,2},{3,11},{11,3},{4,12},{12,4},... | collective-permute-start | bytes 3170312 | tf_op jit(solution)/shard_map/ppermute | solution.py:341
  57.4 5.9 %collective-permute-start.3 = (f16[1032,128]{1,0:T(8,128)(2,1)S(1)}, f16[1032,128]{1,0:T(8,128)(2,1)S(1)}, u32[]{:S(2)}, u32[]{:S(2)}) collective-permute-start(f16[1032,128]{1,0:T(8,128)(2,1)S(1)} %convert_element_type.52), channel_id=1, source_target_pairs={{8,16},{24,32},{40,48},{56,64},{72,80},{88,96},{104,112},{120,128}... | collective-permute-start | bytes 792584 | tf_op jit(solution)/shard_map/ppermute | solution.py:402
  91.0 10.8 %collective-permute-start.4 = (f16[8,392,128]{2,1,0:T(8,128)(2,1)S(1)}, f16[8,392,128]{2,1,0:T(8,128)(2,1)S(1)}, u32[]{:S(2)}, u32[]{:S(2)}) collective-permute-start(f16[8,392,128]{2,1,0:T(8,128)(2,1)S(1)} %all_to_all.21), channel_id=1, source_target_pairs={{0,8},{8,0},{1,9},{9,1},{2,10},{10,2},{3,11},{11,3},{4,12},{12,4},... | collective-permute-start | bytes 2408456 | tf_op jit(solution)/shard_map/ppermute | solution.py:341
  118.6 3.9 %collective-permute-start.5 = (bf16[8,128,128]{2,1,0:T(8,128)(2,1)S(1)}, bf16[8,128,128]{2,1,0:T(8,128)(2,1)S(1)}, u32[]{:S(2)}, u32[]{:S(2)}) collective-permute-start(bf16[8,128,128]{2,1,0:T(8,128)(2,1)S(1)} %all_to_all.22.value_first), channel_id=1, source_target_pairs={{0,8},{8,0},{1,9},{9,1},{2,10},{10,2},{3,11},{11,3},{4,12},{12,4},... | collective-permute-start | bytes 786440 | tf_op jit(solution)/shard_map/ppermute | solution.py:341
  121.1 1.5 %copy-start.1 = (bf16[2,2,256,256]{3,2,1,0:T(8,128)(2,1)S(1)}, bf16[2,2,256,256]{3,2,1,0:T(8,128)(2,1)}, u32[]{:S(2)}) copy-start(bf16[2,2,256,256]{3,2,1,0:T(8,128)(2,1)} %far_upper_ref.1) | copy-start | bytes 1572868
  121.1 1.5 %copy-start.2 = (bf16[2,256,256]{2,1,0:T(8,128)(2,1)S(1)}, bf16[2,256,256]{2,1,0:T(8,128)(2,1)}, u32[]{:S(2)}) copy-start(bf16[2,256,256]{2,1,0:T(8,128)(2,1)} %far_upper_inv_ref.1) | copy-start | bytes 786436
